TPU v7x, 32 devices: a whole 2x2x4 slice. The times are simulated.
32 devices in a mesh: context: 8 (over y, x, core), chan: 4 (over z).
Axes of the slice: x: 2, y: 2, z: 4, core: 2. Of those that a mesh axis runs over, the one named last changes fastest.
Arguments:
- signal: float32 [64, 8192], P('chan', 'context'), may hold values from -6 to 6
- filter_taps: float32 [8192], P('context'), may hold values from -6 to 6
- skip_gain: float32 [64], P('chan'), may hold values from 0.5 to 1.5
- cotangent: float32 [64, 8192], P('chan', 'context'), may hold values from -6 to 6
Outputs:
- output: float32 [64, 8192], P('chan', 'context')
- grad_signal: float32 [64, 8192], P('chan', 'context')
- grad_filter: float32 [8192], P('context')
All inputs are finite; a program needn't handle non-finite values.
Results may differ from a plain program's by a relative error of at most 0.00013.
Values sent between devices are 32-bit elements; how exact they have to be, the bound alone decides.
No kernel may reach another device: no remote copies, remote signals or barrier semaphores. Data moves between devices by JAX's collectives and lax.ppermute only.
A program may use at most 64 MiB of HBM per device.

v0:
```python
import math

import jax
import jax.numpy as jnp
from jax import lax
from jax.sharding import PartitionSpec as P

exact_mode = lax.Precision.HIGHEST


def rotation(first, second, period):
    turned = first * second % period
    return turned.astype(jnp.float32) * (2.0 * math.pi / period)


def table_product(real_part, imag_part, cosine, sine_table):
    return (
        real_part * cosine - imag_part * sine_table,
        real_part * sine_table + imag_part * cosine,
    )


def along_last(real_part, imag_part, angle_table):
    cosine = jnp.cos(angle_table)
    sine_table = jnp.sin(angle_table)
    new_real = jnp.matmul(real_part, cosine, precision=exact_mode) - jnp.matmul(
        imag_part, sine_table, precision=exact_mode
    )
    new_imag = jnp.matmul(real_part, sine_table, precision=exact_mode) + jnp.matmul(
        imag_part, cosine, precision=exact_mode
    )
    return (new_real, new_imag)


def along_slow(real_part, imag_part, angle_table):
    cosine = jnp.cos(angle_table)
    sine_table = jnp.sin(angle_table)
    new_real = jnp.einsum("gsjd,sa->gajd", real_part, cosine, precision=exact_mode) - jnp.einsum(
        "gsjd,sa->gajd", imag_part, sine_table, precision=exact_mode
    )
    new_imag = jnp.einsum(
        "gsjd,sa->gajd", real_part, sine_table, precision=exact_mode
    ) + jnp.einsum("gsjd,sa->gajd", imag_part, cosine, precision=exact_mode)
    return (new_real, new_imag)


def finish_sections(real_part, imag_part, stride, shards, length):
    sources = jnp.arange(shards, dtype=jnp.int32)
    slower = jnp.arange(stride, dtype=jnp.int32)
    slow_angle = -rotation(slower[:, None], slower[None, :], stride)
    real_part, imag_part = along_slow(real_part, imag_part, slow_angle)
    inner_twist = -rotation(slower[:, None, None], sources[None, None, :], length)
    real_part, imag_part = table_product(
        real_part, imag_part, jnp.cos(inner_twist), jnp.sin(inner_twist)
    )
    last_angle = -rotation(sources[:, None], sources[None, :], shards)
    return along_last(real_part, imag_part, last_angle)


def forward(stacked):
    shards = lax.axis_size("context")
    position = lax.axis_index("context")
    signals, length = stacked.shape
    stride = length // shards
    period = 2 * shards * length
    sources = jnp.arange(shards, dtype=jnp.int32)
    slower = jnp.arange(stride, dtype=jnp.int32)
    blocks = stacked.reshape(signals, stride, shards)
    columns = lax.all_to_all(blocks, "context", split_axis=2, concat_axis=2, tiled=True)
    token_ids = shards * slower[:, None] + position
    order = jnp.arange(2 * shards, dtype=jnp.int32)
    first_angle = -rotation(sources[:, None], order[None, :], 2 * shards)
    real_part = jnp.matmul(columns, jnp.cos(first_angle), precision=exact_mode)
    imag_part = jnp.matmul(columns, jnp.sin(first_angle), precision=exact_mode)
    twist = -rotation(token_ids, order[None, :], period)
    real_part, imag_part = table_product(real_part, imag_part, jnp.cos(twist), jnp.sin(twist))
    spectra = jnp.stack([real_part, imag_part]).reshape(2, signals, stride, 2, shards)
    spectra = lax.all_to_all(spectra, "context", split_axis=4, concat_axis=4, tiled=True)
    real_part, imag_part = finish_sections(spectra[0], spectra[1], stride, shards, length)
    return (real_part, imag_part, order)


def inverse(real_part, imag_part, order):
    shards = lax.axis_size("context")
    position = lax.axis_index("context")
    signals, stride = (real_part.shape[0], real_part.shape[1])
    length = stride * shards
    period = 2 * shards * length
    sources = jnp.arange(shards, dtype=jnp.int32)
    slower = jnp.arange(stride, dtype=jnp.int32)
    last_angle = rotation(sources[:, None], sources[None, :], shards)
    real_part, imag_part = along_last(real_part, imag_part, last_angle)
    inner_twist = rotation(slower[:, None, None], sources[None, None, :], length)
    real_part, imag_part = table_product(
        real_part, imag_part, jnp.cos(inner_twist), jnp.sin(inner_twist)
    )
    slow_angle = rotation(slower[:, None], slower[None, :], stride)
    real_part, imag_part = along_slow(real_part, imag_part, slow_angle)
    spectra = lax.all_to_all(
        jnp.stack([real_part, imag_part]), "context", split_axis=4, concat_axis=4, tiled=True
    )
    real_part = spectra[0].reshape(signals, stride, 2 * shards)
    imag_part = spectra[1].reshape(signals, stride, 2 * shards)
    token_ids = shards * slower[:, None] + position
    twist = rotation(token_ids, order[None, :], period)
    real_part, imag_part = table_product(real_part, imag_part, jnp.cos(twist), jnp.sin(twist))
    first_angle = rotation(order[:, None], sources[None, :], 2 * shards)
    cosine = jnp.cos(first_angle)
    sine_table = jnp.sin(first_angle)
    out_real = jnp.matmul(real_part, cosine, precision=exact_mode) - jnp.matmul(
        imag_part, sine_table, precision=exact_mode
    )
    out_imag = jnp.matmul(real_part, sine_table, precision=exact_mode) + jnp.matmul(
        imag_part, cosine, precision=exact_mode
    )
    results = jnp.stack([out_real, out_imag])
    blocks = lax.all_to_all(results, "context", split_axis=3, concat_axis=3, tiled=True)
    return blocks.reshape(blocks.shape[0], signals, length)


def body(signal, filter_taps, skip_gain, cotangent):
    shards = lax.axis_size("context")
    channels, length = signal.shape
    factor = 1.0 / (2 * shards * length * math.sqrt(shards * length))
    stacked = jnp.concatenate([signal, cotangent, filter_taps[None, :]], axis=0)
    real_part, imag_part, order = forward(stacked)
    sig_re = real_part[:channels]
    sig_im = imag_part[:channels]
    cot_re = real_part[channels : 2 * channels]
    cot_im = imag_part[channels : 2 * channels]
    fil_re = real_part[2 * channels :]
    fil_im = imag_part[2 * channels :]
    out_re = sig_re * fil_re - sig_im * fil_im
    out_im = sig_re * fil_im + sig_im * fil_re
    back_re = cot_re * fil_re + cot_im * fil_im
    back_im = cot_im * fil_re - cot_re * fil_im
    grad_re = jnp.sum(cot_re * sig_re + cot_im * sig_im, axis=0, keepdims=True)
    grad_im = jnp.sum(cot_im * sig_re - cot_re * sig_im, axis=0, keepdims=True)
    restored = inverse(
        jnp.concatenate([out_re - back_im, grad_re], axis=0),
        jnp.concatenate([out_im + back_re, grad_im], axis=0),
        order,
    )
    conv_out = restored[0, :channels]
    conv_back = restored[1, :channels]
    partial_value = restored[0, channels]
    output = conv_out * factor + skip_gain[:, None] * signal
    grad_signal = conv_back * factor + skip_gain[:, None] * cotangent
    grad_filter = lax.psum(partial_value * factor, "chan")
    return (output, grad_signal, grad_filter)


def solution(mesh):
    return jax.shard_map(
        body,
        mesh=mesh,
        in_specs=(P("chan", "context"), P("context"), P("chan"), P("chan", "context")),
        out_specs=(P("chan", "context"), P("chan", "context"), P("context")),
        check_vma=False,
    )
```

profile of v0, /device:TPU:0, one launch (start us, length us, event | category | flops | bytes accessed | tf_op | source)
XLA Modules:
  0.0 73.0 jit_solution(10231851044660266293)
XLA Ops:
  0.6 0.0 copy-start.1
  0.6 1.1 %concatenate.23 = f32[1,128,8]{0,2,1:T(8,128)S(1)} reshape(f32[1024]{0:T(1024)} %param.5) | data formatting | bytes 8192 | tf_op jit(solution)/shard_map/concatenate | solution.py:125
  1.7 0.0 copy-done.1
  1.7 0.0 copy-start
  1.7 0.2 copy.189
  1.9 0.6 copy-done
  2.6 0.2 copy.190
  2.8 0.3 pad_maximum_fusion.1
  3.1 0.9 %copy.192 = f32[33,128,8]{1,0,2:T(8,128)} copy(f32[33,128,8]{0,2,1:T(8,128)S(1)} %pad_maximum_fusion.1) | data formatting | bytes 270336 | tf_op jit(solution)/shard_map/concatenate | solution.py:125
  4.0 5.2 %all-to-all-start = ((f32[33,128,8]{1,0,2:T(8,128)}), f32[33,128,8]{1,0,2:T(8,128)S(1)}, u32[]{:S(2)}, u32[]{:S(2)}) async-start(f32[33,128,8]{1,0,2:T(8,128)} %copy.192), calls=%async_computation | async-start | bytes 327680 | tf_op jit(solution)/shard_map/all_to_all | solution.py:69
  9.2 0.1 fusion.92
  9.3 5.8 %all-to-all-done = f32[33,128,8]{1,0,2:T(8,128)S(1)} async-done(((f32[33,128,8]{1,0,2:T(8,128)}), f32[33,128,8]{1,0,2:T(8,128)S(1)}, u32[]{:S(2)}, u32[]{:S(2)}) %all-to-all-start) | async-done | bytes 135200 | tf_op jit(solution)/shard_map/all_to_all | solution.py:69
  15.1 0.5 fusion.21
  15.5 0.5 subtract_bitcast_fusion.1
  16.0 0.1 copy.195
  16.2 0.1 copy.196
  16.3 1.1 %pad_maximum_fusion = f32[2,33,128,2,8]{2,3,1,0,4:T(2,128)} fusion(f32[1,33,128,2,8]{2,3,1,0,4:T(2,128)S(1)} %copy.196, f32[1,33,128,2,8]{2,3,1,0,4:T(2,128)S(1)} %copy.195), kind=kLoop, calls=%fused_computation.14 | loop fusion | flops 135168 | bytes 1081344 | tf_op jit(solution)/shard_map/stack | solution.py:77
  17.4 3.5 %all-to-all-start.1 = ((f32[2,33,128,2,8]{2,3,1,0,4:T(2,128)}), f32[2,33,128,2,8]{2,3,1,0,4:T(2,128)S(1)}, u32[]{:S(2)}, u32[]{:S(2)}) async-start(f32[2,33,128,2,8]{2,3,1,0,4:T(2,128)} %pad_maximum_fusion), calls=%async_computation.1 | async-start | bytes 1081344 | tf_op jit(solution)/shard_map/all_to_all | solution.py:78
  20.9 0.1 fusion.116
  21.0 0.1 negate_sine_fusion.5
  21.1 9.7 %all-to-all-done.1 = f32[2,33,128,2,8]{2,3,1,0,4:T(2,128)S(1)} async-done(((f32[2,33,128,2,8]{2,3,1,0,4:T(2,128)}), f32[2,33,128,2,8]{2,3,1,0,4:T(2,128)S(1)}, u32[]{:S(2)}, u32[]{:S(2)}) %all-to-all-start.1) | async-done | bytes 540704 | tf_op jit(solution)/shard_map/all_to_all | solution.py:78
  30.8 0.7 fusion.5
  31.5 0.7 fusion.6
  32.2 0.7 convolution_add_fusion
  32.9 0.7 add_bitcast_fusion
  33.6 0.4 fusion.9
  34.0 0.4 fusion.11
  34.4 0.4 convolution_subtract_fusion.1
  34.8 0.4 convolution_add_fusion.1
  35.3 0.1 add_add_fusion
  35.4 0.3 fusion.19
  35.7 0.3 fusion.20
  36.0 0.3 convolution_subtract_fusion.3
  36.3 0.3 multiply_add_fusion.1
  36.7 0.6 fusion.15
  37.3 0.6 fusion.17
  37.8 0.6 fusion
  38.4 0.6 fusion.1
  39.0 0.2 copy.207
  39.3 9.5 %all_to_all.20 = f32[2,17,128,2,8]{2,3,1,0,4:T(2,128)S(1)} all-to-all(f32[2,17,128,2,8]{2,3,1,0,4:T(2,128)S(1)} %copy.207), channel_id=1, replica_groups=mesh['context'=8,'chan'=4] {'context'}, dimensions={4} | all-to-all | bytes 557056 | tf_op jit(solution)/shard_map/all_to_all | solution.py:99
  48.8 0.3 fusion.49
  49.1 0.3 fusion.50
  49.3 0.3 fusion.2
  49.6 0.3 fusion.3
  49.9 0.1 copy.210
  50.0 8.0 %all_to_all.21 = f32[2,17,128,8]{2,0,1,3:T(2,128)S(1)} all-to-all(f32[2,17,128,8]{2,0,1,3:T(2,128)S(1)} %copy.210), channel_id=1, replica_groups=mesh['context'=8,'chan'=4] {'context'}, dimensions={3} | all-to-all | bytes 278528 | tf_op jit(solution)/shard_map/all_to_all | solution.py:117
  58.0 0.4 copy.211
  58.4 0.4 fusion.4
  58.8 0.1 fusion.212
  58.8 12.6 %psum.7 = f32[1024]{0:T(1024)} all-reduce(f32[1024]{0:T(1024)S(1)} %fusion.4), channel_id=1, replica_groups=mesh['context'=8,'chan'=4] {'chan'}, use_global_device_ids=true, to_apply=%region_2.3 | all-reduce | flops 1024 | bytes 8192 | tf_op jit(solution)/shard_map/psum | solution.py:149
  71.4 0.2 copy.227
  71.6 0.0 copy-start.2
  71.6 0.2 copy.226
  71.7 0.5 copy-done.2
  72.2 0.7 %bitcast_add_fusion = (f32[16,1024]{1,0:T(8,128)}, f32[16,1024]{1,0:T(8,128)}) fusion(f32[16,1024]{1,0:T(8,128)S(1)} %copy-done, f32[1,16,1024]{2,1,0:T(8,128)S(1)} %copy.227, f32[16]{0:T(128)S(1)} %copy-done.2, f32[16,1024]{1,0:T(8,128)S(1)} %copy-done.1, f32[1,16,1024]{2,1,0:T(8,128)S(1)} %copy.226), kind=kLoop, calls=%fused_computation.64 | loop fusion | flops 98304 | bytes 393280 | tf_op jit(solution)/shard_map/add | solution.py:148
  (7 shorter events, 0.1 us)
Async XLA Ops:
  0.6 1.1 %copy-start.1 = (f32[16,1024]{1,0:T(8,128)S(1)}, f32[16,1024]{1,0:T(8,128)}, u32[]{:S(2)}) copy-start(f32[16,1024]{1,0:T(8,128)} %param.4) | copy-start | bytes 196612
  1.7 0.8 %copy-start = (f32[16,1024]{1,0:T(8,128)S(1)}, f32[16,1024]{1,0:T(8,128)}, u32[]{:S(2)}) copy-start(f32[16,1024]{1,0:T(8,128)} %param.7) | copy-start | bytes 196612
  4.0 11.1 %all-to-all-start = ((f32[33,128,8]{1,0,2:T(8,128)}), f32[33,128,8]{1,0,2:T(8,128)S(1)}, u32[]{:S(2)}, u32[]{:S(2)}) async-start(f32[33,128,8]{1,0,2:T(8,128)} %copy.192), calls=%async_computation | async-start | bytes 327680 | tf_op jit(solution)/shard_map/all_to_all | solution.py:69
  17.4 13.4 %all-to-all-start.1 = ((f32[2,33,128,2,8]{2,3,1,0,4:T(2,128)}), f32[2,33,128,2,8]{2,3,1,0,4:T(2,128)S(1)}, u32[]{:S(2)}, u32[]{:S(2)}) async-start(f32[2,33,128,2,8]{2,3,1,0,4:T(2,128)} %pad_maximum_fusion), calls=%async_computation.1 | async-start | bytes 1081344 | tf_op jit(solution)/shard_map/all_to_all | solution.py:78
  71.6 0.7 copy-start.2
where the time goes:
time: 73.4 us; the launch traced here: 73 us
  blocking collectives  30.1 us (41%)
  waiting for transfers between devices  15.5 us (21%)
  matrix products  9.89 us (13%)
  starting transfers between devices  8.71 us (12%)
  local copies, waits for them, and re-layouts  4.92 us (7%)
  other arithmetic  2.84 us (4%)
  between operations  0.98 us (1%)
    psum x1, blocking collectives, body(): grad_filter = lax.psum(partial_value * factor, 'chan')  12.6 us
    all_to_all x1, waiting for transfers between devices, forward(): lax.all_to_all(spectra, 'context', split_axis=4, concat_axis=4, tiled=True)  9.74 us
    all_to_all x1, blocking collectives, inverse(): lax.all_to_all(jnp.stack([real_part, imag_part]), 'context', split_axis=4...  9.52 us
    all_to_all x1, blocking collectives, inverse(): lax.all_to_all(results, 'context', split_axis=3, concat_axis=3, tiled=True)  8.01 us
    all_to_all x1, waiting for transfers between devices, forward(): lax.all_to_all(blocks, 'context', split_axis=2, concat_axis=2, tiled=True)  5.79 us
    all_to_all x1, starting transfers between devices, forward(): lax.all_to_all(blocks, 'context', split_axis=2, concat_axis=2, tiled=True)  5.17 us
    all_to_all x1, starting transfers between devices, forward(): lax.all_to_all(spectra, 'context', split_axis=4, concat_axis=4, tiled=True)  3.54 us
    concatenate x2, local copies, waits for them, and re-layouts, body(): stacked = jnp.concatenate([signal, cotangent, filter_taps[None, :]], axis=0)  1.95 us
  transfers between devices with their start and end apart: 2, of which 2 were waited for; matrix products, arithmetic and copies ran while one was open for 0% of the time, Pallas kernels for 0%

commit v1 on v0

--- a/solution.py
+++ b/solution.py
@@ -1,11 +1,276 @@
+import functools
 import math
 
 import jax
 import jax.numpy as jnp
 from jax import lax
+from jax.experimental import pallas as pl
+from jax.experimental.pallas import tpu as pltpu
 from jax.sharding import PartitionSpec as P
 
 exact_mode = lax.Precision.HIGHEST
+
+LANES = 128
+BLOCK = 256
+PACKED_ROWS = 16
+KERNEL_BYTES = 48 * 1024 * 1024
+
+
+def halves(value):
+    high = value.astype(jnp.bfloat16)
+    low = (value - high.astype(jnp.float32)).astype(jnp.bfloat16)
+    return high, low
+
+
+def dot(left, right, left_dim, right_dim):
+    return lax.dot_general(
+        left, right, (((left_dim,), (right_dim,)), ((), ())), preferred_element_type=jnp.float32
+    )
+
+
+def dot_halves(left, right, left_dim, right_dim):
+    return (
+        dot(left[0], right[0], left_dim, right_dim)
+        + dot(left[0], right[1], left_dim, right_dim)
+        + dot(left[1], right[0], left_dim, right_dim)
+    )
+
+
+def stack_kernel(signal_ref, cotangent_ref, taps_ref, out_ref):
+    channels, tokens = signal_ref.shape
+    row = 0
+    for source in (signal_ref, cotangent_ref):
+        for tile in range(tokens // LANES):
+            out_ref[row : row + channels, :] = source[:, tile * LANES : (tile + 1) * LANES]
+            row += channels
+    out_ref[row:, :] = taps_ref[...]
+
+
+def stack_local(signal, cotangent, taps):
+    channels, tokens = signal.shape
+    rows = (2 * channels * tokens + tokens) // LANES
+    return pl.pallas_call(
+        stack_kernel,
+        out_shape=jax.ShapeDtypeStruct((rows, LANES), jnp.float32),
+        in_specs=[pl.BlockSpec(memory_space=pltpu.VMEM)] * 3,
+        out_specs=pl.BlockSpec(memory_space=pltpu.VMEM),
+        name="stack_local",
+    )(signal, cotangent, taps.reshape(tokens // LANES, LANES))
+
+
+def gather_blocks(stacked, shards):
+    def flipped(value, bits):
+        return lax.ppermute(value, "context", [(i, i ^ bits) for i in range(shards)])
+
+    found = {0: stacked}
+    for bits in range(2, shards, 2):
+        found[bits] = flipped(stacked, bits)
+    for bits in range(0, shards, 2):
+        found[bits + 1] = flipped(found[bits], 1)
+    return [found[bits] for bits in range(shards)]
+
+
+def place_rows(block_ref, index, channels, tokens, first, high_ref, low_ref, start):
+    per = tokens // BLOCK
+    for tile in range(tokens // LANES):
+        rows = first + tile * channels
+        high, low = halves(block_ref[rows : rows + channels, :])
+        at = pl.multiple_of((index * per + tile // 2) * channels + start, PACKED_ROWS)
+        lanes = slice((tile % 2) * LANES, (tile % 2 + 1) * LANES)
+        high_ref[pl.ds(at, channels), lanes] = high
+        low_ref[pl.ds(at, channels), lanes] = low
+
+
+def filter_grad_kernel(shards, channels, tokens, *refs):
+    blocks, out_ref = refs[:shards], refs[shards]
+    sig_high, sig_low, cot_high, cot_low, folded = refs[shards + 1 :]
+    me = lax.axis_index("context")
+    per = tokens // BLOCK
+    rows = shards * per * channels
+    cot_high[rows:, :] = jnp.zeros((rows, BLOCK), jnp.bfloat16)
+    cot_low[rows:, :] = jnp.zeros((rows, BLOCK), jnp.bfloat16)
+    for bits in range(shards):
+        index = me ^ bits
+        place_rows(blocks[bits], index, channels, tokens, 0, sig_high, sig_low, 0)
+        place_rows(
+            blocks[bits], index, channels, tokens, channels * tokens // LANES, cot_high, cot_low, 0
+        )
+    sig = (sig_high[...], sig_low[...])
+    for lag in range(per + 1):
+        at = pl.multiple_of((me * per + lag) * channels, PACKED_ROWS)
+        window = (cot_high[pl.ds(at, rows), :], cot_low[pl.ds(at, rows), :])
+        folded[:, lag * BLOCK : (lag + 1) * BLOCK] = dot_halves(sig, window, 0, 0)
+    width = (per + 1) * BLOCK - LANES
+    total = None
+    for group in range(LANES // 8):
+        part = (
+            folded[8 * group : 8 * group + 8, :width]
+            + folded[LANES + 8 * group : LANES + 8 * group + 8, LANES:]
+        )
+        if group:
+            part = pltpu.roll(part, width - 8 * group, 1)
+        total = part if total is None else total + part
+    row = lax.broadcasted_iota(jnp.int32, total.shape, 0)
+    for step in (1, 2, 4):
+        total = jnp.where((row & step) != 0, pltpu.roll(total, width - step, 1), total)
+    out_ref[...] = jnp.sum(total, axis=0, keepdims=True)[:, :tokens]
+
+
+def filter_grad(blocks, shards, channels, tokens):
+    rows = shards * tokens // BLOCK * channels
+    per = tokens // BLOCK
+    return pl.pallas_call(
+        functools.partial(filter_grad_kernel, shards, channels, tokens),
+        out_shape=jax.ShapeDtypeStruct((1, tokens), jnp.float32),
+        in_specs=[pl.BlockSpec(memory_space=pltpu.VMEM)] * shards,
+        out_specs=pl.BlockSpec(memory_space=pltpu.VMEM),
+        scratch_shapes=[
+            pltpu.VMEM((rows, BLOCK), jnp.bfloat16),
+            pltpu.VMEM((rows, BLOCK), jnp.bfloat16),
+            pltpu.VMEM((2 * rows, BLOCK), jnp.bfloat16),
+            pltpu.VMEM((2 * rows, BLOCK), jnp.bfloat16),
+            pltpu.VMEM((BLOCK, (per + 1) * BLOCK), jnp.float32),
+        ],
+        compiler_params=pltpu.CompilerParams(vmem_limit_bytes=KERNEL_BYTES),
+        cost_estimate=pl.CostEstimate(
+            flops=2 * 3 * (per + 1) * rows * BLOCK * BLOCK, bytes_accessed=4 * rows * BLOCK * 2, transcendentals=0
+        ),
+        name="filter_grad",
+    )(*blocks)
+
+
+def convolve_kernel(shards, channels, tokens, *refs):
+    blocks, gain_ref, out_ref, back_ref = refs[:shards], *refs[shards : shards + 3]
+    sig_high, sig_low, cot_high, cot_low, taps, toe_high, toe_low = refs[shards + 3 :]
+    me = lax.axis_index("context")
+    per = tokens // BLOCK
+    rows = shards * per * channels
+    tiles = tokens // LANES
+    for ref in (sig_high, sig_low):
+        ref[:rows, :] = jnp.zeros((rows, BLOCK), jnp.bfloat16)
+    for ref in (cot_high, cot_low):
+        ref[rows:, :] = jnp.zeros((rows, BLOCK), jnp.bfloat16)
+    for bits in range(shards):
+        index = me ^ bits
+        place_rows(blocks[bits], index, channels, tokens, 0, sig_high, sig_low, rows)
+        place_rows(
+            blocks[bits], index, channels, tokens, channels * tiles, cot_high, cot_low, 0
+        )
+        taps[pl.ds(pl.multiple_of(index * tiles, 8), tiles), :] = blocks[bits][2 * channels * tiles :, :]
+    row = lax.broadcasted_iota(jnp.int32, (8, LANES), 0)
+    lane = lax.broadcasted_iota(jnp.int32, (8, LANES), 1)
+    groups = LANES // 8
+    toe_high[0] = jnp.zeros((LANES, LANES), jnp.bfloat16)
+    toe_low[0] = jnp.zeros((LANES, LANES), jnp.bfloat16)
+
+    def build(step, carry):
+        last, rolled = carry
+        sheet = taps[pl.ds(pl.multiple_of(step * 8, 8), 8), :]
+        for line in range(8):
+            now = jnp.broadcast_to(sheet[line : line + 1, :], (8, LANES))
+            for bit in (1, 2, 4):
+                now = jnp.where((row & bit) != 0, pltpu.roll(now, bit, 1), now)
+            skewed = jnp.where(lane < row, last, now)
+            last = now
+            turned = [skewed] + [pltpu.roll(skewed, 8 * g, 1) for g in range(1, groups)]
+            parts = [turned[0]] + [
+                jnp.where(lane < 8 * g, rolled[g], turned[g]) for g in range(1, groups)
+            ]
+            rolled = turned
+            high, low = halves(jnp.concatenate(parts, axis=0))
+            toe_high[step * 8 + line + 1] = high
+            toe_low[step * 8 + line + 1] = low
+        return last, rolled
+
+    blank = jnp.zeros((8, LANES), jnp.float32)
+    lax.fori_loop(0, shards * tiles // 8, build, (blank, [blank] * groups))
+
+    def square(ref, step):
+        return jnp.concatenate(
+            [
+                jnp.concatenate([ref[2 * step + 1], ref[2 * step + 2]], axis=1),
+                jnp.concatenate([ref[2 * step], ref[2 * step + 1]], axis=1),
+            ],
+            axis=0,
+        )
+
+    def forward(trip, total):
+        for inner in range(per):
+            step = trip * per + inner
+            at = pl.multiple_of(rows + (me * per - step) * channels, PACKED_ROWS)
+            window = (sig_high[pl.ds(at, per * channels), :], sig_low[pl.ds(at, per * channels), :])
+            total = total + dot_halves(window, (square(toe_high, step), square(toe_low, step)), 1, 0)
+        return total
+
+    def backward(trip, total):
+        for inner in range(per):
+            step = trip * per + inner
+            at = pl.multiple_of((me * per + step) * channels, PACKED_ROWS)
+            window = (cot_high[pl.ds(at, per * channels), :], cot_low[pl.ds(at, per * channels), :])
+            total = total + dot_halves(window, (square(toe_high, step), square(toe_low, step)), 1, 1)
+        return total
+
+    start = jnp.zeros((per * channels, BLOCK), jnp.float32)
+    conv = lax.fori_loop(0, me + 1, forward, start)
+    back = lax.fori_loop(0, shards - me, backward, start)
+    factor = 1.0 / math.sqrt(shards * tokens)
+    square_row = lax.broadcasted_iota(jnp.int32, (channels, channels), 0)
+    square_lane = lax.broadcasted_iota(jnp.int32, (channels, channels), 1)
+    gain = jnp.sum(
+        jnp.where(square_row == square_lane, jnp.broadcast_to(gain_ref[...], (channels, channels)), 0.0),
+        axis=1,
+        keepdims=True,
+    )
+    for tile in range(tiles):
+        spot = slice((tile // 2) * channels, (tile // 2 + 1) * channels)
+        part = slice((tile % 2) * LANES, (tile % 2 + 1) * LANES)
+        lanes = slice(tile * LANES, (tile + 1) * LANES)
+        own = blocks[0][tile * channels : (tile + 1) * channels, :]
+        out_ref[:, lanes] = conv[spot, part] * factor + gain * own
+        own = blocks[0][(tiles + tile) * channels : (tiles + tile + 1) * channels, :]
+        back_ref[:, lanes] = back[spot, part] * factor + gain * own
+
+
+def convolve(blocks, skip_gain, shards, channels, tokens):
+    per = tokens // BLOCK
+    rows = shards * per * channels
+    tiles = shards * tokens // LANES
+    return pl.pallas_call(
+        functools.partial(convolve_kernel, shards, channels, tokens),
+        out_shape=[jax.ShapeDtypeStruct((channels, tokens), jnp.float32)] * 2,
+        in_specs=[pl.BlockSpec(memory_space=pltpu.VMEM)] * (shards + 1),
+        out_specs=[pl.BlockSpec(memory_space=pltpu.VMEM)] * 2,
+        scratch_shapes=[pltpu.VMEM((2 * rows, BLOCK), jnp.bfloat16)] * 4
+        + [pltpu.VMEM((tiles, LANES), jnp.float32)]
+        + [pltpu.VMEM((tiles + 1, LANES, LANES), jnp.bfloat16)] * 2,
+        compiler_params=pltpu.CompilerParams(vmem_limit_bytes=KERNEL_BYTES),
+        cost_estimate=pl.CostEstimate(
+            flops=2 * 3 * (shards + 1) * per * per * channels * BLOCK * BLOCK,
+            bytes_accessed=4 * rows * BLOCK * 2,
+            transcendentals=0,
+        ),
+        name="convolve",
+    )(*blocks, skip_gain.reshape(1, channels))
+
+
+def sum_over_chan(value):
+    groups = lax.axis_size("chan")
+    parts = [
+        lax.ppermute(value, "chan", [(i, (i + step) % groups) for i in range(groups)])
+        for step in range(1, groups)
+    ]
+    return sum(parts, value)
+
+
+def direct_body(signal, filter_taps, skip_gain, cotangent):
+    shards = lax.axis_size("context")
+    channels, tokens = signal.shape
+    stacked = stack_local(signal, cotangent, filter_taps)
+    blocks = gather_blocks(stacked, shards)
+    partial_value = filter_grad(blocks, shards, channels, tokens)
+    output, grad_signal = convolve(blocks, skip_gain, shards, channels, tokens)
+    grad_filter = sum_over_chan(partial_value).reshape(tokens) * (1.0 / math.sqrt(shards * tokens))
+    return (output, grad_signal, grad_filter)
 
 
 def rotation(first, second, period):
@@ -118,7 +383,7 @@
     return blocks.reshape(blocks.shape[0], signals, length)
 
 
-def body(signal, filter_taps, skip_gain, cotangent):
+def transform_body(signal, filter_taps, skip_gain, cotangent):
     shards = lax.axis_size("context")
     channels, length = signal.shape
     factor = 1.0 / (2 * shards * length * math.sqrt(shards * length))
@@ -150,6 +415,20 @@
     return (output, grad_signal, grad_filter)
 
 
+def fits_direct(channels, tokens, shards):
+    held = 4 * shards * tokens * (2 * channels + 1)
+    scratch = 16 * shards * tokens * channels + 4 * (shards * tokens + LANES) * LANES
+    whole = channels % PACKED_ROWS == 0 and tokens % (8 * LANES) == 0 and shards & (shards - 1) == 0
+    return whole and shards > 1 and 2 * held + scratch < KERNEL_BYTES // 2
+
+
+def body(signal, filter_taps, skip_gain, cotangent):
+    channels, tokens = signal.shape
+    if fits_direct(channels, tokens, lax.axis_size("context")):
+        return direct_body(signal, filter_taps, skip_gain, cotangent)
+    return transform_body(signal, filter_taps, skip_gain, cotangent)
+
+
 def solution(mesh):
     return jax.shard_map(
         body,

time: 73.4 us -> 32.4 us (0.44)
  blocking collectives: 30.1 us -> 0 us
  Pallas kernels: 0 us -> 12.7 us
  matrix products: 9.89 us -> 0 us
  waiting for transfers between devices: 15.5 us -> 7.66 us
  local copies, waits for them, and re-layouts: 4.92 us -> 0.91 us
  other arithmetic: 2.84 us -> 0.61 us
  starting transfers between devices: 8.71 us -> 9.64 us
    all_to_all x2 -> x0, blocking collectives: 17.5 us -> none  [the longest x1 9.52 us: inverse(): lax.all_to_all(jnp.stack([real_part, imag_part]), 'context', split_axis=4...]
    all_to_all x2 -> x0, waiting for transfers between devices: 15.5 us -> none  [the longest x1 9.74 us: forward(): lax.all_to_all(spectra, 'context', split_axis=4, concat_axis=4, tiled=True)]
    pallas_call x0 -> x3, Pallas kernels: none -> 12.7 us  [the longest x1 9.43 us: convolve(): pl.pallas_call(functools.partial(convolve_kernel, shards, channels, token...]
    psum x1 -> x0, blocking collectives: 12.6 us -> none  [body(): grad_filter = lax.psum(partial_value * factor, 'chan')]
    dot_general x22 -> x0, matrix products: 9.89 us -> none  [the longest x2 1.29 us: along_slow(): jnp.einsum('gsjd,sa->gajd', imag_part, sine_table, precision=exact_mode)]
    ppermute x0 -> x10, starting transfers between devices: none -> 9.64 us  [the longest x7 4.98 us: flipped(): lax.ppermute(value, 'context', [(i, i ^ bits) for i in range(shards)])]
    all_to_all x2 -> x0, starting transfers between devices: 8.71 us -> none  [the longest x1 5.17 us: forward(): lax.all_to_all(blocks, 'context', split_axis=2, concat_axis=2, tiled=True)]
    ppermute x0 -> x10, waiting for transfers between devices: none -> 7.66 us  [the longest x7 7.66 us: flipped(): lax.ppermute(value, 'context', [(i, i ^ bits) for i in range(shards)])]
  transfers between devices with their start and end apart: 2 -> 10, of which waited for: 2 -> 4; matrix products, arithmetic and copies ran while one was open for 0% -> 0% of each run, Pallas kernels for 0% -> 29%
where the time goes in v1:
time: 32.4 us; the launch traced here: 32.2 us
  Pallas kernels  12.7 us (39%)
  starting transfers between devices  9.64 us (30%)
  waiting for transfers between devices  7.66 us (24%)
  local copies, waits for them, and re-layouts  0.91 us (3%)
  between operations  0.66 us (2%)
  other arithmetic  0.61 us (2%)
    pallas_call x1, Pallas kernels, convolve(): pl.pallas_call(functools.partial(convolve_kernel, shards, channels, token...  9.43 us
    ppermute x7, waiting for transfers between devices, flipped(): lax.ppermute(value, 'context', [(i, i ^ bits) for i in range(shards)])  7.66 us
    ppermute x7, starting transfers between devices, flipped(): lax.ppermute(value, 'context', [(i, i ^ bits) for i in range(shards)])  4.98 us
    ppermute x3, starting transfers between devices, sum_over_chan(): lax.ppermute(value, 'chan', [(i, (i + step) % groups) for i in range(grou...  4.66 us
    pallas_call x1, Pallas kernels, filter_grad(): pl.pallas_call(functools.partial(filter_grad_kernel, shards, channels, to...  1.75 us
    pallas_call x1, Pallas kernels, stack_local(): pl.pallas_call(stack_kernel, out_shape=jax.ShapeDtypeStruct((rows, LANES)...  1.54 us
    unnamed x4, local copies, waits for them, and re-layouts  0.91 us
  transfers between devices with their start and end apart: 10, of which 4 were waited for; matrix products, arithmetic and copies ran while one was open for 0% of the time, Pallas kernels for 29%

profile of v1, /device:TPU:0, one launch (start us, length us, event | category | flops | bytes accessed | tf_op | source)
XLA Modules:
  0.0 32.2 jit_solution(17267171743528067212)
XLA Ops:
  0.6 1.5 %stack_local.1.refs_0_ = f32[264,128]{1,0:T(8,128)} custom-call(f32[16,1024]{1,0:T(8,128)} %signal_ref.1, f32[16,1024]{1,0:T(8,128)} %cotangent_ref.1, f32[8,128]{1,0:T(8,128)} %bitcast.4), custom_call_target="tpu_custom_call" | custom-call | tf_op jit(solution)/shard_map/stack_local/pallas_call | solution.py:52
  2.2 2.9 %collective-permute-start.1 = (f32[264,128]{1,0:T(8,128)}, f32[264,128]{1,0:T(8,128)S(1)}, u32[]{:S(2)}, u32[]{:S(2)}) collective-permute-start(f32[264,128]{1,0:T(8,128)} %stack_local.1.refs_0_), channel_id=1, source_target_pairs={{0,8},{4,12},{8,0},{12,4},{16,24},{20,28},{24,16},{28,20},{1,9},{5... | collective-permute-start | bytes 405512 | tf_op jit(solution)/shard_map/ppermute | solution.py:63
  5.1 1.5 %collective-permute-start.3 = (f32[264,128]{1,0:T(8,128)}, f32[264,128]{1,0:T(8,128)S(1)}, u32[]{:S(2)}, u32[]{:S(2)}) collective-permute-start(f32[264,128]{1,0:T(8,128)} %stack_local.1.refs_0_), channel_id=1, source_target_pairs={{0,16},{4,20},{8,24},{12,28},{16,0},{20,4},{24,8},{28,12},{1,17},{... | collective-permute-start | bytes 405512 | tf_op jit(solution)/shard_map/ppermute | solution.py:63
  6.6 0.0 collective-permute-start.5
  6.6 0.0 collective-permute-start
  6.6 2.8 %collective-permute-done.1.refs_2_ = f32[264,128]{1,0:T(8,128)S(1)} collective-permute-done((f32[264,128]{1,0:T(8,128)}, f32[264,128]{1,0:T(8,128)S(1)}, u32[]{:S(2)}, u32[]{:S(2)}) %collective-permute-start.1) | collective-permute-done | bytes 135200 | tf_op jit(solution)/shard_map/ppermute | solution.py:63
  9.4 0.0 collective-permute-start.2
  9.4 3.8 %collective-permute-done.3.refs_4_ = f32[264,128]{1,0:T(8,128)S(1)} collective-permute-done((f32[264,128]{1,0:T(8,128)}, f32[264,128]{1,0:T(8,128)S(1)}, u32[]{:S(2)}, u32[]{:S(2)}) %collective-permute-start.3) | collective-permute-done | bytes 135200 | tf_op jit(solution)/shard_map/ppermute | solution.py:63
  13.3 0.0 collective-permute-start.4
  13.3 0.0 collective-permute-done.5.refs_6_
  13.3 0.5 %collective-permute-start.6 = (f32[264,128]{1,0:T(8,128)S(1)}, f32[264,128]{1,0:T(8,128)S(1)}, u32[]{:S(2)}, u32[]{:S(2)}) collective-permute-start(f32[264,128]{1,0:T(8,128)S(1)} %collective-permute-done.5.refs_6_), channel_id=1, source_target_pairs={{0,4},{4,0},{8,12},{12,8},{16,20},{20,16},{24,28},{28,24},{1,5},{5... | collective-permute-start | bytes 405512 | tf_op jit(solution)/shard_map/ppermute | solution.py:63
  13.8 0.0 collective-permute-done.refs_1_
  13.8 0.0 collective-permute-done.2.refs_3_
  13.8 0.8 %collective-permute-done.4.refs_5_ = f32[264,128]{1,0:T(8,128)S(1)} collective-permute-done((f32[264,128]{1,0:T(8,128)S(1)}, f32[264,128]{1,0:T(8,128)S(1)}, u32[]{:S(2)}, u32[]{:S(2)}) %collective-permute-start.4) | collective-permute-done | bytes 135200 | tf_op jit(solution)/shard_map/ppermute | solution.py:63
  14.6 0.2 collective-permute-done.6.refs_7_
  14.8 0.0 copy-start
  14.8 0.9 %copy-done = f32[264,128]{1,0:T(8,128)S(1)} copy-done((f32[264,128]{1,0:T(8,128)S(1)}, f32[264,128]{1,0:T(8,128)}, u32[]{:S(2)}) %copy-start) | copy-done | bytes 135192
  15.7 1.8 %filter_grad.1 = f32[1,1024]{1,0:T(1,128)S(1)} custom-call(f32[264,128]{1,0:T(8,128)S(1)} %copy-done, f32[264,128]{1,0:T(8,128)S(1)} %collective-permute-done.refs_1_, f32[264,128]{1,0:T(8,128)S(1)} %collective-permute-done.1.refs_2_, f32[264,128]{1,0:T(8,128)S(1)} %collective-permute-done.2.refs_3_, f32[264,128]{1,0:T(8,128)S(1)} %collective-permute-done.3.refs_4_, ...), custom_call_target="tpu_custom_call" | custom-call | flops 1006632960 | bytes 1048576 | tf_op jit(solution)/shard_map/filter_grad/pallas_call | solution.py:122
  17.5 0.0 copy-start.1
  17.5 3.7 %collective-permute-start.9 = (f32[1,1024]{1,0:T(1,128)S(1)}, f32[1,1024]{1,0:T(1,128)S(1)}, u32[]{:S(2)}, u32[]{:S(2)}) collective-permute-start(f32[1,1024]{1,0:T(1,128)S(1)} %filter_grad.1), channel_id=1, source_target_pairs={{0,3},{1,0},{2,1},{3,2},{4,7},{5,4},{6,5},{7,6},{8,11},{9,8},{10,9... | collective-permute-start | bytes 12296 | tf_op jit(solution)/shard_map/ppermute | solution.py:259
  21.1 0.0 collective-permute-start.8
  21.1 1.0 %collective-permute-start.7 = (f32[1,1024]{1,0:T(1,128)S(1)}, f32[1,1024]{1,0:T(1,128)S(1)}, u32[]{:S(2)}, u32[]{:S(2)}) collective-permute-start(f32[1,1024]{1,0:T(1,128)S(1)} %filter_grad.1), channel_id=1, source_target_pairs={{0,1},{1,2},{2,3},{3,0},{4,5},{5,6},{6,7},{7,4},{8,9},{9,10},{10,1... | collective-permute-start | bytes 12296 | tf_op jit(solution)/shard_map/ppermute | solution.py:259
  22.2 0.0 copy-done.1
  22.2 9.4 %convolve.1 = (f32[16,1024]{1,0:T(8,128)}, f32[16,1024]{1,0:T(8,128)}) custom-call(f32[264,128]{1,0:T(8,128)S(1)} %copy-done, f32[264,128]{1,0:T(8,128)S(1)} %collective-permute-done.refs_1_, f32[264,128]{1,0:T(8,128)S(1)} %collective-permute-done.1.refs_2_, f32[264,128]{1,0:T(8,128)S(1)} %collective-permute-done.2.refs_3_, ...), custom_call_target="tpu_custom_call" | custom-call | flops 905969664 | bytes 1048576 | tf_op jit(solution)/shard_map/convolve/pallas_call | solution.py:238
  31.6 0.0 collective-permute-done.9
  31.6 0.0 collective-permute-done.8
  31.6 0.0 collective-permute-done.7
  31.6 0.6 %add_multiply_fusion = f32[1,1024]{1,0:T(1,128)} fusion(f32[1,1024]{1,0:T(1,128)S(1)} %collective-permute-done.9, f32[1,1024]{1,0:T(1,128)S(1)} %collective-permute-done.8, f32[1,1024]{1,0:T(1,128)S(1)} %filter_grad.1, f32[1,1024]{1,0:T(1,128)S(1)} %collective-permute-done.7), kind=kLoop, calls=%fused_computation | loop fusion | flops 4096 | bytes 20480 | tf_op jit(solution)/shard_map/mul | solution.py:272
Async XLA Ops:
  2.2 7.2 %collective-permute-start.1 = (f32[264,128]{1,0:T(8,128)}, f32[264,128]{1,0:T(8,128)S(1)}, u32[]{:S(2)}, u32[]{:S(2)}) collective-permute-start(f32[264,128]{1,0:T(8,128)} %stack_local.1.refs_0_), channel_id=1, source_target_pairs={{0,8},{4,12},{8,0},{12,4},{16,24},{20,28},{24,16},{28,20},{1,9},{5... | collective-permute-start | bytes 405512 | tf_op jit(solution)/shard_map/ppermute | solution.py:63
  5.1 8.2 %collective-permute-start.3 = (f32[264,128]{1,0:T(8,128)}, f32[264,128]{1,0:T(8,128)S(1)}, u32[]{:S(2)}, u32[]{:S(2)}) collective-permute-start(f32[264,128]{1,0:T(8,128)} %stack_local.1.refs_0_), channel_id=1, source_target_pairs={{0,16},{4,20},{8,24},{12,28},{16,0},{20,4},{24,8},{28,12},{1,17},{... | collective-permute-start | bytes 405512 | tf_op jit(solution)/shard_map/ppermute | solution.py:63
  6.6 6.6 %collective-permute-start.5 = (f32[264,128]{1,0:T(8,128)}, f32[264,128]{1,0:T(8,128)S(1)}, u32[]{:S(2)}, u32[]{:S(2)}) collective-permute-start(f32[264,128]{1,0:T(8,128)} %stack_local.1.refs_0_), channel_id=1, source_target_pairs={{0,24},{4,28},{8,16},{12,20},{16,8},{20,12},{24,0},{28,4},{1,25},{... | collective-permute-start | bytes 405512 | tf_op jit(solution)/shard_map/ppermute | solution.py:63
  6.6 7.1 %collective-permute-start = (f32[264,128]{1,0:T(8,128)}, f32[264,128]{1,0:T(8,128)S(1)}, u32[]{:S(2)}, u32[]{:S(2)}) collective-permute-start(f32[264,128]{1,0:T(8,128)} %stack_local.1.refs_0_), channel_id=1, source_target_pairs={{0,4},{4,0},{8,12},{12,8},{16,20},{20,16},{24,28},{28,24},{1,5},{5... | collective-permute-start | bytes 405512 | tf_op jit(solution)/shard_map/ppermute | solution.py:63
  9.4 4.4 %collective-permute-start.2 = (f32[264,128]{1,0:T(8,128)S(1)}, f32[264,128]{1,0:T(8,128)S(1)}, u32[]{:S(2)}, u32[]{:S(2)}) collective-permute-start(f32[264,128]{1,0:T(8,128)S(1)} %collective-permute-done.1.refs_2_), channel_id=1, source_target_pairs={{0,4},{4,0},{8,12},{12,8},{16,20},{20,16},{24,28},{28,24},{1,5},{5... | collective-permute-start | bytes 405512 | tf_op jit(solution)/shard_map/ppermute | solution.py:63
  13.3 1.4 %collective-permute-start.4 = (f32[264,128]{1,0:T(8,128)S(1)}, f32[264,128]{1,0:T(8,128)S(1)}, u32[]{:S(2)}, u32[]{:S(2)}) collective-permute-start(f32[264,128]{1,0:T(8,128)S(1)} %collective-permute-done.3.refs_4_), channel_id=1, source_target_pairs={{0,4},{4,0},{8,12},{12,8},{16,20},{20,16},{24,28},{28,24},{1,5},{5... | collective-permute-start | bytes 405512 | tf_op jit(solution)/shard_map/ppermute | solution.py:63
  13.3 1.5 %collective-permute-start.6 = (f32[264,128]{1,0:T(8,128)S(1)}, f32[264,128]{1,0:T(8,128)S(1)}, u32[]{:S(2)}, u32[]{:S(2)}) collective-permute-start(f32[264,128]{1,0:T(8,128)S(1)} %collective-permute-done.5.refs_6_), channel_id=1, source_target_pairs={{0,4},{4,0},{8,12},{12,8},{16,20},{20,16},{24,28},{28,24},{1,5},{5... | collective-permute-start | bytes 405512 | tf_op jit(solution)/shard_map/ppermute | solution.py:63
  14.8 0.9 %copy-start = (f32[264,128]{1,0:T(8,128)S(1)}, f32[264,128]{1,0:T(8,128)}, u32[]{:S(2)}) copy-start(f32[264,128]{1,0:T(8,128)} %stack_local.1.refs_0_) | copy-start | bytes 405508
  17.5 4.7 %copy-start.1 = (f32[16]{0:T(128)S(1)}, f32[16]{0:T(128)}, u32[]{:S(2)}) copy-start(f32[16]{0:T(128)} %param.6) | copy-start | bytes 196
  17.5 14.1 %collective-permute-start.9 = (f32[1,1024]{1,0:T(1,128)S(1)}, f32[1,1024]{1,0:T(1,128)S(1)}, u32[]{:S(2)}, u32[]{:S(2)}) collective-permute-start(f32[1,1024]{1,0:T(1,128)S(1)} %filter_grad.1), channel_id=1, source_target_pairs={{0,3},{1,0},{2,1},{3,2},{4,7},{5,4},{6,5},{7,6},{8,11},{9,8},{10,9... | collective-permute-start | bytes 12296 | tf_op jit(solution)/shard_map/ppermute | solution.py:259
  21.1 10.5 %collective-permute-start.8 = (f32[1,1024]{1,0:T(1,128)S(1)}, f32[1,1024]{1,0:T(1,128)S(1)}, u32[]{:S(2)}, u32[]{:S(2)}) collective-permute-start(f32[1,1024]{1,0:T(1,128)S(1)} %filter_grad.1), channel_id=1, source_target_pairs={{0,2},{1,3},{2,0},{3,1},{4,6},{5,7},{6,4},{7,5},{8,10},{9,11},{10,... | collective-permute-start | bytes 12296 | tf_op jit(solution)/shard_map/ppermute | solution.py:259
  21.1 10.5 %collective-permute-start.7 = (f32[1,1024]{1,0:T(1,128)S(1)}, f32[1,1024]{1,0:T(1,128)S(1)}, u32[]{:S(2)}, u32[]{:S(2)}) collective-permute-start(f32[1,1024]{1,0:T(1,128)S(1)} %filter_grad.1), channel_id=1, source_target_pairs={{0,1},{1,2},{2,3},{3,0},{4,5},{5,6},{6,7},{7,4},{8,9},{9,10},{10,1... | collective-permute-start | bytes 12296 | tf_op jit(solution)/shard_map/ppermute | solution.py:259

commit v2 on v1

--- a/solution.py
+++ b/solution.py
@@ -51,7 +51,7 @@
     rows = (2 * channels * tokens + tokens) // LANES
     return pl.pallas_call(
         stack_kernel,
-        out_shape=jax.ShapeDtypeStruct((rows, LANES), jnp.float32),
+        out_shape=pltpu.VMEM((rows, LANES), jnp.float32),
         in_specs=[pl.BlockSpec(memory_space=pltpu.VMEM)] * 3,
         out_specs=pl.BlockSpec(memory_space=pltpu.VMEM),
         name="stack_local",
@@ -139,78 +139,100 @@
     )(*blocks)
 
 
+def toeplitz_kernel(shards, channels, tokens, *refs):
+    blocks, high_ref, low_ref, taps = refs[:shards], *refs[shards:]
+    me = lax.axis_index("context")
+    tiles = tokens // LANES
+    first = 2 * channels * tiles
+    taps[0] = jnp.zeros((tiles, LANES), jnp.float32)
+    for bits in range(shards):
+        taps[(me ^ bits) + 1] = blocks[bits][first : first + tiles, :]
+    high_ref[0] = jnp.zeros((LANES, LANES), jnp.bfloat16)
+    low_ref[0] = jnp.zeros((LANES, LANES), jnp.bfloat16)
+    width = (tiles + 1) * LANES
+    row = lax.broadcasted_iota(jnp.int32, (8, width), 0)
+
+    def build(step, carry):
+        last, sheet = taps[step], taps[step + 1]
+        lines = [last[tiles - 1 : tiles, :]] + [sheet[n : n + 1, :] for n in range(tiles)]
+        skewed = jnp.concatenate([jnp.broadcast_to(line, (8, LANES)) for line in lines], axis=1)
+        for bit in (1, 2, 4):
+            skewed = jnp.where((row & bit) != 0, pltpu.roll(skewed, bit, 1), skewed)
+        for group in range(LANES // PACKED_ROWS):
+            top, bottom = (
+                pltpu.roll(skewed, PACKED_ROWS * group + rows, 1) if group + rows else skewed
+                for rows in (0, 8)
+            )
+            pair = halves(jnp.concatenate([top, bottom], axis=0))
+            for ref, part in zip((high_ref, low_ref), pair):
+                for tile in range(tiles):
+                    ref[
+                        step * tiles + tile + 1, group * PACKED_ROWS : (group + 1) * PACKED_ROWS, :
+                    ] = part[:, (tile + 1) * LANES : (tile + 2) * LANES]
+        return carry
+
+    lax.fori_loop(0, shards, build, 0)
+
+
+def toeplitz_tiles(blocks, shards, channels, tokens):
+    tiles = tokens // LANES
+    shape = (shards * tiles + 1, LANES, LANES)
+    return pl.pallas_call(
+        functools.partial(toeplitz_kernel, shards, channels, tokens),
+        out_shape=[pltpu.VMEM(shape, jnp.bfloat16)] * 2,
+        in_specs=[pl.BlockSpec(memory_space=pltpu.VMEM)] * shards,
+        out_specs=[pl.BlockSpec(memory_space=pltpu.VMEM)] * 2,
+        scratch_shapes=[pltpu.VMEM((shards + 1, tiles, LANES), jnp.float32)],
+        compiler_params=pltpu.CompilerParams(vmem_limit_bytes=KERNEL_BYTES),
+        cost_estimate=pl.CostEstimate(
+            flops=16 * shape[0] * LANES * LANES, bytes_accessed=4 * shape[0] * LANES * LANES, transcendentals=0
+        ),
+        name="toeplitz_tiles",
+    )(*blocks)
+
+
+def place_stacked(block_ref, index, channels, tokens, first, ref, start):
+    for tile in range(tokens // LANES):
+        rows = first + tile * channels
+        both = jnp.concatenate(halves(block_ref[rows : rows + channels, :]), axis=0)
+        at = pl.multiple_of((index * (tokens // LANES) + tile) * 2 * channels + start, PACKED_ROWS)
+        ref[pl.ds(at, 2 * channels), :] = both
+
+
 def convolve_kernel(shards, channels, tokens, *refs):
-    blocks, gain_ref, out_ref, back_ref = refs[:shards], *refs[shards : shards + 3]
-    sig_high, sig_low, cot_high, cot_low, taps, toe_high, toe_low = refs[shards + 3 :]
+    blocks, toe_high, toe_low, gain_ref = refs[:shards], *refs[shards : shards + 3]
+    out_ref, back_ref, sig, cot = refs[shards + 3 :]
     me = lax.axis_index("context")
-    per = tokens // BLOCK
-    rows = shards * per * channels
     tiles = tokens // LANES
-    for ref in (sig_high, sig_low):
-        ref[:rows, :] = jnp.zeros((rows, BLOCK), jnp.bfloat16)
-    for ref in (cot_high, cot_low):
-        ref[rows:, :] = jnp.zeros((rows, BLOCK), jnp.bfloat16)
+    rows = 2 * shards * tiles * channels
+    sig[:rows, :] = jnp.zeros((rows, LANES), jnp.bfloat16)
+    cot[rows:, :] = jnp.zeros((rows, LANES), jnp.bfloat16)
     for bits in range(shards):
         index = me ^ bits
-        place_rows(blocks[bits], index, channels, tokens, 0, sig_high, sig_low, rows)
-        place_rows(
-            blocks[bits], index, channels, tokens, channels * tiles, cot_high, cot_low, 0
+        place_stacked(blocks[bits], index, channels, tokens, 0, sig, rows)
+        place_stacked(blocks[bits], index, channels, tokens, channels * tiles, cot, 0)
+    count = 2 * tiles * channels
+
+    def window(ref, tile):
+        return ref[pl.ds(pl.multiple_of(tile * 2 * channels, PACKED_ROWS), count), :]
+
+    def forward(trip, total):
+        lags = [trip * tiles + n for n in range(tiles)]
+        left = jnp.concatenate([window(sig, (shards + me) * tiles - lag) for lag in lags], axis=1)
+        right = jnp.concatenate(
+            [jnp.concatenate([toe_high[lag + 1], toe_low[lag + 1]], axis=1) for lag in lags], axis=0
         )
-        taps[pl.ds(pl.multiple_of(index * tiles, 8), tiles), :] = blocks[bits][2 * channels * tiles :, :]
-    row = lax.broadcasted_iota(jnp.int32, (8, LANES), 0)
-    lane = lax.broadcasted_iota(jnp.int32, (8, LANES), 1)
-    groups = LANES // 8
-    toe_high[0] = jnp.zeros((LANES, LANES), jnp.bfloat16)
-    toe_low[0] = jnp.zeros((LANES, LANES), jnp.bfloat16)
-
-    def build(step, carry):
-        last, rolled = carry
-        sheet = taps[pl.ds(pl.multiple_of(step * 8, 8), 8), :]
-        for line in range(8):
-            now = jnp.broadcast_to(sheet[line : line + 1, :], (8, LANES))
-            for bit in (1, 2, 4):
-                now = jnp.where((row & bit) != 0, pltpu.roll(now, bit, 1), now)
-            skewed = jnp.where(lane < row, last, now)
-            last = now
-            turned = [skewed] + [pltpu.roll(skewed, 8 * g, 1) for g in range(1, groups)]
-            parts = [turned[0]] + [
-                jnp.where(lane < 8 * g, rolled[g], turned[g]) for g in range(1, groups)
-            ]
-            rolled = turned
-            high, low = halves(jnp.concatenate(parts, axis=0))
-            toe_high[step * 8 + line + 1] = high
-            toe_low[step * 8 + line + 1] = low
-        return last, rolled
-
-    blank = jnp.zeros((8, LANES), jnp.float32)
-    lax.fori_loop(0, shards * tiles // 8, build, (blank, [blank] * groups))
-
-    def square(ref, step):
-        return jnp.concatenate(
-            [
-                jnp.concatenate([ref[2 * step + 1], ref[2 * step + 2]], axis=1),
-                jnp.concatenate([ref[2 * step], ref[2 * step + 1]], axis=1),
-            ],
-            axis=0,
+        return total + dot(left, right, 1, 0)
+
+    def backward(trip, total):
+        lags = [trip * tiles + n for n in range(tiles)]
+        left = jnp.concatenate([window(cot, me * tiles + lag) for lag in lags], axis=1)
+        right = jnp.concatenate(
+            [jnp.concatenate([toe_high[lag + 1], toe_low[lag + 1]], axis=0) for lag in lags], axis=1
         )
-
-    def forward(trip, total):
-        for inner in range(per):
-            step = trip * per + inner
-            at = pl.multiple_of(rows + (me * per - step) * channels, PACKED_ROWS)
-            window = (sig_high[pl.ds(at, per * channels), :], sig_low[pl.ds(at, per * channels), :])
-            total = total + dot_halves(window, (square(toe_high, step), square(toe_low, step)), 1, 0)
-        return total
-
-    def backward(trip, total):
-        for inner in range(per):
-            step = trip * per + inner
-            at = pl.multiple_of((me * per + step) * channels, PACKED_ROWS)
-            window = (cot_high[pl.ds(at, per * channels), :], cot_low[pl.ds(at, per * channels), :])
-            total = total + dot_halves(window, (square(toe_high, step), square(toe_low, step)), 1, 1)
-        return total
-
-    start = jnp.zeros((per * channels, BLOCK), jnp.float32)
+        return total + dot(left, right, 1, 1)
+
+    start = jnp.zeros((count, 2 * LANES), jnp.float32)
     conv = lax.fori_loop(0, me + 1, forward, start)
     back = lax.fori_loop(0, shards - me, backward, start)
     factor = 1.0 / math.sqrt(shards * tokens)
@@ -222,54 +244,48 @@
         keepdims=True,
     )
     for tile in range(tiles):
-        spot = slice((tile // 2) * channels, (tile // 2 + 1) * channels)
-        part = slice((tile % 2) * LANES, (tile % 2 + 1) * LANES)
         lanes = slice(tile * LANES, (tile + 1) * LANES)
-        own = blocks[0][tile * channels : (tile + 1) * channels, :]
-        out_ref[:, lanes] = conv[spot, part] * factor + gain * own
-        own = blocks[0][(tiles + tile) * channels : (tiles + tile + 1) * channels, :]
-        back_ref[:, lanes] = back[spot, part] * factor + gain * own
-
-
-def convolve(blocks, skip_gain, shards, channels, tokens):
+        for ref, value, first in ((out_ref, conv, 0), (back_ref, back, tiles)):
+            own = blocks[0][(first + tile) * channels : (first + tile + 1) * channels, :]
+            quarters = value[tile * 2 * channels : (tile + 1) * 2 * channels, :]
+            both = quarters[:channels, :] + quarters[channels:, :]
+            ref[:, lanes] = (both[:, :LANES] + both[:, LANES:]) * factor + gain * own
+
+
+def convolve(blocks, toeplitz, skip_gain, shards, channels, tokens):
     per = tokens // BLOCK
     rows = shards * per * channels
-    tiles = shards * tokens // LANES
     return pl.pallas_call(
         functools.partial(convolve_kernel, shards, channels, tokens),
         out_shape=[jax.ShapeDtypeStruct((channels, tokens), jnp.float32)] * 2,
-        in_specs=[pl.BlockSpec(memory_space=pltpu.VMEM)] * (shards + 1),
+        in_specs=[pl.BlockSpec(memory_space=pltpu.VMEM)] * (shards + 3),
         out_specs=[pl.BlockSpec(memory_space=pltpu.VMEM)] * 2,
-        scratch_shapes=[pltpu.VMEM((2 * rows, BLOCK), jnp.bfloat16)] * 4
-        + [pltpu.VMEM((tiles, LANES), jnp.float32)]
-        + [pltpu.VMEM((tiles + 1, LANES, LANES), jnp.bfloat16)] * 2,
+        scratch_shapes=[pltpu.VMEM((8 * rows, LANES), jnp.bfloat16)] * 2,
         compiler_params=pltpu.CompilerParams(vmem_limit_bytes=KERNEL_BYTES),
         cost_estimate=pl.CostEstimate(
-            flops=2 * 3 * (shards + 1) * per * per * channels * BLOCK * BLOCK,
+            flops=2 * 4 * (shards + 1) * per * per * channels * BLOCK * BLOCK,
             bytes_accessed=4 * rows * BLOCK * 2,
             transcendentals=0,
         ),
         name="convolve",
-    )(*blocks, skip_gain.reshape(1, channels))
-
-
-def sum_over_chan(value):
-    groups = lax.axis_size("chan")
-    parts = [
-        lax.ppermute(value, "chan", [(i, (i + step) % groups) for i in range(groups)])
-        for step in range(1, groups)
-    ]
-    return sum(parts, value)
+    )(*blocks, *toeplitz, skip_gain.reshape(1, channels))
 
 
 def direct_body(signal, filter_taps, skip_gain, cotangent):
-    shards = lax.axis_size("context")
+    shards, groups = lax.axis_size("context"), lax.axis_size("chan")
     channels, tokens = signal.shape
     stacked = stack_local(signal, cotangent, filter_taps)
     blocks = gather_blocks(stacked, shards)
-    partial_value = filter_grad(blocks, shards, channels, tokens)
-    output, grad_signal = convolve(blocks, skip_gain, shards, channels, tokens)
-    grad_filter = sum_over_chan(partial_value).reshape(tokens) * (1.0 / math.sqrt(shards * tokens))
+    value = filter_grad(blocks, shards, channels, tokens)
+    toeplitz = toeplitz_tiles(blocks, shards, channels, tokens)
+    bits = 1
+    while bits < groups:
+        value = value + lax.ppermute(value, "chan", [(i, i ^ bits) for i in range(groups)])
+        if bits == 1:
+            value, *toeplitz = lax.optimization_barrier((value, *toeplitz))
+        bits *= 2
+    output, grad_signal = convolve(blocks, toeplitz, skip_gain, shards, channels, tokens)
+    grad_filter = value.reshape(tokens) * (1.0 / math.sqrt(shards * tokens))
     return (output, grad_signal, grad_filter)
 
 
@@ -418,7 +434,8 @@
 def fits_direct(channels, tokens, shards):
     held = 4 * shards * tokens * (2 * channels + 1)
     scratch = 16 * shards * tokens * channels + 4 * (shards * tokens + LANES) * LANES
-    whole = channels % PACKED_ROWS == 0 and tokens % (8 * LANES) == 0 and shards & (shards - 1) == 0
+    groups = lax.axis_size("chan")
+    whole = groups & (groups - 1) == 0 and channels % PACKED_ROWS == 0 and tokens % (8 * LANES) == 0 and shards & (shards - 1) == 0
     return whole and shards > 1 and 2 * held + scratch < KERNEL_BYTES // 2
 
 

time: 32.4 us -> 28.4 us (0.88)
  Pallas kernels: 12.7 us -> 10.4 us
  local copies, waits for them, and re-layouts: 0.91 us -> 0.01 us
  waiting for transfers between devices: 7.66 us -> 7.16 us
    pallas_call x1, Pallas kernels: 9.43 us -> 4.21 us  [convolve(): pl.pallas_call(functools.partial(convolve_kernel, shards, channels, token...]
    pallas_call x1 -> x2, Pallas kernels: 1.54 us -> 4.47 us  [the longest x1 3.59 us: toeplitz_tiles(): pl.pallas_call(functools.partial(toeplitz_kernel, shards, channels, token...]
    unnamed x4 -> x2, local copies, waits for them, and re-layouts: 0.91 us -> 0.01 us
    ppermute x7, waiting for transfers between devices: 7.66 us -> 7.16 us  [flipped(): lax.ppermute(value, 'context', [(i, i ^ bits) for i in range(shards)])]
    ppermute x3 -> x2, starting transfers between devices: 4.66 us -> 4.43 us  [direct_body(): lax.ppermute(value, 'chan', [(i, i ^ bits) for i in range(groups)])]
  transfers between devices with their start and end apart: 10 -> 9, of which waited for: 4 -> 5; matrix products, arithmetic and copies ran while one was open for 0% -> 0% of each run, Pallas kernels for 29% -> 28%
where the time goes in v2:
time: 28.4 us; the launch traced here: 28.2 us
  Pallas kernels  10.4 us (37%)
  starting transfers between devices  9.32 us (33%)
  waiting for transfers between devices  7.16 us (25%)
  between operations  0.68 us (2%)
  other arithmetic  0.61 us (2%)
    ppermute x7, waiting for transfers between devices, flipped(): lax.ppermute(value, 'context', [(i, i ^ bits) for i in range(shards)])  7.16 us
    ppermute x7, starting transfers between devices, flipped(): lax.ppermute(value, 'context', [(i, i ^ bits) for i in range(shards)])  4.88 us
    ppermute x2, starting transfers between devices, direct_body(): lax.ppermute(value, 'chan', [(i, i ^ bits) for i in range(groups)])  4.43 us
    pallas_call x1, Pallas kernels, convolve(): pl.pallas_call(functools.partial(convolve_kernel, shards, channels, token...  4.21 us
    pallas_call x1, Pallas kernels, toeplitz_tiles(): pl.pallas_call(functools.partial(toeplitz_kernel, shards, channels, token...  3.59 us
    pallas_call x1, Pallas kernels, filter_grad(): pl.pallas_call(functools.partial(filter_grad_kernel, shards, channels, to...  1.76 us
    pallas_call x1, Pallas kernels, stack_local(): pl.pallas_call(stack_kernel, out_shape=pltpu.VMEM((rows, LANES), jnp.floa...  0.88 us
    mul x1, other arithmetic, direct_body(): grad_filter = value.reshape(tokens) * (1.0 / math.sqrt(shards * tokens))  0.6 us
  transfers between devices with their start and end apart: 9, of which 5 were waited for; matrix products, arithmetic and copies ran while one was open for 0% of the time, Pallas kernels for 28%

profile of v2, /device:TPU:0, one launch (start us, length us, event | category | flops | bytes accessed | tf_op | source)
XLA Modules:
  0.0 28.2 jit_solution(1782982656148128196)
XLA Ops:
  0.6 0.9 %stack_local.1.refs_0_ = f32[264,128]{1,0:T(8,128)S(1)} custom-call(f32[16,1024]{1,0:T(8,128)} %signal_ref.1, f32[16,1024]{1,0:T(8,128)} %cotangent_ref.1, f32[8,128]{1,0:T(8,128)} %bitcast.4), custom_call_target="tpu_custom_call" | custom-call | tf_op jit(solution)/shard_map/stack_local/pallas_call | solution.py:52
  1.5 0.0 copy-start
  1.5 4.0 %collective-permute-start.5 = (f32[264,128]{1,0:T(8,128)S(1)}, f32[264,128]{1,0:T(8,128)S(1)}, u32[]{:S(2)}, u32[]{:S(2)}) collective-permute-start(f32[264,128]{1,0:T(8,128)S(1)} %stack_local.1.refs_0_), channel_id=1, source_target_pairs={{0,24},{4,28},{8,16},{12,20},{16,8},{20,12},{24,0},{28,4},{1,25},{... | collective-permute-start | bytes 405512 | tf_op jit(solution)/shard_map/ppermute | solution.py:63
  5.5 0.5 %collective-permute-start.3 = (f32[264,128]{1,0:T(8,128)S(1)}, f32[264,128]{1,0:T(8,128)S(1)}, u32[]{:S(2)}, u32[]{:S(2)}) collective-permute-start(f32[264,128]{1,0:T(8,128)S(1)} %stack_local.1.refs_0_), channel_id=1, source_target_pairs={{0,16},{4,20},{8,24},{12,28},{16,0},{20,4},{24,8},{28,12},{1,17},{... | collective-permute-start | bytes 405512 | tf_op jit(solution)/shard_map/ppermute | solution.py:63
  6.0 0.1 collective-permute-start.1
  6.1 0.0 collective-permute-start
  6.1 3.3 %collective-permute-done.5.refs_6_ = f32[264,128]{1,0:T(8,128)S(1)} collective-permute-done((f32[264,128]{1,0:T(8,128)S(1)}, f32[264,128]{1,0:T(8,128)S(1)}, u32[]{:S(2)}, u32[]{:S(2)}) %collective-permute-start.5) | collective-permute-done | bytes 135200 | tf_op jit(solution)/shard_map/ppermute | solution.py:63
  9.5 0.0 collective-permute-start.6
  9.5 2.5 %collective-permute-done.3.refs_4_ = f32[264,128]{1,0:T(8,128)S(1)} collective-permute-done((f32[264,128]{1,0:T(8,128)S(1)}, f32[264,128]{1,0:T(8,128)S(1)}, u32[]{:S(2)}, u32[]{:S(2)}) %collective-permute-start.3) | collective-permute-done | bytes 135200 | tf_op jit(solution)/shard_map/ppermute | solution.py:63
  12.0 0.0 collective-permute-start.4
  12.0 0.2 collective-permute-done.1.refs_2_
  12.2 0.3 collective-permute-start.2
  12.5 0.0 collective-permute-done.refs_1_
  12.5 0.0 collective-permute-done.6.refs_7_
  12.5 0.8 %collective-permute-done.4.refs_5_ = f32[264,128]{1,0:T(8,128)S(1)} collective-permute-done((f32[264,128]{1,0:T(8,128)S(1)}, f32[264,128]{1,0:T(8,128)S(1)}, u32[]{:S(2)}, u32[]{:S(2)}) %collective-permute-start.4) | collective-permute-done | bytes 135200 | tf_op jit(solution)/shard_map/ppermute | solution.py:63
  13.3 0.2 collective-permute-done.2.refs_3_
  13.6 1.8 %filter_grad.1 = f32[1,1024]{1,0:T(1,128)S(1)} custom-call(f32[264,128]{1,0:T(8,128)S(1)} %stack_local.1.refs_0_, f32[264,128]{1,0:T(8,128)S(1)} %collective-permute-done.refs_1_, f32[264,128]{1,0:T(8,128)S(1)} %collective-permute-done.1.refs_2_, f32[264,128]{1,0:T(8,128)S(1)} %collective-permute-done.2.refs_3_, ...), custom_call_target="tpu_custom_call" | custom-call | flops 1006632960 | bytes 1048576 | tf_op jit(solution)/shard_map/filter_grad/pallas_call | solution.py:122
  15.3 1.8 %collective-permute-start.7 = (f32[1,1024]{1,0:T(1,128)S(1)}, f32[1,1024]{1,0:T(1,128)S(1)}, u32[]{:S(2)}, u32[]{:S(2)}) collective-permute-start(f32[1,1024]{1,0:T(1,128)S(1)} %filter_grad.1), channel_id=1, source_target_pairs={{0,1},{1,0},{2,3},{3,2},{4,5},{5,4},{6,7},{7,6},{8,9},{9,8},{10,11... | collective-permute-start | bytes 12296 | tf_op jit(solution)/shard_map/ppermute | solution.py:283
  17.1 3.6 %toeplitz_tiles.1 = (bf16[65,128,128]{2,1,0:T(8,128)(2,1)S(1)}, bf16[65,128,128]{2,1,0:T(8,128)(2,1)S(1)}) custom-call(f32[264,128]{1,0:T(8,128)S(1)} %stack_local.1.refs_0_, f32[264,128]{1,0:T(8,128)S(1)} %collective-permute-done.refs_1_, f32[264,128]{1,0:T(8,128)S(1)} %collective-permute-done.1.refs_2_, f32[264,128]{1,0:T(8,128)S(1)} %collective-permute-done.2.refs_3_, ...), custom_call_target="tpu_custom_call" | custom-call | flops 17039360 | bytes 4259840 | tf_op jit(solution)/shard_map/toeplitz_tiles/pallas_call | solution.py:180
  20.7 0.0 collective-permute-done.7
  20.7 2.7 %collective-permute-start.8 = (f32[1,1024]{1,0:T(1,128)S(1)}, f32[1,1024]{1,0:T(1,128)S(1)}, u32[]{:S(2)}, u32[]{:S(2)}) collective-permute-start(f32[1,1024]{1,0:T(1,128)S(1)} %add.6), channel_id=1, source_target_pairs={{0,2},{1,3},{2,0},{3,1},{4,6},{5,7},{6,4},{7,5},{8,10},{9,11},{10,... | collective-permute-start | bytes 12296 | tf_op jit(solution)/shard_map/ppermute | solution.py:283
  23.4 0.0 copy-done
  23.4 4.2 %convolve.1 = (f32[16,1024]{1,0:T(8,128)}, f32[16,1024]{1,0:T(8,128)}) custom-call(f32[264,128]{1,0:T(8,128)S(1)} %stack_local.1.refs_0_, f32[264,128]{1,0:T(8,128)S(1)} %collective-permute-done.refs_1_, f32[264,128]{1,0:T(8,128)S(1)} %collective-permute-done.1.refs_2_, f32[264,128]{1,0:T(8,128)S(1)} %collective-permute-done.2.refs_3_, ...), custom_call_target="tpu_custom_call" | custom-call | flops 1207959552 | bytes 1048576 | tf_op jit(solution)/shard_map/convolve/pallas_call | solution.py:258
  27.6 0.0 collective-permute-done.8
  27.6 0.6 %add_multiply_fusion = f32[1,1024]{1,0:T(1,128)} fusion(f32[1,1024]{1,0:T(1,128)S(1)} %add.6, f32[1,1024]{1,0:T(1,128)S(1)} %collective-permute-done.8), kind=kLoop, calls=%fused_computation | loop fusion | flops 2048 | bytes 12288 | tf_op jit(solution)/shard_map/mul | solution.py:288
  (1 shorter events, 0.0 us)
Async XLA Ops:
  1.5 21.9 %copy-start = (f32[16]{0:T(128)S(1)}, f32[16]{0:T(128)}, u32[]{:S(2)}) copy-start(f32[16]{0:T(128)} %param.6) | copy-start | bytes 196
  1.5 8.0 %collective-permute-start.5 = (f32[264,128]{1,0:T(8,128)S(1)}, f32[264,128]{1,0:T(8,128)S(1)}, u32[]{:S(2)}, u32[]{:S(2)}) collective-permute-start(f32[264,128]{1,0:T(8,128)S(1)} %stack_local.1.refs_0_), channel_id=1, source_target_pairs={{0,24},{4,28},{8,16},{12,20},{16,8},{20,12},{24,0},{28,4},{1,25},{... | collective-permute-start | bytes 405512 | tf_op jit(solution)/shard_map/ppermute | solution.py:63
  5.5 6.5 %collective-permute-start.3 = (f32[264,128]{1,0:T(8,128)S(1)}, f32[264,128]{1,0:T(8,128)S(1)}, u32[]{:S(2)}, u32[]{:S(2)}) collective-permute-start(f32[264,128]{1,0:T(8,128)S(1)} %stack_local.1.refs_0_), channel_id=1, source_target_pairs={{0,16},{4,20},{8,24},{12,28},{16,0},{20,4},{24,8},{28,12},{1,17},{... | collective-permute-start | bytes 405512 | tf_op jit(solution)/shard_map/ppermute | solution.py:63
  6.0 6.2 %collective-permute-start.1 = (f32[264,128]{1,0:T(8,128)S(1)}, f32[264,128]{1,0:T(8,128)S(1)}, u32[]{:S(2)}, u32[]{:S(2)}) collective-permute-start(f32[264,128]{1,0:T(8,128)S(1)} %stack_local.1.refs_0_), channel_id=1, source_target_pairs={{0,8},{4,12},{8,0},{12,4},{16,24},{20,28},{24,16},{28,20},{1,9},{5... | collective-permute-start | bytes 405512 | tf_op jit(solution)/shard_map/ppermute | solution.py:63
  6.1 6.4 %collective-permute-start = (f32[264,128]{1,0:T(8,128)S(1)}, f32[264,128]{1,0:T(8,128)S(1)}, u32[]{:S(2)}, u32[]{:S(2)}) collective-permute-start(f32[264,128]{1,0:T(8,128)S(1)} %stack_local.1.refs_0_), channel_id=1, source_target_pairs={{0,4},{4,0},{8,12},{12,8},{16,20},{20,16},{24,28},{28,24},{1,5},{5... | collective-permute-start | bytes 405512 | tf_op jit(solution)/shard_map/ppermute | solution.py:63
  9.5 3.0 %collective-permute-start.6 = (f32[264,128]{1,0:T(8,128)S(1)}, f32[264,128]{1,0:T(8,128)S(1)}, u32[]{:S(2)}, u32[]{:S(2)}) collective-permute-start(f32[264,128]{1,0:T(8,128)S(1)} %collective-permute-done.5.refs_6_), channel_id=1, source_target_pairs={{0,4},{4,0},{8,12},{12,8},{16,20},{20,16},{24,28},{28,24},{1,5},{5... | collective-permute-start | bytes 405512 | tf_op jit(solution)/shard_map/ppermute | solution.py:63
  12.0 1.4 %collective-permute-start.4 = (f32[264,128]{1,0:T(8,128)S(1)}, f32[264,128]{1,0:T(8,128)S(1)}, u32[]{:S(2)}, u32[]{:S(2)}) collective-permute-start(f32[264,128]{1,0:T(8,128)S(1)} %collective-permute-done.3.refs_4_), channel_id=1, source_target_pairs={{0,4},{4,0},{8,12},{12,8},{16,20},{20,16},{24,28},{28,24},{1,5},{5... | collective-permute-start | bytes 405512 | tf_op jit(solution)/shard_map/ppermute | solution.py:63
  12.2 1.4 %collective-permute-start.2 = (f32[264,128]{1,0:T(8,128)S(1)}, f32[264,128]{1,0:T(8,128)S(1)}, u32[]{:S(2)}, u32[]{:S(2)}) collective-permute-start(f32[264,128]{1,0:T(8,128)S(1)} %collective-permute-done.1.refs_2_), channel_id=1, source_target_pairs={{0,4},{4,0},{8,12},{12,8},{16,20},{20,16},{24,28},{28,24},{1,5},{5... | collective-permute-start | bytes 405512 | tf_op jit(solution)/shard_map/ppermute | solution.py:63
  15.3 5.4 %collective-permute-start.7 = (f32[1,1024]{1,0:T(1,128)S(1)}, f32[1,1024]{1,0:T(1,128)S(1)}, u32[]{:S(2)}, u32[]{:S(2)}) collective-permute-start(f32[1,1024]{1,0:T(1,128)S(1)} %filter_grad.1), channel_id=1, source_target_pairs={{0,1},{1,0},{2,3},{3,2},{4,5},{5,4},{6,7},{7,6},{8,9},{9,8},{10,11... | collective-permute-start | bytes 12296 | tf_op jit(solution)/shard_map/ppermute | solution.py:283
  20.7 6.9 %collective-permute-start.8 = (f32[1,1024]{1,0:T(1,128)S(1)}, f32[1,1024]{1,0:T(1,128)S(1)}, u32[]{:S(2)}, u32[]{:S(2)}) collective-permute-start(f32[1,1024]{1,0:T(1,128)S(1)} %add.6), channel_id=1, source_target_pairs={{0,2},{1,3},{2,0},{3,1},{4,6},{5,7},{6,4},{7,5},{8,10},{9,11},{10,... | collective-permute-start | bytes 12296 | tf_op jit(solution)/shard_map/ppermute | solution.py:283

commit v3 on v2

--- a/solution.py
+++ b/solution.py
@@ -140,7 +140,7 @@
 
 
 def toeplitz_kernel(shards, channels, tokens, *refs):
-    blocks, high_ref, low_ref, taps = refs[:shards], *refs[shards:]
+    blocks, high_ref, low_ref, taps, skew = refs[:shards], *refs[shards:]
     me = lax.axis_index("context")
     tiles = tokens // LANES
     first = 2 * channels * tiles
@@ -150,14 +150,16 @@
     high_ref[0] = jnp.zeros((LANES, LANES), jnp.bfloat16)
     low_ref[0] = jnp.zeros((LANES, LANES), jnp.bfloat16)
     width = (tiles + 1) * LANES
-    row = lax.broadcasted_iota(jnp.int32, (8, width), 0)
-
-    def build(step, carry):
+
+    for step in range(shards):
         last, sheet = taps[step], taps[step + 1]
         lines = [last[tiles - 1 : tiles, :]] + [sheet[n : n + 1, :] for n in range(tiles)]
-        skewed = jnp.concatenate([jnp.broadcast_to(line, (8, LANES)) for line in lines], axis=1)
-        for bit in (1, 2, 4):
-            skewed = jnp.where((row & bit) != 0, pltpu.roll(skewed, bit, 1), skewed)
+        lean = jnp.concatenate([jnp.broadcast_to(line, (8, LANES)) for line in lines], axis=1)
+        lean = pltpu.roll(lean, 0, 1, stride=1, stride_axis=0)
+        skew[step] = lean
+
+    def build(step, carry):
+        skewed = skew[step]
         for group in range(LANES // PACKED_ROWS):
             top, bottom = (
                 pltpu.roll(skewed, PACKED_ROWS * group + rows, 1) if group + rows else skewed
@@ -171,7 +173,7 @@
                     ] = part[:, (tile + 1) * LANES : (tile + 2) * LANES]
         return carry
 
-    lax.fori_loop(0, shards, build, 0)
+    lax.fori_loop(0, shards, build, 0, unroll=min(4, shards))
 
 
 def toeplitz_tiles(blocks, shards, channels, tokens):
@@ -182,7 +184,7 @@
         out_shape=[pltpu.VMEM(shape, jnp.bfloat16)] * 2,
         in_specs=[pl.BlockSpec(memory_space=pltpu.VMEM)] * shards,
         out_specs=[pl.BlockSpec(memory_space=pltpu.VMEM)] * 2,
-        scratch_shapes=[pltpu.VMEM((shards + 1, tiles, LANES), jnp.float32)],
+        scratch_shapes=[pltpu.VMEM((shards + 1, tiles, LANES), jnp.float32), pltpu.VMEM((shards, 8, (tiles + 1) * LANES), jnp.float32)],
         compiler_params=pltpu.CompilerParams(vmem_limit_bytes=KERNEL_BYTES),
         cost_estimate=pl.CostEstimate(
             flops=16 * shape[0] * LANES * LANES, bytes_accessed=4 * shape[0] * LANES * LANES, transcendentals=0
@@ -217,24 +219,28 @@
         return ref[pl.ds(pl.multiple_of(tile * 2 * channels, PACKED_ROWS), count), :]
 
     def forward(trip, total):
-        lags = [trip * tiles + n for n in range(tiles)]
-        left = jnp.concatenate([window(sig, (shards + me) * tiles - lag) for lag in lags], axis=1)
-        right = jnp.concatenate(
-            [jnp.concatenate([toe_high[lag + 1], toe_low[lag + 1]], axis=1) for lag in lags], axis=0
-        )
-        return total + dot(left, right, 1, 0)
+        for part in range(2):
+            lags = [(trip * 2 + part) * tiles + n for n in range(tiles)]
+            left = jnp.concatenate([window(sig, (shards + me) * tiles - lag) for lag in lags], axis=1)
+            right = jnp.concatenate(
+                [jnp.concatenate([toe_high[lag + 1], toe_low[lag + 1]], axis=1) for lag in lags], axis=0
+            )
+            total = total + dot(left, right, 1, 0)
+        return total
 
     def backward(trip, total):
-        lags = [trip * tiles + n for n in range(tiles)]
-        left = jnp.concatenate([window(cot, me * tiles + lag) for lag in lags], axis=1)
-        right = jnp.concatenate(
-            [jnp.concatenate([toe_high[lag + 1], toe_low[lag + 1]], axis=0) for lag in lags], axis=1
-        )
-        return total + dot(left, right, 1, 1)
+        for part in range(2):
+            lags = [(trip * 2 + part) * tiles + n for n in range(tiles)]
+            left = jnp.concatenate([window(cot, me * tiles + lag) for lag in lags], axis=1)
+            right = jnp.concatenate(
+                [jnp.concatenate([toe_high[lag + 1], toe_low[lag + 1]], axis=0) for lag in lags], axis=1
+            )
+            total = total + dot(left, right, 1, 1)
+        return total
 
     start = jnp.zeros((count, 2 * LANES), jnp.float32)
-    conv = lax.fori_loop(0, me + 1, forward, start)
-    back = lax.fori_loop(0, shards - me, backward, start)
+    conv = lax.fori_loop(0, me // 2 + 1, forward, start)
+    back = lax.fori_loop(0, (shards - me + 1) // 2, backward, start)
     factor = 1.0 / math.sqrt(shards * tokens)
     square_row = lax.broadcasted_iota(jnp.int32, (channels, channels), 0)
     square_lane = lax.broadcasted_iota(jnp.int32, (channels, channels), 1)

time: 28.4 us -> 26 us (0.915)
  Pallas kernels: 10.4 us -> 7.58 us
  waiting for transfers between devices: 7.16 us -> 7.61 us
    pallas_call x1, Pallas kernels: 3.59 us -> 1.44 us  [toeplitz_tiles(): pl.pallas_call(functools.partial(toeplitz_kernel, shards, channels, token...]
    pallas_call x1, Pallas kernels: 4.21 us -> 3.5 us  [convolve(): pl.pallas_call(functools.partial(convolve_kernel, shards, channels, token...]
    ppermute x2, waiting for transfers between devices: 0.01 us -> 0.45 us  [direct_body(): lax.ppermute(value, 'chan', [(i, i ^ bits) for i in range(groups)])]
  transfers between devices with their start and end apart: 9 -> 9, of which waited for: 5 -> 6; matrix products, arithmetic and copies ran while one was open for 0% -> 0% of each run, Pallas kernels for 28% -> 19%
where the time goes in v3:
time: 26 us; the launch traced here: 25.8 us
  starting transfers between devices  9.39 us (36%)
  waiting for transfers between devices  7.61 us (29%)
  Pallas kernels  7.58 us (29%)
  between operations  0.67 us (3%)
  other arithmetic  0.61 us (2%)
    ppermute x7, waiting for transfers between devices, flipped(): lax.ppermute(value, 'context', [(i, i ^ bits) for i in range(shards)])  7.16 us
    ppermute x7, starting transfers between devices, flipped(): lax.ppermute(value, 'context', [(i, i ^ bits) for i in range(shards)])  4.88 us
    ppermute x2, starting transfers between devices, direct_body(): lax.ppermute(value, 'chan', [(i, i ^ bits) for i in range(groups)])  4.5 us
    pallas_call x1, Pallas kernels, convolve(): pl.pallas_call(functools.partial(convolve_kernel, shards, channels, token...  3.5 us
    pallas_call x1, Pallas kernels, filter_grad(): pl.pallas_call(functools.partial(filter_grad_kernel, shards, channels, to...  1.76 us
    pallas_call x1, Pallas kernels, toeplitz_tiles(): pl.pallas_call(functools.partial(toeplitz_kernel, shards, channels, token...  1.44 us
    pallas_call x1, Pallas kernels, stack_local(): pl.pallas_call(stack_kernel, out_shape=pltpu.VMEM((rows, LANES), jnp.floa...  0.88 us
    mul x1, other arithmetic, direct_body(): grad_filter = value.reshape(tokens) * (1.0 / math.sqrt(shards * tokens))  0.6 us
  transfers between devices with their start and end apart: 9, of which 6 were waited for; matrix products, arithmetic and copies ran while one was open for 0% of the time, Pallas kernels for 19%

profile of v3, /device:TPU:0, one launch (start us, length us, event | category | flops | bytes accessed | tf_op | source)
XLA Modules:
  0.0 25.8 jit_solution(13752905577945120699)
XLA Ops:
  0.6 0.9 %stack_local.1.refs_0_ = f32[264,128]{1,0:T(8,128)S(1)} custom-call(f32[16,1024]{1,0:T(8,128)} %signal_ref.1, f32[16,1024]{1,0:T(8,128)} %cotangent_ref.1, f32[8,128]{1,0:T(8,128)} %bitcast.4), custom_call_target="tpu_custom_call" | custom-call | tf_op jit(solution)/shard_map/stack_local/pallas_call | solution.py:52
  1.5 0.0 copy-start
  1.5 4.0 %collective-permute-start.5 = (f32[264,128]{1,0:T(8,128)S(1)}, f32[264,128]{1,0:T(8,128)S(1)}, u32[]{:S(2)}, u32[]{:S(2)}) collective-permute-start(f32[264,128]{1,0:T(8,128)S(1)} %stack_local.1.refs_0_), channel_id=1, source_target_pairs={{0,24},{4,28},{8,16},{12,20},{16,8},{20,12},{24,0},{28,4},{1,25},{... | collective-permute-start | bytes 405512 | tf_op jit(solution)/shard_map/ppermute | solution.py:63
  5.5 0.5 %collective-permute-start.3 = (f32[264,128]{1,0:T(8,128)S(1)}, f32[264,128]{1,0:T(8,128)S(1)}, u32[]{:S(2)}, u32[]{:S(2)}) collective-permute-start(f32[264,128]{1,0:T(8,128)S(1)} %stack_local.1.refs_0_), channel_id=1, source_target_pairs={{0,16},{4,20},{8,24},{12,28},{16,0},{20,4},{24,8},{28,12},{1,17},{... | collective-permute-start | bytes 405512 | tf_op jit(solution)/shard_map/ppermute | solution.py:63
  6.0 0.1 collective-permute-start.1
  6.1 0.0 collective-permute-start
  6.1 3.3 %collective-permute-done.5.refs_6_ = f32[264,128]{1,0:T(8,128)S(1)} collective-permute-done((f32[264,128]{1,0:T(8,128)S(1)}, f32[264,128]{1,0:T(8,128)S(1)}, u32[]{:S(2)}, u32[]{:S(2)}) %collective-permute-start.5) | collective-permute-done | bytes 135200 | tf_op jit(solution)/shard_map/ppermute | solution.py:63
  9.5 0.0 collective-permute-start.6
  9.5 2.5 %collective-permute-done.3.refs_4_ = f32[264,128]{1,0:T(8,128)S(1)} collective-permute-done((f32[264,128]{1,0:T(8,128)S(1)}, f32[264,128]{1,0:T(8,128)S(1)}, u32[]{:S(2)}, u32[]{:S(2)}) %collective-permute-start.3) | collective-permute-done | bytes 135200 | tf_op jit(solution)/shard_map/ppermute | solution.py:63
  12.0 0.0 collective-permute-start.4
  12.0 0.2 collective-permute-done.1.refs_2_
  12.2 0.3 %collective-permute-start.2 = (f32[264,128]{1,0:T(8,128)S(1)}, f32[264,128]{1,0:T(8,128)S(1)}, u32[]{:S(2)}, u32[]{:S(2)}) collective-permute-start(f32[264,128]{1,0:T(8,128)S(1)} %collective-permute-done.1.refs_2_), channel_id=1, source_target_pairs={{0,4},{4,0},{8,12},{12,8},{16,20},{20,16},{24,28},{28,24},{1,5},{5... | collective-permute-start | bytes 405512 | tf_op jit(solution)/shard_map/ppermute | solution.py:63
  12.5 0.0 collective-permute-done.refs_1_
  12.5 0.0 collective-permute-done.6.refs_7_
  12.5 0.8 %collective-permute-done.4.refs_5_ = f32[264,128]{1,0:T(8,128)S(1)} collective-permute-done((f32[264,128]{1,0:T(8,128)S(1)}, f32[264,128]{1,0:T(8,128)S(1)}, u32[]{:S(2)}, u32[]{:S(2)}) %collective-permute-start.4) | collective-permute-done | bytes 135200 | tf_op jit(solution)/shard_map/ppermute | solution.py:63
  13.3 0.2 collective-permute-done.2.refs_3_
  13.6 1.8 %filter_grad.1 = f32[1,1024]{1,0:T(1,128)S(1)} custom-call(f32[264,128]{1,0:T(8,128)S(1)} %stack_local.1.refs_0_, f32[264,128]{1,0:T(8,128)S(1)} %collective-permute-done.refs_1_, f32[264,128]{1,0:T(8,128)S(1)} %collective-permute-done.1.refs_2_, f32[264,128]{1,0:T(8,128)S(1)} %collective-permute-done.2.refs_3_, ...), custom_call_target="tpu_custom_call" | custom-call | flops 1006632960 | bytes 1048576 | tf_op jit(solution)/shard_map/filter_grad/pallas_call | solution.py:122
  15.3 1.8 %collective-permute-start.7 = (f32[1,1024]{1,0:T(1,128)S(1)}, f32[1,1024]{1,0:T(1,128)S(1)}, u32[]{:S(2)}, u32[]{:S(2)}) collective-permute-start(f32[1,1024]{1,0:T(1,128)S(1)} %filter_grad.1), channel_id=1, source_target_pairs={{0,1},{1,0},{2,3},{3,2},{4,5},{5,4},{6,7},{7,6},{8,9},{9,8},{10,11... | collective-permute-start | bytes 12296 | tf_op jit(solution)/shard_map/ppermute | solution.py:289
  17.1 1.4 %toeplitz_tiles.1 = (bf16[65,128,128]{2,1,0:T(8,128)(2,1)S(1)}, bf16[65,128,128]{2,1,0:T(8,128)(2,1)S(1)}) custom-call(f32[264,128]{1,0:T(8,128)S(1)} %stack_local.1.refs_0_, f32[264,128]{1,0:T(8,128)S(1)} %collective-permute-done.refs_1_, f32[264,128]{1,0:T(8,128)S(1)} %collective-permute-done.1.refs_2_, f32[264,128]{1,0:T(8,128)S(1)} %collective-permute-done.2.refs_3_, ...), custom_call_target="tpu_custom_call" | custom-call | flops 17039360 | bytes 4259840 | tf_op jit(solution)/shard_map/toeplitz_tiles/pallas_call | solution.py:182
  18.6 0.4 %collective-permute-done.7 = f32[1,1024]{1,0:T(1,128)S(1)} collective-permute-done((f32[1,1024]{1,0:T(1,128)S(1)}, f32[1,1024]{1,0:T(1,128)S(1)}, u32[]{:S(2)}, u32[]{:S(2)}) %collective-permute-start.7) | collective-permute-done | bytes 4128 | tf_op jit(solution)/shard_map/ppermute | solution.py:289
  19.0 2.7 %collective-permute-start.8 = (f32[1,1024]{1,0:T(1,128)S(1)}, f32[1,1024]{1,0:T(1,128)S(1)}, u32[]{:S(2)}, u32[]{:S(2)}) collective-permute-start(f32[1,1024]{1,0:T(1,128)S(1)} %add.6), channel_id=1, source_target_pairs={{0,2},{1,3},{2,0},{3,1},{4,6},{5,7},{6,4},{7,5},{8,10},{9,11},{10,... | collective-permute-start | bytes 12296 | tf_op jit(solution)/shard_map/ppermute | solution.py:289
  21.7 0.0 copy-done
  21.7 3.5 %convolve.1 = (f32[16,1024]{1,0:T(8,128)}, f32[16,1024]{1,0:T(8,128)}) custom-call(f32[264,128]{1,0:T(8,128)S(1)} %stack_local.1.refs_0_, f32[264,128]{1,0:T(8,128)S(1)} %collective-permute-done.refs_1_, f32[264,128]{1,0:T(8,128)S(1)} %collective-permute-done.1.refs_2_, f32[264,128]{1,0:T(8,128)S(1)} %collective-permute-done.2.refs_3_, ...), custom_call_target="tpu_custom_call" | custom-call | flops 1207959552 | bytes 1048576 | tf_op jit(solution)/shard_map/convolve/pallas_call | solution.py:264
  25.2 0.0 collective-permute-done.8
  25.2 0.6 %add_multiply_fusion = f32[1,1024]{1,0:T(1,128)} fusion(f32[1,1024]{1,0:T(1,128)S(1)} %add.6, f32[1,1024]{1,0:T(1,128)S(1)} %collective-permute-done.8), kind=kLoop, calls=%fused_computation | loop fusion | flops 2048 | bytes 12288 | tf_op jit(solution)/shard_map/mul | solution.py:294
  (1 shorter events, 0.0 us)
Async XLA Ops:
  1.5 20.2 %copy-start = (f32[16]{0:T(128)S(1)}, f32[16]{0:T(128)}, u32[]{:S(2)}) copy-start(f32[16]{0:T(128)} %param.6) | copy-start | bytes 196
  1.5 8.0 %collective-permute-start.5 = (f32[264,128]{1,0:T(8,128)S(1)}, f32[264,128]{1,0:T(8,128)S(1)}, u32[]{:S(2)}, u32[]{:S(2)}) collective-permute-start(f32[264,128]{1,0:T(8,128)S(1)} %stack_local.1.refs_0_), channel_id=1, source_target_pairs={{0,24},{4,28},{8,16},{12,20},{16,8},{20,12},{24,0},{28,4},{1,25},{... | collective-permute-start | bytes 405512 | tf_op jit(solution)/shard_map/ppermute | solution.py:63
  5.5 6.5 %collective-permute-start.3 = (f32[264,128]{1,0:T(8,128)S(1)}, f32[264,128]{1,0:T(8,128)S(1)}, u32[]{:S(2)}, u32[]{:S(2)}) collective-permute-start(f32[264,128]{1,0:T(8,128)S(1)} %stack_local.1.refs_0_), channel_id=1, source_target_pairs={{0,16},{4,20},{8,24},{12,28},{16,0},{20,4},{24,8},{28,12},{1,17},{... | collective-permute-start | bytes 405512 | tf_op jit(solution)/shard_map/ppermute | solution.py:63
  6.0 6.2 %collective-permute-start.1 = (f32[264,128]{1,0:T(8,128)S(1)}, f32[264,128]{1,0:T(8,128)S(1)}, u32[]{:S(2)}, u32[]{:S(2)}) collective-permute-start(f32[264,128]{1,0:T(8,128)S(1)} %stack_local.1.refs_0_), channel_id=1, source_target_pairs={{0,8},{4,12},{8,0},{12,4},{16,24},{20,28},{24,16},{28,20},{1,9},{5... | collective-permute-start | bytes 405512 | tf_op jit(solution)/shard_map/ppermute | solution.py:63
  6.1 6.4 %collective-permute-start = (f32[264,128]{1,0:T(8,128)S(1)}, f32[264,128]{1,0:T(8,128)S(1)}, u32[]{:S(2)}, u32[]{:S(2)}) collective-permute-start(f32[264,128]{1,0:T(8,128)S(1)} %stack_local.1.refs_0_), channel_id=1, source_target_pairs={{0,4},{4,0},{8,12},{12,8},{16,20},{20,16},{24,28},{28,24},{1,5},{5... | collective-permute-start | bytes 405512 | tf_op jit(solution)/shard_map/ppermute | solution.py:63
  9.5 3.0 %collective-permute-start.6 = (f32[264,128]{1,0:T(8,128)S(1)}, f32[264,128]{1,0:T(8,128)S(1)}, u32[]{:S(2)}, u32[]{:S(2)}) collective-permute-start(f32[264,128]{1,0:T(8,128)S(1)} %collective-permute-done.5.refs_6_), channel_id=1, source_target_pairs={{0,4},{4,0},{8,12},{12,8},{16,20},{20,16},{24,28},{28,24},{1,5},{5... | collective-permute-start | bytes 405512 | tf_op jit(solution)/shard_map/ppermute | solution.py:63
  12.0 1.4 %collective-permute-start.4 = (f32[264,128]{1,0:T(8,128)S(1)}, f32[264,128]{1,0:T(8,128)S(1)}, u32[]{:S(2)}, u32[]{:S(2)}) collective-permute-start(f32[264,128]{1,0:T(8,128)S(1)} %collective-permute-done.3.refs_4_), channel_id=1, source_target_pairs={{0,4},{4,0},{8,12},{12,8},{16,20},{20,16},{24,28},{28,24},{1,5},{5... | collective-permute-start | bytes 405512 | tf_op jit(solution)/shard_map/ppermute | solution.py:63
  12.2 1.4 %collective-permute-start.2 = (f32[264,128]{1,0:T(8,128)S(1)}, f32[264,128]{1,0:T(8,128)S(1)}, u32[]{:S(2)}, u32[]{:S(2)}) collective-permute-start(f32[264,128]{1,0:T(8,128)S(1)} %collective-permute-done.1.refs_2_), channel_id=1, source_target_pairs={{0,4},{4,0},{8,12},{12,8},{16,20},{20,16},{24,28},{28,24},{1,5},{5... | collective-permute-start | bytes 405512 | tf_op jit(solution)/shard_map/ppermute | solution.py:63
  15.3 3.7 %collective-permute-start.7 = (f32[1,1024]{1,0:T(1,128)S(1)}, f32[1,1024]{1,0:T(1,128)S(1)}, u32[]{:S(2)}, u32[]{:S(2)}) collective-permute-start(f32[1,1024]{1,0:T(1,128)S(1)} %filter_grad.1), channel_id=1, source_target_pairs={{0,1},{1,0},{2,3},{3,2},{4,5},{5,4},{6,7},{7,6},{8,9},{9,8},{10,11... | collective-permute-start | bytes 12296 | tf_op jit(solution)/shard_map/ppermute | solution.py:289
  19.0 6.2 %collective-permute-start.8 = (f32[1,1024]{1,0:T(1,128)S(1)}, f32[1,1024]{1,0:T(1,128)S(1)}, u32[]{:S(2)}, u32[]{:S(2)}) collective-permute-start(f32[1,1024]{1,0:T(1,128)S(1)} %add.6), channel_id=1, source_target_pairs={{0,2},{1,3},{2,0},{3,1},{4,6},{5,7},{6,4},{7,5},{8,10},{9,11},{10,... | collective-permute-start | bytes 12296 | tf_op jit(solution)/shard_map/ppermute | solution.py:289

commit v4 on v3

--- a/solution.py
+++ b/solution.py
@@ -13,7 +13,7 @@
 LANES = 128
 BLOCK = 256
 PACKED_ROWS = 16
-KERNEL_BYTES = 48 * 1024 * 1024
+KERNEL_BYTES = 16 * 1024 * 1024
 
 
 def halves(value):
@@ -70,36 +70,42 @@
     return [found[bits] for bits in range(shards)]
 
 
-def place_rows(block_ref, index, channels, tokens, first, high_ref, low_ref, start):
-    per = tokens // BLOCK
-    for tile in range(tokens // LANES):
+def place_rows(block_ref, first, index, channels, tokens, ref, start):
+    tiles = tokens // LANES
+    for tile in range(tiles):
         rows = first + tile * channels
-        high, low = halves(block_ref[rows : rows + channels, :])
-        at = pl.multiple_of((index * per + tile // 2) * channels + start, PACKED_ROWS)
-        lanes = slice((tile % 2) * LANES, (tile % 2 + 1) * LANES)
-        high_ref[pl.ds(at, channels), lanes] = high
-        low_ref[pl.ds(at, channels), lanes] = low
+        both = jnp.concatenate(halves(block_ref[rows : rows + channels, :]), axis=0)
+        at = pl.multiple_of((index * tiles + tile) * 2 * channels + start, PACKED_ROWS)
+        ref[pl.ds(at, 2 * channels), :] = both
+
+
+def paired_tiles(ref, start, count, channels, half):
+    def rows(tile):
+        at = pl.multiple_of((start + tile) * 2 * channels + half * channels, PACKED_ROWS)
+        return ref[pl.ds(at, channels), :]
+
+    return jnp.concatenate(
+        [jnp.concatenate([rows(tile), rows(tile + 1)], axis=1) for tile in range(0, count, 2)], axis=0
+    )
 
 
 def filter_grad_kernel(shards, channels, tokens, *refs):
-    blocks, out_ref = refs[:shards], refs[shards]
-    sig_high, sig_low, cot_high, cot_low, folded = refs[shards + 1 :]
+    blocks, out_ref, sig, cot, folded = refs[:shards], *refs[shards:]
     me = lax.axis_index("context")
-    per = tokens // BLOCK
-    rows = shards * per * channels
-    cot_high[rows:, :] = jnp.zeros((rows, BLOCK), jnp.bfloat16)
-    cot_low[rows:, :] = jnp.zeros((rows, BLOCK), jnp.bfloat16)
+    per, tiles = tokens // BLOCK, tokens // LANES
+    count = 2 * tiles * channels
+    rows = shards * count
+    sig[:count, :] = jnp.zeros((count, LANES), jnp.bfloat16)
+    cot[rows:, :] = jnp.zeros((rows, LANES), jnp.bfloat16)
     for bits in range(shards):
-        index = me ^ bits
-        place_rows(blocks[bits], index, channels, tokens, 0, sig_high, sig_low, 0)
-        place_rows(
-            blocks[bits], index, channels, tokens, channels * tokens // LANES, cot_high, cot_low, 0
-        )
-    sig = (sig_high[...], sig_low[...])
+        place_rows(blocks[bits], 0, me ^ bits, channels, tokens, sig, count)
+        place_rows(blocks[bits], channels * tiles, me ^ bits, channels, tokens, cot, 0)
+    held = [paired_tiles(sig, tiles, shards * tiles, channels, half) for half in range(2)]
     for lag in range(per + 1):
-        at = pl.multiple_of((me * per + lag) * channels, PACKED_ROWS)
-        window = (cot_high[pl.ds(at, rows), :], cot_low[pl.ds(at, rows), :])
-        folded[:, lag * BLOCK : (lag + 1) * BLOCK] = dot_halves(sig, window, 0, 0)
+        window = [
+            paired_tiles(cot, me * tiles + 2 * lag, shards * tiles, channels, half) for half in range(2)
+        ]
+        folded[:, lag * BLOCK : (lag + 1) * BLOCK] = dot(jnp.concatenate([held[0], held[0], held[1]], axis=0), jnp.concatenate([window[0], window[1], window[0]], axis=0), 0, 0)
     width = (per + 1) * BLOCK - LANES
     total = None
     for group in range(LANES // 8):
@@ -117,20 +123,18 @@
 
 
 def filter_grad(blocks, shards, channels, tokens):
-    rows = shards * tokens // BLOCK * channels
     per = tokens // BLOCK
+    rows = shards * per * channels
     return pl.pallas_call(
         functools.partial(filter_grad_kernel, shards, channels, tokens),
-        out_shape=jax.ShapeDtypeStruct((1, tokens), jnp.float32),
+        out_shape=[
+            jax.ShapeDtypeStruct((1, tokens), jnp.float32),
+            pltpu.VMEM((4 * rows // shards * (shards + 1), LANES), jnp.bfloat16),
+            pltpu.VMEM((8 * rows, LANES), jnp.bfloat16),
+        ],
         in_specs=[pl.BlockSpec(memory_space=pltpu.VMEM)] * shards,
-        out_specs=pl.BlockSpec(memory_space=pltpu.VMEM),
-        scratch_shapes=[
-            pltpu.VMEM((rows, BLOCK), jnp.bfloat16),
-            pltpu.VMEM((rows, BLOCK), jnp.bfloat16),
-            pltpu.VMEM((2 * rows, BLOCK), jnp.bfloat16),
-            pltpu.VMEM((2 * rows, BLOCK), jnp.bfloat16),
-            pltpu.VMEM((BLOCK, (per + 1) * BLOCK), jnp.float32),
-        ],
+        out_specs=[pl.BlockSpec(memory_space=pltpu.VMEM)] * 3,
+        scratch_shapes=[pltpu.VMEM((BLOCK, (per + 1) * BLOCK), jnp.float32)],
         compiler_params=pltpu.CompilerParams(vmem_limit_bytes=KERNEL_BYTES),
         cost_estimate=pl.CostEstimate(
             flops=2 * 3 * (per + 1) * rows * BLOCK * BLOCK, bytes_accessed=4 * rows * BLOCK * 2, transcendentals=0
@@ -193,54 +197,35 @@
     )(*blocks)
 
 
-def place_stacked(block_ref, index, channels, tokens, first, ref, start):
-    for tile in range(tokens // LANES):
-        rows = first + tile * channels
-        both = jnp.concatenate(halves(block_ref[rows : rows + channels, :]), axis=0)
-        at = pl.multiple_of((index * (tokens // LANES) + tile) * 2 * channels + start, PACKED_ROWS)
-        ref[pl.ds(at, 2 * channels), :] = both
-
-
 def convolve_kernel(shards, channels, tokens, *refs):
-    blocks, toe_high, toe_low, gain_ref = refs[:shards], *refs[shards : shards + 3]
-    out_ref, back_ref, sig, cot = refs[shards + 3 :]
+    own_ref, sig, cot, toe_high, toe_low, gain_ref, out_ref, back_ref, conv, back = refs
     me = lax.axis_index("context")
     tiles = tokens // LANES
-    rows = 2 * shards * tiles * channels
-    sig[:rows, :] = jnp.zeros((rows, LANES), jnp.bfloat16)
-    cot[rows:, :] = jnp.zeros((rows, LANES), jnp.bfloat16)
-    for bits in range(shards):
-        index = me ^ bits
-        place_stacked(blocks[bits], index, channels, tokens, 0, sig, rows)
-        place_stacked(blocks[bits], index, channels, tokens, channels * tiles, cot, 0)
     count = 2 * tiles * channels
 
     def window(ref, tile):
         return ref[pl.ds(pl.multiple_of(tile * 2 * channels, PACKED_ROWS), count), :]
 
-    def forward(trip, total):
-        for part in range(2):
-            lags = [(trip * 2 + part) * tiles + n for n in range(tiles)]
-            left = jnp.concatenate([window(sig, (shards + me) * tiles - lag) for lag in lags], axis=1)
-            right = jnp.concatenate(
-                [jnp.concatenate([toe_high[lag + 1], toe_low[lag + 1]], axis=1) for lag in lags], axis=0
-            )
-            total = total + dot(left, right, 1, 0)
-        return total
-
-    def backward(trip, total):
-        for part in range(2):
-            lags = [(trip * 2 + part) * tiles + n for n in range(tiles)]
-            left = jnp.concatenate([window(cot, me * tiles + lag) for lag in lags], axis=1)
-            right = jnp.concatenate(
-                [jnp.concatenate([toe_high[lag + 1], toe_low[lag + 1]], axis=0) for lag in lags], axis=1
-            )
-            total = total + dot(left, right, 1, 1)
-        return total
-
-    start = jnp.zeros((count, 2 * LANES), jnp.float32)
-    conv = lax.fori_loop(0, me // 2 + 1, forward, start)
-    back = lax.fori_loop(0, (shards - me + 1) // 2, backward, start)
+    def forward(lags):
+        left = jnp.concatenate([window(sig, (me + 1) * tiles - lag) for lag in lags], axis=1)
+        pairs = [jnp.concatenate([toe_high[lag + 1], toe_low[lag + 1]], axis=1) for lag in lags]
+        return dot(left, jnp.concatenate(pairs, axis=0), 1, 0)
+
+    def backward(lags):
+        left = jnp.concatenate([window(cot, me * tiles + lag) for lag in lags], axis=1)
+        pairs = [jnp.concatenate([toe_high[lag + 1], toe_low[lag + 1]], axis=0) for lag in lags]
+        return dot(left, jnp.concatenate(pairs, axis=1), 1, 1)
+
+    def total(product, blocks):
+        parts = [product([block * tiles + n for n in range(tiles)]) for block in range(blocks)]
+        return sum(parts[1:], parts[0])
+
+    def run(index):
+        conv[...] = total(forward, index + 1)
+        back[...] = total(backward, shards - index)
+
+    for index in range(shards):
+        pl.when(me == index)(functools.partial(run, index))
     factor = 1.0 / math.sqrt(shards * tokens)
     square_row = lax.broadcasted_iota(jnp.int32, (channels, channels), 0)
     square_lane = lax.broadcasted_iota(jnp.int32, (channels, channels), 1)
@@ -252,29 +237,28 @@
     for tile in range(tiles):
         lanes = slice(tile * LANES, (tile + 1) * LANES)
         for ref, value, first in ((out_ref, conv, 0), (back_ref, back, tiles)):
-            own = blocks[0][(first + tile) * channels : (first + tile + 1) * channels, :]
-            quarters = value[tile * 2 * channels : (tile + 1) * 2 * channels, :]
-            both = quarters[:channels, :] + quarters[channels:, :]
+            own = own_ref[(first + tile) * channels : (first + tile + 1) * channels, :]
+            top = tile * 2 * channels
+            both = value[top : top + channels, :] + value[top + channels : top + 2 * channels, :]
             ref[:, lanes] = (both[:, :LANES] + both[:, LANES:]) * factor + gain * own
 
 
-def convolve(blocks, toeplitz, skip_gain, shards, channels, tokens):
-    per = tokens // BLOCK
-    rows = shards * per * channels
+def convolve(own, held, toeplitz, skip_gain, shards, channels, tokens):
+    count = 2 * channels * tokens // LANES
     return pl.pallas_call(
         functools.partial(convolve_kernel, shards, channels, tokens),
         out_shape=[jax.ShapeDtypeStruct((channels, tokens), jnp.float32)] * 2,
-        in_specs=[pl.BlockSpec(memory_space=pltpu.VMEM)] * (shards + 3),
+        in_specs=[pl.BlockSpec(memory_space=pltpu.VMEM)] * 6,
         out_specs=[pl.BlockSpec(memory_space=pltpu.VMEM)] * 2,
-        scratch_shapes=[pltpu.VMEM((8 * rows, LANES), jnp.bfloat16)] * 2,
+        scratch_shapes=[pltpu.VMEM((count, 2 * LANES), jnp.float32)] * 2,
         compiler_params=pltpu.CompilerParams(vmem_limit_bytes=KERNEL_BYTES),
         cost_estimate=pl.CostEstimate(
-            flops=2 * 4 * (shards + 1) * per * per * channels * BLOCK * BLOCK,
-            bytes_accessed=4 * rows * BLOCK * 2,
+            flops=2 * (shards + 1) * tokens * count * 2 * LANES,
+            bytes_accessed=8 * shards * count * LANES,
             transcendentals=0,
         ),
         name="convolve",
-    )(*blocks, *toeplitz, skip_gain.reshape(1, channels))
+    )(own, *held, *toeplitz, skip_gain.reshape(1, channels))
 
 
 def direct_body(signal, filter_taps, skip_gain, cotangent):
@@ -282,7 +266,7 @@
     channels, tokens = signal.shape
     stacked = stack_local(signal, cotangent, filter_taps)
     blocks = gather_blocks(stacked, shards)
-    value = filter_grad(blocks, shards, channels, tokens)
+    value, *held = filter_grad(blocks, shards, channels, tokens)
     toeplitz = toeplitz_tiles(blocks, shards, channels, tokens)
     bits = 1
     while bits < groups:
@@ -290,7 +274,7 @@
         if bits == 1:
             value, *toeplitz = lax.optimization_barrier((value, *toeplitz))
         bits *= 2
-    output, grad_signal = convolve(blocks, toeplitz, skip_gain, shards, channels, tokens)
+    output, grad_signal = convolve(blocks[0], held, toeplitz, skip_gain, shards, channels, tokens)
     grad_filter = value.reshape(tokens) * (1.0 / math.sqrt(shards * tokens))
     return (output, grad_signal, grad_filter)
 
@@ -442,7 +426,7 @@
     scratch = 16 * shards * tokens * channels + 4 * (shards * tokens + LANES) * LANES
     groups = lax.axis_size("chan")
     whole = groups & (groups - 1) == 0 and channels % PACKED_ROWS == 0 and tokens % (8 * LANES) == 0 and shards & (shards - 1) == 0
-    return whole and shards > 1 and 2 * held + scratch < KERNEL_BYTES // 2
+    return whole and shards > 1 and 2 * held + scratch < KERNEL_BYTES
 
 
 def body(signal, filter_taps, skip_gain, cotangent):

time: 26 us -> 24.8 us (0.954)
  Pallas kernels: 7.58 us -> 6.33 us
    pallas_call x1, Pallas kernels: 3.5 us -> 2.18 us  [convolve(): pl.pallas_call(functools.partial(convolve_kernel, shards, channels, token...]
  transfers between devices with their start and end apart: 9 -> 9, of which waited for: 6 -> 6; matrix products, arithmetic and copies ran while one was open for 0% -> 0% of each run, Pallas kernels for 19% -> 15%
where the time goes in v4:
time: 24.8 us; the launch traced here: 24.6 us
  starting transfers between devices  9.38 us (38%)
  waiting for transfers between devices  7.61 us (31%)
  Pallas kernels  6.33 us (26%)
  between operations  0.67 us (3%)
  other arithmetic  0.61 us (2%)
    ppermute x7, waiting for transfers between devices, flipped(): lax.ppermute(value, 'context', [(i, i ^ bits) for i in range(shards)])  7.16 us
    ppermute x7, starting transfers between devices, flipped(): lax.ppermute(value, 'context', [(i, i ^ bits) for i in range(shards)])  4.88 us
    ppermute x2, starting transfers between devices, direct_body(): lax.ppermute(value, 'chan', [(i, i ^ bits) for i in range(groups)])  4.5 us
    pallas_call x1, Pallas kernels, convolve(): pl.pallas_call(functools.partial(convolve_kernel, shards, channels, token...  2.18 us
    pallas_call x1, Pallas kernels, filter_grad(): pl.pallas_call(functools.partial(filter_grad_kernel, shards, channels, to...  1.83 us
    pallas_call x1, Pallas kernels, toeplitz_tiles(): pl.pallas_call(functools.partial(toeplitz_kernel, shards, channels, token...  1.44 us
    pallas_call x1, Pallas kernels, stack_local(): pl.pallas_call(stack_kernel, out_shape=pltpu.VMEM((rows, LANES), jnp.floa...  0.88 us
    mul x1, other arithmetic, direct_body(): grad_filter = value.reshape(tokens) * (1.0 / math.sqrt(shards * tokens))  0.6 us
  transfers between devices with their start and end apart: 9, of which 6 were waited for; matrix products, arithmetic and copies ran while one was open for 0% of the time, Pallas kernels for 15%

profile of v4, /device:TPU:0, one launch (start us, length us, event | category | flops | bytes accessed | tf_op | source)
XLA Modules:
  0.0 24.6 jit_solution(1672472239514120830)
XLA Ops:
  0.6 0.9 %stack_local.1.refs_0_ = f32[264,128]{1,0:T(8,128)S(1)} custom-call(f32[16,1024]{1,0:T(8,128)} %signal_ref.1, f32[16,1024]{1,0:T(8,128)} %cotangent_ref.1, f32[8,128]{1,0:T(8,128)} %bitcast.4), custom_call_target="tpu_custom_call" | custom-call | tf_op jit(solution)/shard_map/stack_local/pallas_call | solution.py:52
  1.5 0.0 copy-start
  1.5 4.0 %collective-permute-start.5 = (f32[264,128]{1,0:T(8,128)S(1)}, f32[264,128]{1,0:T(8,128)S(1)}, u32[]{:S(2)}, u32[]{:S(2)}) collective-permute-start(f32[264,128]{1,0:T(8,128)S(1)} %stack_local.1.refs_0_), channel_id=1, source_target_pairs={{0,24},{4,28},{8,16},{12,20},{16,8},{20,12},{24,0},{28,4},{1,25},{... | collective-permute-start | bytes 405512 | tf_op jit(solution)/shard_map/ppermute | solution.py:63
  5.5 0.5 %collective-permute-start.3 = (f32[264,128]{1,0:T(8,128)S(1)}, f32[264,128]{1,0:T(8,128)S(1)}, u32[]{:S(2)}, u32[]{:S(2)}) collective-permute-start(f32[264,128]{1,0:T(8,128)S(1)} %stack_local.1.refs_0_), channel_id=1, source_target_pairs={{0,16},{4,20},{8,24},{12,28},{16,0},{20,4},{24,8},{28,12},{1,17},{... | collective-permute-start | bytes 405512 | tf_op jit(solution)/shard_map/ppermute | solution.py:63
  6.0 0.1 collective-permute-start.1
  6.1 0.0 collective-permute-start
  6.1 3.3 %collective-permute-done.5.refs_6_ = f32[264,128]{1,0:T(8,128)S(1)} collective-permute-done((f32[264,128]{1,0:T(8,128)S(1)}, f32[264,128]{1,0:T(8,128)S(1)}, u32[]{:S(2)}, u32[]{:S(2)}) %collective-permute-start.5) | collective-permute-done | bytes 135200 | tf_op jit(solution)/shard_map/ppermute | solution.py:63
  9.5 0.0 collective-permute-start.6
  9.5 2.5 %collective-permute-done.3.refs_4_ = f32[264,128]{1,0:T(8,128)S(1)} collective-permute-done((f32[264,128]{1,0:T(8,128)S(1)}, f32[264,128]{1,0:T(8,128)S(1)}, u32[]{:S(2)}, u32[]{:S(2)}) %collective-permute-start.3) | collective-permute-done | bytes 135200 | tf_op jit(solution)/shard_map/ppermute | solution.py:63
  12.0 0.0 collective-permute-start.4
  12.0 0.2 collective-permute-done.1.refs_2_
  12.2 0.3 %collective-permute-start.2 = (f32[264,128]{1,0:T(8,128)S(1)}, f32[264,128]{1,0:T(8,128)S(1)}, u32[]{:S(2)}, u32[]{:S(2)}) collective-permute-start(f32[264,128]{1,0:T(8,128)S(1)} %collective-permute-done.1.refs_2_), channel_id=1, source_target_pairs={{0,4},{4,0},{8,12},{12,8},{16,20},{20,16},{24,28},{28,24},{1,5},{5... | collective-permute-start | bytes 405512 | tf_op jit(solution)/shard_map/ppermute | solution.py:63
  12.5 0.0 collective-permute-done.refs_1_
  12.5 0.0 collective-permute-done.6.refs_7_
  12.5 0.8 %collective-permute-done.4.refs_5_ = f32[264,128]{1,0:T(8,128)S(1)} collective-permute-done((f32[264,128]{1,0:T(8,128)S(1)}, f32[264,128]{1,0:T(8,128)S(1)}, u32[]{:S(2)}, u32[]{:S(2)}) %collective-permute-start.4) | collective-permute-done | bytes 135200 | tf_op jit(solution)/shard_map/ppermute | solution.py:63
  13.3 0.2 %collective-permute-done.2.refs_3_ = f32[264,128]{1,0:T(8,128)S(1)} collective-permute-done((f32[264,128]{1,0:T(8,128)S(1)}, f32[264,128]{1,0:T(8,128)S(1)}, u32[]{:S(2)}, u32[]{:S(2)}) %collective-permute-start.2) | collective-permute-done | bytes 135200 | tf_op jit(solution)/shard_map/ppermute | solution.py:63
  13.6 1.8 %filter_grad.1 = (f32[1,1024]{1,0:T(1,128)S(1)}, bf16[2304,128]{1,0:T(8,128)(2,1)S(1)}, bf16[4096,128]{1,0:T(8,128)(2,1)S(1)}) custom-call(f32[264,128]{1,0:T(8,128)S(1)} %stack_local.1.refs_0_, f32[264,128]{1,0:T(8,128)S(1)} %collective-permute-done.refs_1_, f32[264,128]{1,0:T(8,128)S(1)} %collective-permute-done.1.refs_2_, ...), custom_call_target="tpu_custom_call" | custom-call | flops 1006632960 | bytes 1048576 | tf_op jit(solution)/shard_map/filter_grad/pallas_call | solution.py:128
  15.4 1.8 %collective-permute-start.7 = (f32[1,1024]{1,0:T(1,128)S(1)}, f32[1,1024]{1,0:T(1,128)S(1)}, u32[]{:S(2)}, u32[]{:S(2)}) collective-permute-start(f32[1,1024]{1,0:T(1,128)S(1)} %get-tuple-element.15), channel_id=1, source_target_pairs={{0,1},{1,0},{2,3},{3,2},{4,5},{5,4},{6,7},{7,6},{8,9},{9,8},{10,11... | collective-permute-start | bytes 12296 | tf_op jit(solution)/shard_map/ppermute | solution.py:273
  17.2 1.4 %toeplitz_tiles.1 = (bf16[65,128,128]{2,1,0:T(8,128)(2,1)S(1)}, bf16[65,128,128]{2,1,0:T(8,128)(2,1)S(1)}) custom-call(f32[264,128]{1,0:T(8,128)S(1)} %stack_local.1.refs_0_, f32[264,128]{1,0:T(8,128)S(1)} %collective-permute-done.refs_1_, f32[264,128]{1,0:T(8,128)S(1)} %collective-permute-done.1.refs_2_, f32[264,128]{1,0:T(8,128)S(1)} %collective-permute-done.2.refs_3_, ...), custom_call_target="tpu_custom_call" | custom-call | flops 17039360 | bytes 4259840 | tf_op jit(solution)/shard_map/toeplitz_tiles/pallas_call | solution.py:186
  18.6 0.5 %collective-permute-done.7 = f32[1,1024]{1,0:T(1,128)S(1)} collective-permute-done((f32[1,1024]{1,0:T(1,128)S(1)}, f32[1,1024]{1,0:T(1,128)S(1)}, u32[]{:S(2)}, u32[]{:S(2)}) %collective-permute-start.7) | collective-permute-done | bytes 4128 | tf_op jit(solution)/shard_map/ppermute | solution.py:273
  19.1 2.7 %collective-permute-start.8 = (f32[1,1024]{1,0:T(1,128)S(1)}, f32[1,1024]{1,0:T(1,128)S(1)}, u32[]{:S(2)}, u32[]{:S(2)}) collective-permute-start(f32[1,1024]{1,0:T(1,128)S(1)} %add.6), channel_id=1, source_target_pairs={{0,2},{1,3},{2,0},{3,1},{4,6},{5,7},{6,4},{7,5},{8,10},{9,11},{10,... | collective-permute-start | bytes 12296 | tf_op jit(solution)/shard_map/ppermute | solution.py:273
  21.8 0.0 copy-done
  21.8 2.2 %convolve.1 = (f32[16,1024]{1,0:T(8,128)}, f32[16,1024]{1,0:T(8,128)}) custom-call(f32[264,128]{1,0:T(8,128)S(1)} %stack_local.1.refs_0_, bf16[2304,128]{1,0:T(8,128)(2,1)S(1)} %get-tuple-element.13.refs_1_, bf16[4096,128]{1,0:T(8,128)(2,1)S(1)} %get-tuple-element.14.refs_2_, bf16[65,128,128]{2,1,0:T(8,128)(2,1)S(1)} %get-tuple-element.18.refs_3_, ...), custom_call_target="tpu_custom_call" | custom-call | flops 1207959552 | bytes 2097152 | tf_op jit(solution)/shard_map/convolve/pallas_call | solution.py:248
  24.0 0.0 collective-permute-done.8
  24.0 0.6 %add_multiply_fusion = f32[1,1024]{1,0:T(1,128)} fusion(f32[1,1024]{1,0:T(1,128)S(1)} %add.6, f32[1,1024]{1,0:T(1,128)S(1)} %collective-permute-done.8), kind=kLoop, calls=%fused_computation | loop fusion | flops 2048 | bytes 12288 | tf_op jit(solution)/shard_map/mul | solution.py:278
  (1 shorter events, 0.0 us)
Async XLA Ops:
  1.5 20.3 %copy-start = (f32[16]{0:T(128)S(1)}, f32[16]{0:T(128)}, u32[]{:S(2)}) copy-start(f32[16]{0:T(128)} %param.6) | copy-start | bytes 196
  1.5 8.0 %collective-permute-start.5 = (f32[264,128]{1,0:T(8,128)S(1)}, f32[264,128]{1,0:T(8,128)S(1)}, u32[]{:S(2)}, u32[]{:S(2)}) collective-permute-start(f32[264,128]{1,0:T(8,128)S(1)} %stack_local.1.refs_0_), channel_id=1, source_target_pairs={{0,24},{4,28},{8,16},{12,20},{16,8},{20,12},{24,0},{28,4},{1,25},{... | collective-permute-start | bytes 405512 | tf_op jit(solution)/shard_map/ppermute | solution.py:63
  5.5 6.5 %collective-permute-start.3 = (f32[264,128]{1,0:T(8,128)S(1)}, f32[264,128]{1,0:T(8,128)S(1)}, u32[]{:S(2)}, u32[]{:S(2)}) collective-permute-start(f32[264,128]{1,0:T(8,128)S(1)} %stack_local.1.refs_0_), channel_id=1, source_target_pairs={{0,16},{4,20},{8,24},{12,28},{16,0},{20,4},{24,8},{28,12},{1,17},{... | collective-permute-start | bytes 405512 | tf_op jit(solution)/shard_map/ppermute | solution.py:63
  6.0 6.2 %collective-permute-start.1 = (f32[264,128]{1,0:T(8,128)S(1)}, f32[264,128]{1,0:T(8,128)S(1)}, u32[]{:S(2)}, u32[]{:S(2)}) collective-permute-start(f32[264,128]{1,0:T(8,128)S(1)} %stack_local.1.refs_0_), channel_id=1, source_target_pairs={{0,8},{4,12},{8,0},{12,4},{16,24},{20,28},{24,16},{28,20},{1,9},{5... | collective-permute-start | bytes 405512 | tf_op jit(solution)/shard_map/ppermute | solution.py:63
  6.1 6.4 %collective-permute-start = (f32[264,128]{1,0:T(8,128)S(1)}, f32[264,128]{1,0:T(8,128)S(1)}, u32[]{:S(2)}, u32[]{:S(2)}) collective-permute-start(f32[264,128]{1,0:T(8,128)S(1)} %stack_local.1.refs_0_), channel_id=1, source_target_pairs={{0,4},{4,0},{8,12},{12,8},{16,20},{20,16},{24,28},{28,24},{1,5},{5... | collective-permute-start | bytes 405512 | tf_op jit(solution)/shard_map/ppermute | solution.py:63
  9.5 3.0 %collective-permute-start.6 = (f32[264,128]{1,0:T(8,128)S(1)}, f32[264,128]{1,0:T(8,128)S(1)}, u32[]{:S(2)}, u32[]{:S(2)}) collective-permute-start(f32[264,128]{1,0:T(8,128)S(1)} %collective-permute-done.5.refs_6_), channel_id=1, source_target_pairs={{0,4},{4,0},{8,12},{12,8},{16,20},{20,16},{24,28},{28,24},{1,5},{5... | collective-permute-start | bytes 405512 | tf_op jit(solution)/shard_map/ppermute | solution.py:63
  12.0 1.4 %collective-permute-start.4 = (f32[264,128]{1,0:T(8,128)S(1)}, f32[264,128]{1,0:T(8,128)S(1)}, u32[]{:S(2)}, u32[]{:S(2)}) collective-permute-start(f32[264,128]{1,0:T(8,128)S(1)} %collective-permute-done.3.refs_4_), channel_id=1, source_target_pairs={{0,4},{4,0},{8,12},{12,8},{16,20},{20,16},{24,28},{28,24},{1,5},{5... | collective-permute-start | bytes 405512 | tf_op jit(solution)/shard_map/ppermute | solution.py:63
  12.2 1.4 %collective-permute-start.2 = (f32[264,128]{1,0:T(8,128)S(1)}, f32[264,128]{1,0:T(8,128)S(1)}, u32[]{:S(2)}, u32[]{:S(2)}) collective-permute-start(f32[264,128]{1,0:T(8,128)S(1)} %collective-permute-done.1.refs_2_), channel_id=1, source_target_pairs={{0,4},{4,0},{8,12},{12,8},{16,20},{20,16},{24,28},{28,24},{1,5},{5... | collective-permute-start | bytes 405512 | tf_op jit(solution)/shard_map/ppermute | solution.py:63
  15.4 3.7 %collective-permute-start.7 = (f32[1,1024]{1,0:T(1,128)S(1)}, f32[1,1024]{1,0:T(1,128)S(1)}, u32[]{:S(2)}, u32[]{:S(2)}) collective-permute-start(f32[1,1024]{1,0:T(1,128)S(1)} %get-tuple-element.15), channel_id=1, source_target_pairs={{0,1},{1,0},{2,3},{3,2},{4,5},{5,4},{6,7},{7,6},{8,9},{9,8},{10,11... | collective-permute-start | bytes 12296 | tf_op jit(solution)/shard_map/ppermute | solution.py:273
  19.1 4.9 %collective-permute-start.8 = (f32[1,1024]{1,0:T(1,128)S(1)}, f32[1,1024]{1,0:T(1,128)S(1)}, u32[]{:S(2)}, u32[]{:S(2)}) collective-permute-start(f32[1,1024]{1,0:T(1,128)S(1)} %add.6), channel_id=1, source_target_pairs={{0,2},{1,3},{2,0},{3,1},{4,6},{5,7},{6,4},{7,5},{8,10},{9,11},{10,... | collective-permute-start | bytes 12296 | tf_op jit(solution)/shard_map/ppermute | solution.py:273

commit v5 on v4

--- a/solution.py
+++ b/solution.py
@@ -13,6 +13,7 @@
 LANES = 128
 BLOCK = 256
 PACKED_ROWS = 16
+EARLY = 2
 KERNEL_BYTES = 16 * 1024 * 1024
 
 
@@ -143,8 +144,22 @@
     )(*blocks)
 
 
-def toeplitz_kernel(shards, channels, tokens, *refs):
-    blocks, high_ref, low_ref, taps, skew = refs[:shards], *refs[shards:]
+def convolve_block(held, me, tiles, channels, toe_high, toe_low, block, adjoint):
+    count = 2 * tiles * channels
+    lags = [block * tiles + n for n in range(tiles)]
+
+    def window(lag):
+        tile = me * tiles + lag if adjoint else (me + 1) * tiles - lag
+        return held[pl.ds(pl.multiple_of(tile * 2 * channels, PACKED_ROWS), count), :]
+
+    side = 0 if adjoint else 1
+    left = jnp.concatenate([window(lag) for lag in lags], axis=1)
+    pairs = [jnp.concatenate([toe_high[lag + 1], toe_low[lag + 1]], axis=side) for lag in lags]
+    return dot(left, jnp.concatenate(pairs, axis=1 - side), 1, 1 - side)
+
+
+def toeplitz_kernel(shards, channels, tokens, early, *refs):
+    blocks, sig, cot, high_ref, low_ref, start_ref, taps, skew = refs[:shards], *refs[shards:]
     me = lax.axis_index("context")
     tiles = tokens // LANES
     first = 2 * channels * tiles
@@ -179,50 +194,48 @@
 
     lax.fori_loop(0, shards, build, 0, unroll=min(4, shards))
 
-
-def toeplitz_tiles(blocks, shards, channels, tokens):
+    def begin(held, adjoint):
+        parts = [
+            convolve_block(held, me, tiles, channels, high_ref, low_ref, block, adjoint) for block in range(early)
+        ]
+        start_ref[...] = sum(parts[1:], parts[0])
+
+    pl.when(me >= shards // 2)(functools.partial(begin, sig, False))
+    pl.when(me < shards // 2)(functools.partial(begin, cot, True))
+
+
+def toeplitz_tiles(blocks, held, shards, channels, tokens, early):
     tiles = tokens // LANES
     shape = (shards * tiles + 1, LANES, LANES)
     return pl.pallas_call(
-        functools.partial(toeplitz_kernel, shards, channels, tokens),
-        out_shape=[pltpu.VMEM(shape, jnp.bfloat16)] * 2,
-        in_specs=[pl.BlockSpec(memory_space=pltpu.VMEM)] * shards,
-        out_specs=[pl.BlockSpec(memory_space=pltpu.VMEM)] * 2,
+        functools.partial(toeplitz_kernel, shards, channels, tokens, early),
+        out_shape=[pltpu.VMEM(shape, jnp.bfloat16)] * 2
+        + [pltpu.VMEM((2 * channels * tiles, 2 * LANES), jnp.float32)],
+        in_specs=[pl.BlockSpec(memory_space=pltpu.VMEM)] * (shards + 2),
+        out_specs=[pl.BlockSpec(memory_space=pltpu.VMEM)] * 3,
         scratch_shapes=[pltpu.VMEM((shards + 1, tiles, LANES), jnp.float32), pltpu.VMEM((shards, 8, (tiles + 1) * LANES), jnp.float32)],
         compiler_params=pltpu.CompilerParams(vmem_limit_bytes=KERNEL_BYTES),
         cost_estimate=pl.CostEstimate(
             flops=16 * shape[0] * LANES * LANES, bytes_accessed=4 * shape[0] * LANES * LANES, transcendentals=0
         ),
         name="toeplitz_tiles",
-    )(*blocks)
-
-
-def convolve_kernel(shards, channels, tokens, *refs):
-    own_ref, sig, cot, toe_high, toe_low, gain_ref, out_ref, back_ref, conv, back = refs
+    )(*blocks, *held)
+
+
+def convolve_kernel(shards, channels, tokens, early, *refs):
+    own_ref, sig, cot, toe_high, toe_low, start_ref, gain_ref, out_ref, back_ref, conv, back = refs
     me = lax.axis_index("context")
     tiles = tokens // LANES
-    count = 2 * tiles * channels
-
-    def window(ref, tile):
-        return ref[pl.ds(pl.multiple_of(tile * 2 * channels, PACKED_ROWS), count), :]
-
-    def forward(lags):
-        left = jnp.concatenate([window(sig, (me + 1) * tiles - lag) for lag in lags], axis=1)
-        pairs = [jnp.concatenate([toe_high[lag + 1], toe_low[lag + 1]], axis=1) for lag in lags]
-        return dot(left, jnp.concatenate(pairs, axis=0), 1, 0)
-
-    def backward(lags):
-        left = jnp.concatenate([window(cot, me * tiles + lag) for lag in lags], axis=1)
-        pairs = [jnp.concatenate([toe_high[lag + 1], toe_low[lag + 1]], axis=0) for lag in lags]
-        return dot(left, jnp.concatenate(pairs, axis=1), 1, 1)
-
-    def total(product, blocks):
-        parts = [product([block * tiles + n for n in range(tiles)]) for block in range(blocks)]
+
+    def total(held, blocks, adjoint, begun):
+        parts = [start_ref[...]] if begun else []
+        for block in range(early if begun else 0, blocks):
+            parts.append(convolve_block(held, me, tiles, channels, toe_high, toe_low, block, adjoint))
         return sum(parts[1:], parts[0])
 
     def run(index):
-        conv[...] = total(forward, index + 1)
-        back[...] = total(backward, shards - index)
+        conv[...] = total(sig, index + 1, False, index >= shards // 2)
+        back[...] = total(cot, shards - index, True, index < shards // 2)
 
     for index in range(shards):
         pl.when(me == index)(functools.partial(run, index))
@@ -243,12 +256,12 @@
             ref[:, lanes] = (both[:, :LANES] + both[:, LANES:]) * factor + gain * own
 
 
-def convolve(own, held, toeplitz, skip_gain, shards, channels, tokens):
+def convolve(own, held, toeplitz, skip_gain, shards, channels, tokens, early):
     count = 2 * channels * tokens // LANES
     return pl.pallas_call(
-        functools.partial(convolve_kernel, shards, channels, tokens),
+        functools.partial(convolve_kernel, shards, channels, tokens, early),
         out_shape=[jax.ShapeDtypeStruct((channels, tokens), jnp.float32)] * 2,
-        in_specs=[pl.BlockSpec(memory_space=pltpu.VMEM)] * 6,
+        in_specs=[pl.BlockSpec(memory_space=pltpu.VMEM)] * 7,
         out_specs=[pl.BlockSpec(memory_space=pltpu.VMEM)] * 2,
         scratch_shapes=[pltpu.VMEM((count, 2 * LANES), jnp.float32)] * 2,
         compiler_params=pltpu.CompilerParams(vmem_limit_bytes=KERNEL_BYTES),
@@ -267,14 +280,14 @@
     stacked = stack_local(signal, cotangent, filter_taps)
     blocks = gather_blocks(stacked, shards)
     value, *held = filter_grad(blocks, shards, channels, tokens)
-    toeplitz = toeplitz_tiles(blocks, shards, channels, tokens)
+    toeplitz = toeplitz_tiles(blocks, held, shards, channels, tokens, EARLY)
     bits = 1
     while bits < groups:
         value = value + lax.ppermute(value, "chan", [(i, i ^ bits) for i in range(groups)])
         if bits == 1:
             value, *toeplitz = lax.optimization_barrier((value, *toeplitz))
         bits *= 2
-    output, grad_signal = convolve(blocks[0], held, toeplitz, skip_gain, shards, channels, tokens)
+    output, grad_signal = convolve(blocks[0], held, toeplitz, skip_gain, shards, channels, tokens, EARLY)
     grad_filter = value.reshape(tokens) * (1.0 / math.sqrt(shards * tokens))
     return (output, grad_signal, grad_filter)
 
@@ -426,7 +439,7 @@
     scratch = 16 * shards * tokens * channels + 4 * (shards * tokens + LANES) * LANES
     groups = lax.axis_size("chan")
     whole = groups & (groups - 1) == 0 and channels % PACKED_ROWS == 0 and tokens % (8 * LANES) == 0 and shards & (shards - 1) == 0
-    return whole and shards > 1 and 2 * held + scratch < KERNEL_BYTES
+    return whole and shards >= 2 * EARLY and 2 * held + scratch < KERNEL_BYTES
 
 
 def body(signal, filter_taps, skip_gain, cotangent):

time: 24.8 us -> 24.5 us (0.988)
  waiting for transfers between devices: 7.61 us -> 7.16 us
    pallas_call x1, Pallas kernels: 1.44 us -> 1.92 us  [toeplitz_tiles(): pl.pallas_call(functools.partial(toeplitz_kernel, shards, channels, token...]
    ppermute x2, waiting for transfers between devices: 0.45 us -> 0.01 us  [direct_body(): lax.ppermute(value, 'chan', [(i, i ^ bits) for i in range(groups)])]
    pallas_call x1, Pallas kernels: 2.18 us -> 1.9 us  [convolve(): pl.pallas_call(functools.partial(convolve_kernel, shards, channels, token...]
  transfers between devices with their start and end apart: 9 -> 9, of which waited for: 6 -> 5; matrix products, arithmetic and copies ran while one was open for 0% -> 0% of each run, Pallas kernels for 15% -> 16%
where the time goes in v5:
time: 24.5 us; the launch traced here: 24.4 us
  starting transfers between devices  9.36 us (38%)
  waiting for transfers between devices  7.16 us (29%)
  Pallas kernels  6.54 us (27%)
  between operations  0.68 us (3%)
  other arithmetic  0.61 us (2%)
    ppermute x7, waiting for transfers between devices, flipped(): lax.ppermute(value, 'context', [(i, i ^ bits) for i in range(shards)])  7.16 us
    ppermute x7, starting transfers between devices, flipped(): lax.ppermute(value, 'context', [(i, i ^ bits) for i in range(shards)])  4.88 us
    ppermute x2, starting transfers between devices, direct_body(): lax.ppermute(value, 'chan', [(i, i ^ bits) for i in range(groups)])  4.48 us
    pallas_call x1, Pallas kernels, toeplitz_tiles(): pl.pallas_call(functools.partial(toeplitz_kernel, shards, channels, token...  1.92 us
    pallas_call x1, Pallas kernels, convolve(): pl.pallas_call(functools.partial(convolve_kernel, shards, channels, token...  1.9 us
    pallas_call x1, Pallas kernels, filter_grad(): pl.pallas_call(functools.partial(filter_grad_kernel, shards, channels, to...  1.84 us
    pallas_call x1, Pallas kernels, stack_local(): pl.pallas_call(stack_kernel, out_shape=pltpu.VMEM((rows, LANES), jnp.floa...  0.88 us
    mul x1, other arithmetic, direct_body(): grad_filter = value.reshape(tokens) * (1.0 / math.sqrt(shards * tokens))  0.6 us
  transfers between devices with their start and end apart: 9, of which 5 were waited for; matrix products, arithmetic and copies ran while one was open for 0% of the time, Pallas kernels for 16%

profile of v5, /device:TPU:0, one launch (start us, length us, event | category | flops | bytes accessed | tf_op | source)
XLA Modules:
  0.0 24.4 jit_solution(10313820092430968610)
XLA Ops:
  0.6 0.9 %stack_local.1.refs_0_ = f32[264,128]{1,0:T(8,128)S(1)} custom-call(f32[16,1024]{1,0:T(8,128)} %signal_ref.1, f32[16,1024]{1,0:T(8,128)} %cotangent_ref.1, f32[8,128]{1,0:T(8,128)} %bitcast.4), custom_call_target="tpu_custom_call" | custom-call | tf_op jit(solution)/shard_map/stack_local/pallas_call | solution.py:53
  1.5 4.0 %collective-permute-start.5 = (f32[264,128]{1,0:T(8,128)S(1)}, f32[264,128]{1,0:T(8,128)S(1)}, u32[]{:S(2)}, u32[]{:S(2)}) collective-permute-start(f32[264,128]{1,0:T(8,128)S(1)} %stack_local.1.refs_0_), channel_id=1, source_target_pairs={{0,24},{4,28},{8,16},{12,20},{16,8},{20,12},{24,0},{28,4},{1,25},{... | collective-permute-start | bytes 405512 | tf_op jit(solution)/shard_map/ppermute | solution.py:64
  5.5 0.5 %collective-permute-start.3 = (f32[264,128]{1,0:T(8,128)S(1)}, f32[264,128]{1,0:T(8,128)S(1)}, u32[]{:S(2)}, u32[]{:S(2)}) collective-permute-start(f32[264,128]{1,0:T(8,128)S(1)} %stack_local.1.refs_0_), channel_id=1, source_target_pairs={{0,16},{4,20},{8,24},{12,28},{16,0},{20,4},{24,8},{28,12},{1,17},{... | collective-permute-start | bytes 405512 | tf_op jit(solution)/shard_map/ppermute | solution.py:64
  6.0 0.1 collective-permute-start.1
  6.1 0.0 collective-permute-start
  6.1 3.3 %collective-permute-done.5.refs_6_ = f32[264,128]{1,0:T(8,128)S(1)} collective-permute-done((f32[264,128]{1,0:T(8,128)S(1)}, f32[264,128]{1,0:T(8,128)S(1)}, u32[]{:S(2)}, u32[]{:S(2)}) %collective-permute-start.5) | collective-permute-done | bytes 135200 | tf_op jit(solution)/shard_map/ppermute | solution.py:64
  9.5 0.0 collective-permute-start.6
  9.5 2.5 %collective-permute-done.3.refs_4_ = f32[264,128]{1,0:T(8,128)S(1)} collective-permute-done((f32[264,128]{1,0:T(8,128)S(1)}, f32[264,128]{1,0:T(8,128)S(1)}, u32[]{:S(2)}, u32[]{:S(2)}) %collective-permute-start.3) | collective-permute-done | bytes 135200 | tf_op jit(solution)/shard_map/ppermute | solution.py:64
  12.0 0.0 collective-permute-start.4
  12.0 0.2 collective-permute-done.1.refs_2_
  12.2 0.3 %collective-permute-start.2 = (f32[264,128]{1,0:T(8,128)S(1)}, f32[264,128]{1,0:T(8,128)S(1)}, u32[]{:S(2)}, u32[]{:S(2)}) collective-permute-start(f32[264,128]{1,0:T(8,128)S(1)} %collective-permute-done.1.refs_2_), channel_id=1, source_target_pairs={{0,4},{4,0},{8,12},{12,8},{16,20},{20,16},{24,28},{28,24},{1,5},{5... | collective-permute-start | bytes 405512 | tf_op jit(solution)/shard_map/ppermute | solution.py:64
  12.5 0.0 collective-permute-done.refs_1_
  12.5 0.0 collective-permute-done.6.refs_7_
  12.5 0.8 %collective-permute-done.4.refs_5_ = f32[264,128]{1,0:T(8,128)S(1)} collective-permute-done((f32[264,128]{1,0:T(8,128)S(1)}, f32[264,128]{1,0:T(8,128)S(1)}, u32[]{:S(2)}, u32[]{:S(2)}) %collective-permute-start.4) | collective-permute-done | bytes 135200 | tf_op jit(solution)/shard_map/ppermute | solution.py:64
  13.3 0.2 %collective-permute-done.2.refs_3_ = f32[264,128]{1,0:T(8,128)S(1)} collective-permute-done((f32[264,128]{1,0:T(8,128)S(1)}, f32[264,128]{1,0:T(8,128)S(1)}, u32[]{:S(2)}, u32[]{:S(2)}) %collective-permute-start.2) | collective-permute-done | bytes 135200 | tf_op jit(solution)/shard_map/ppermute | solution.py:64
  13.6 1.8 %filter_grad.1 = (f32[1,1024]{1,0:T(1,128)S(1)}, bf16[2304,128]{1,0:T(8,128)(2,1)S(1)}, bf16[4096,128]{1,0:T(8,128)(2,1)S(1)}) custom-call(f32[264,128]{1,0:T(8,128)S(1)} %stack_local.1.refs_0_, f32[264,128]{1,0:T(8,128)S(1)} %collective-permute-done.refs_1_, f32[264,128]{1,0:T(8,128)S(1)} %collective-permute-done.1.refs_2_, ...), custom_call_target="tpu_custom_call" | custom-call | flops 1006632960 | bytes 1048576 | tf_op jit(solution)/shard_map/filter_grad/pallas_call | solution.py:129
  15.4 0.0 copy-start
  15.4 1.8 %collective-permute-start.7 = (f32[1,1024]{1,0:T(1,128)S(1)}, f32[1,1024]{1,0:T(1,128)S(1)}, u32[]{:S(2)}, u32[]{:S(2)}) collective-permute-start(f32[1,1024]{1,0:T(1,128)S(1)} %get-tuple-element.17), channel_id=1, source_target_pairs={{0,1},{1,0},{2,3},{3,2},{4,5},{5,4},{6,7},{7,6},{8,9},{9,8},{10,11... | collective-permute-start | bytes 12296 | tf_op jit(solution)/shard_map/ppermute | solution.py:286
  17.2 1.9 %toeplitz_tiles.1 = (bf16[65,128,128]{2,1,0:T(8,128)(2,1)S(1)}, bf16[65,128,128]{2,1,0:T(8,128)(2,1)S(1)}, f32[256,256]{1,0:T(8,128)S(1)}) custom-call(f32[264,128]{1,0:T(8,128)S(1)} %stack_local.1.refs_0_, f32[264,128]{1,0:T(8,128)S(1)} %collective-permute-done.refs_1_, f32[264,128]{1,0:T(8,128)S(1)} %collective-permute-done.1.refs_2_, ...), custom_call_target="tpu_custom_call" | custom-call | flops 17039360 | bytes 4259840 | tf_op jit(solution)/shard_map/toeplitz_tiles/pallas_call | solution.py:210
  19.1 0.0 collective-permute-done.7
  19.1 2.7 %collective-permute-start.8 = (f32[1,1024]{1,0:T(1,128)S(1)}, f32[1,1024]{1,0:T(1,128)S(1)}, u32[]{:S(2)}, u32[]{:S(2)}) collective-permute-start(f32[1,1024]{1,0:T(1,128)S(1)} %add.6), channel_id=1, source_target_pairs={{0,2},{1,3},{2,0},{3,1},{4,6},{5,7},{6,4},{7,5},{8,10},{9,11},{10,... | collective-permute-start | bytes 12296 | tf_op jit(solution)/shard_map/ppermute | solution.py:286
  21.8 0.0 copy-done
  21.9 1.9 %convolve.1 = (f32[16,1024]{1,0:T(8,128)}, f32[16,1024]{1,0:T(8,128)}) custom-call(f32[264,128]{1,0:T(8,128)S(1)} %stack_local.1.refs_0_, bf16[2304,128]{1,0:T(8,128)(2,1)S(1)} %get-tuple-element.15.refs_8_.refs_1_, bf16[4096,128]{1,0:T(8,128)(2,1)S(1)} %get-tuple-element.16.refs_9_.refs_2_, bf16[65,128,128]{2,1,0:T(8,128)(2,1)S(1)} %get-tuple-element.21.refs_3_, ...), custom_call_target="tpu_custom_call" | custom-call | flops 1207959552 | bytes 2097152 | tf_op jit(solution)/shard_map/convolve/pallas_call | solution.py:261
  23.7 0.0 collective-permute-done.8
  23.8 0.6 %add_multiply_fusion = f32[1,1024]{1,0:T(1,128)} fusion(f32[1,1024]{1,0:T(1,128)S(1)} %add.6, f32[1,1024]{1,0:T(1,128)S(1)} %collective-permute-done.8), kind=kLoop, calls=%fused_computation | loop fusion | flops 2048 | bytes 12288 | tf_op jit(solution)/shard_map/mul | solution.py:291
  (1 shorter events, 0.0 us)
Async XLA Ops:
  1.5 8.0 %collective-permute-start.5 = (f32[264,128]{1,0:T(8,128)S(1)}, f32[264,128]{1,0:T(8,128)S(1)}, u32[]{:S(2)}, u32[]{:S(2)}) collective-permute-start(f32[264,128]{1,0:T(8,128)S(1)} %stack_local.1.refs_0_), channel_id=1, source_target_pairs={{0,24},{4,28},{8,16},{12,20},{16,8},{20,12},{24,0},{28,4},{1,25},{... | collective-permute-start | bytes 405512 | tf_op jit(solution)/shard_map/ppermute | solution.py:64
  5.5 6.5 %collective-permute-start.3 = (f32[264,128]{1,0:T(8,128)S(1)}, f32[264,128]{1,0:T(8,128)S(1)}, u32[]{:S(2)}, u32[]{:S(2)}) collective-permute-start(f32[264,128]{1,0:T(8,128)S(1)} %stack_local.1.refs_0_), channel_id=1, source_target_pairs={{0,16},{4,20},{8,24},{12,28},{16,0},{20,4},{24,8},{28,12},{1,17},{... | collective-permute-start | bytes 405512 | tf_op jit(solution)/shard_map/ppermute | solution.py:64
  6.0 6.2 %collective-permute-start.1 = (f32[264,128]{1,0:T(8,128)S(1)}, f32[264,128]{1,0:T(8,128)S(1)}, u32[]{:S(2)}, u32[]{:S(2)}) collective-permute-start(f32[264,128]{1,0:T(8,128)S(1)} %stack_local.1.refs_0_), channel_id=1, source_target_pairs={{0,8},{4,12},{8,0},{12,4},{16,24},{20,28},{24,16},{28,20},{1,9},{5... | collective-permute-start | bytes 405512 | tf_op jit(solution)/shard_map/ppermute | solution.py:64
  6.1 6.4 %collective-permute-start = (f32[264,128]{1,0:T(8,128)S(1)}, f32[264,128]{1,0:T(8,128)S(1)}, u32[]{:S(2)}, u32[]{:S(2)}) collective-permute-start(f32[264,128]{1,0:T(8,128)S(1)} %stack_local.1.refs_0_), channel_id=1, source_target_pairs={{0,4},{4,0},{8,12},{12,8},{16,20},{20,16},{24,28},{28,24},{1,5},{5... | collective-permute-start | bytes 405512 | tf_op jit(solution)/shard_map/ppermute | solution.py:64
  9.5 3.0 %collective-permute-start.6 = (f32[264,128]{1,0:T(8,128)S(1)}, f32[264,128]{1,0:T(8,128)S(1)}, u32[]{:S(2)}, u32[]{:S(2)}) collective-permute-start(f32[264,128]{1,0:T(8,128)S(1)} %collective-permute-done.5.refs_6_), channel_id=1, source_target_pairs={{0,4},{4,0},{8,12},{12,8},{16,20},{20,16},{24,28},{28,24},{1,5},{5... | collective-permute-start | bytes 405512 | tf_op jit(solution)/shard_map/ppermute | solution.py:64
  12.0 1.4 %collective-permute-start.4 = (f32[264,128]{1,0:T(8,128)S(1)}, f32[264,128]{1,0:T(8,128)S(1)}, u32[]{:S(2)}, u32[]{:S(2)}) collective-permute-start(f32[264,128]{1,0:T(8,128)S(1)} %collective-permute-done.3.refs_4_), channel_id=1, source_target_pairs={{0,4},{4,0},{8,12},{12,8},{16,20},{20,16},{24,28},{28,24},{1,5},{5... | collective-permute-start | bytes 405512 | tf_op jit(solution)/shard_map/ppermute | solution.py:64
  12.2 1.4 %collective-permute-start.2 = (f32[264,128]{1,0:T(8,128)S(1)}, f32[264,128]{1,0:T(8,128)S(1)}, u32[]{:S(2)}, u32[]{:S(2)}) collective-permute-start(f32[264,128]{1,0:T(8,128)S(1)} %collective-permute-done.1.refs_2_), channel_id=1, source_target_pairs={{0,4},{4,0},{8,12},{12,8},{16,20},{20,16},{24,28},{28,24},{1,5},{5... | collective-permute-start | bytes 405512 | tf_op jit(solution)/shard_map/ppermute | solution.py:64
  15.4 6.4 %copy-start = (f32[16]{0:T(128)S(1)}, f32[16]{0:T(128)}, u32[]{:S(2)}) copy-start(f32[16]{0:T(128)} %param.6) | copy-start | bytes 196
  15.4 3.7 %collective-permute-start.7 = (f32[1,1024]{1,0:T(1,128)S(1)}, f32[1,1024]{1,0:T(1,128)S(1)}, u32[]{:S(2)}, u32[]{:S(2)}) collective-permute-start(f32[1,1024]{1,0:T(1,128)S(1)} %get-tuple-element.17), channel_id=1, source_target_pairs={{0,1},{1,0},{2,3},{3,2},{4,5},{5,4},{6,7},{7,6},{8,9},{9,8},{10,11... | collective-permute-start | bytes 12296 | tf_op jit(solution)/shard_map/ppermute | solution.py:286
  19.1 4.6 %collective-permute-start.8 = (f32[1,1024]{1,0:T(1,128)S(1)}, f32[1,1024]{1,0:T(1,128)S(1)}, u32[]{:S(2)}, u32[]{:S(2)}) collective-permute-start(f32[1,1024]{1,0:T(1,128)S(1)} %add.6), channel_id=1, source_target_pairs={{0,2},{1,3},{2,0},{3,1},{4,6},{5,7},{6,4},{7,5},{8,10},{9,11},{10,... | collective-permute-start | bytes 12296 | tf_op jit(solution)/shard_map/ppermute | solution.py:286

commit v6 on v4

--- a/solution.py
+++ b/solution.py
@@ -143,6 +143,20 @@
     )(*blocks)
 
 
+def convolve_block(held, me, tiles, channels, toe_high, toe_low, block, adjoint):
+    count = 2 * tiles * channels
+    lags = [block * tiles + n for n in range(tiles)]
+
+    def window(lag):
+        tile = me * tiles + lag if adjoint else (me + 1) * tiles - lag
+        return held[pl.ds(pl.multiple_of(tile * 2 * channels, PACKED_ROWS), count), :]
+
+    side = 0 if adjoint else 1
+    left = jnp.concatenate([window(lag) for lag in lags], axis=1)
+    pairs = [jnp.concatenate([toe_high[lag + 1], toe_low[lag + 1]], axis=side) for lag in lags]
+    return dot(left, jnp.concatenate(pairs, axis=1 - side), 1, 1 - side)
+
+
 def toeplitz_kernel(shards, channels, tokens, *refs):
     blocks, high_ref, low_ref, taps, skew = refs[:shards], *refs[shards:]
     me = lax.axis_index("context")
@@ -201,28 +215,16 @@
     own_ref, sig, cot, toe_high, toe_low, gain_ref, out_ref, back_ref, conv, back = refs
     me = lax.axis_index("context")
     tiles = tokens // LANES
-    count = 2 * tiles * channels
-
-    def window(ref, tile):
-        return ref[pl.ds(pl.multiple_of(tile * 2 * channels, PACKED_ROWS), count), :]
-
-    def forward(lags):
-        left = jnp.concatenate([window(sig, (me + 1) * tiles - lag) for lag in lags], axis=1)
-        pairs = [jnp.concatenate([toe_high[lag + 1], toe_low[lag + 1]], axis=1) for lag in lags]
-        return dot(left, jnp.concatenate(pairs, axis=0), 1, 0)
-
-    def backward(lags):
-        left = jnp.concatenate([window(cot, me * tiles + lag) for lag in lags], axis=1)
-        pairs = [jnp.concatenate([toe_high[lag + 1], toe_low[lag + 1]], axis=0) for lag in lags]
-        return dot(left, jnp.concatenate(pairs, axis=1), 1, 1)
-
-    def total(product, blocks):
-        parts = [product([block * tiles + n for n in range(tiles)]) for block in range(blocks)]
+
+    def total(held, blocks, adjoint):
+        parts = [
+            convolve_block(held, me, tiles, channels, toe_high, toe_low, block, adjoint) for block in range(blocks)
+        ]
         return sum(parts[1:], parts[0])
 
     def run(index):
-        conv[...] = total(forward, index + 1)
-        back[...] = total(backward, shards - index)
+        conv[...] = total(sig, index + 1, False)
+        back[...] = total(cot, shards - index, True)
 
     for index in range(shards):
         pl.when(me == index)(functools.partial(run, index))
@@ -247,7 +249,7 @@
     count = 2 * channels * tokens // LANES
     return pl.pallas_call(
         functools.partial(convolve_kernel, shards, channels, tokens),
-        out_shape=[jax.ShapeDtypeStruct((channels, tokens), jnp.float32)] * 2,
+        out_shape=[pltpu.VMEM((channels, tokens), jnp.float32)] * 2,
         in_specs=[pl.BlockSpec(memory_space=pltpu.VMEM)] * 6,
         out_specs=[pl.BlockSpec(memory_space=pltpu.VMEM)] * 2,
         scratch_shapes=[pltpu.VMEM((count, 2 * LANES), jnp.float32)] * 2,
@@ -261,6 +263,23 @@
     )(own, *held, *toeplitz, skip_gain.reshape(1, channels))
 
 
+def finish_kernel(scale, value_ref, other_ref, output_ref, grad_ref, filter_out, output_out, grad_out):
+    filter_out[...] = (value_ref[...] + other_ref[...]) * scale
+    output_out[...] = output_ref[...]
+    grad_out[...] = grad_ref[...]
+
+
+def finish(value, other, output, grad_signal, scale):
+    return pl.pallas_call(
+        functools.partial(finish_kernel, scale),
+        out_shape=[jax.ShapeDtypeStruct(x.shape, x.dtype) for x in (value, output, grad_signal)],
+        in_specs=[pl.BlockSpec(memory_space=pltpu.VMEM)] * 4,
+        out_specs=[pl.BlockSpec(memory_space=pltpu.VMEM)] * 3,
+        compiler_params=pltpu.CompilerParams(vmem_limit_bytes=KERNEL_BYTES),
+        name="finish",
+    )(value, other, output, grad_signal)
+
+
 def direct_body(signal, filter_taps, skip_gain, cotangent):
     shards, groups = lax.axis_size("context"), lax.axis_size("chan")
     channels, tokens = signal.shape
@@ -268,15 +287,18 @@
     blocks = gather_blocks(stacked, shards)
     value, *held = filter_grad(blocks, shards, channels, tokens)
     toeplitz = toeplitz_tiles(blocks, shards, channels, tokens)
+    other = None
     bits = 1
     while bits < groups:
-        value = value + lax.ppermute(value, "chan", [(i, i ^ bits) for i in range(groups)])
-        if bits == 1:
+        if other is not None:
+            value = value + other
             value, *toeplitz = lax.optimization_barrier((value, *toeplitz))
+        other = lax.ppermute(value, "chan", [(i, i ^ bits) for i in range(groups)])
         bits *= 2
     output, grad_signal = convolve(blocks[0], held, toeplitz, skip_gain, shards, channels, tokens)
-    grad_filter = value.reshape(tokens) * (1.0 / math.sqrt(shards * tokens))
-    return (output, grad_signal, grad_filter)
+    scale = 1.0 / math.sqrt(shards * tokens)
+    grad_filter, output, grad_signal = finish(value, other, output, grad_signal, scale)
+    return (output, grad_signal, grad_filter.reshape(tokens))
 
 
 def rotation(first, second, period):

time: 24.8 us -> 24.4 us (0.984)
  other arithmetic: 0.61 us -> 0.01 us
  waiting for transfers between devices: 7.61 us -> 7.86 us
    pallas_call x0 -> x1, Pallas kernels: none -> 0.66 us  [finish(): pl.pallas_call(functools.partial(finish_kernel, scale), out_shape=[jax.Sh...]
    pallas_call x1, Pallas kernels: 2.18 us -> 1.53 us  [convolve(): pl.pallas_call(functools.partial(convolve_kernel, shards, channels, token...]
    mul x1 -> x0, other arithmetic: 0.6 us -> none  [direct_body(): grad_filter = value.reshape(tokens) * (1.0 / math.sqrt(shards * tokens))]
  transfers between devices with their start and end apart: 9 -> 9, of which waited for: 6 -> 7; matrix products, arithmetic and copies ran while one was open for 0% -> 0% of each run, Pallas kernels for 15% -> 12%
where the time goes in v6:
time: 24.4 us; the launch traced here: 24.3 us
  starting transfers between devices  9.38 us (38%)
  waiting for transfers between devices  7.86 us (32%)
  Pallas kernels  6.34 us (26%)
  between operations  0.67 us (3%)
    ppermute x7, waiting for transfers between devices, flipped(): lax.ppermute(value, 'context', [(i, i ^ bits) for i in range(shards)])  7.16 us
    ppermute x7, starting transfers between devices, flipped(): lax.ppermute(value, 'context', [(i, i ^ bits) for i in range(shards)])  4.88 us
    ppermute x2, starting transfers between devices, direct_body(): other = lax.ppermute(value, 'chan', [(i, i ^ bits) for i in range(groups)])  4.5 us
    pallas_call x1, Pallas kernels, filter_grad(): pl.pallas_call(functools.partial(filter_grad_kernel, shards, channels, to...  1.83 us
    pallas_call x1, Pallas kernels, convolve(): pl.pallas_call(functools.partial(convolve_kernel, shards, channels, token...  1.53 us
    pallas_call x1, Pallas kernels, toeplitz_tiles(): pl.pallas_call(functools.partial(toeplitz_kernel, shards, channels, token...  1.44 us
    pallas_call x1, Pallas kernels, stack_local(): pl.pallas_call(stack_kernel, out_shape=pltpu.VMEM((rows, LANES), jnp.floa...  0.88 us
    ppermute x2, waiting for transfers between devices, direct_body(): other = lax.ppermute(value, 'chan', [(i, i ^ bits) for i in range(groups)])  0.7 us
  transfers between devices with their start and end apart: 9, of which 7 were waited for; matrix products, arithmetic and copies ran while one was open for 0% of the time, Pallas kernels for 12%

profile of v6, /device:TPU:0, one launch (start us, length us, event | category | flops | bytes accessed | tf_op | source)
XLA Modules:
  0.0 24.3 jit_solution(6988980163088449999)
XLA Ops:
  0.6 0.9 %stack_local.1.refs_0_ = f32[264,128]{1,0:T(8,128)S(1)} custom-call(f32[16,1024]{1,0:T(8,128)} %signal_ref.1, f32[16,1024]{1,0:T(8,128)} %cotangent_ref.1, f32[8,128]{1,0:T(8,128)} %bitcast.4), custom_call_target="tpu_custom_call" | custom-call | tf_op jit(solution)/shard_map/stack_local/pallas_call | solution.py:52
  1.5 0.0 copy-start
  1.5 4.0 %collective-permute-start.5 = (f32[264,128]{1,0:T(8,128)S(1)}, f32[264,128]{1,0:T(8,128)S(1)}, u32[]{:S(2)}, u32[]{:S(2)}) collective-permute-start(f32[264,128]{1,0:T(8,128)S(1)} %stack_local.1.refs_0_), channel_id=1, source_target_pairs={{0,24},{4,28},{8,16},{12,20},{16,8},{20,12},{24,0},{28,4},{1,25},{... | collective-permute-start | bytes 405512 | tf_op jit(solution)/shard_map/ppermute | solution.py:63
  5.5 0.5 %collective-permute-start.3 = (f32[264,128]{1,0:T(8,128)S(1)}, f32[264,128]{1,0:T(8,128)S(1)}, u32[]{:S(2)}, u32[]{:S(2)}) collective-permute-start(f32[264,128]{1,0:T(8,128)S(1)} %stack_local.1.refs_0_), channel_id=1, source_target_pairs={{0,16},{4,20},{8,24},{12,28},{16,0},{20,4},{24,8},{28,12},{1,17},{... | collective-permute-start | bytes 405512 | tf_op jit(solution)/shard_map/ppermute | solution.py:63
  6.0 0.1 collective-permute-start.1
  6.1 0.0 collective-permute-start
  6.1 3.3 %collective-permute-done.5.refs_6_ = f32[264,128]{1,0:T(8,128)S(1)} collective-permute-done((f32[264,128]{1,0:T(8,128)S(1)}, f32[264,128]{1,0:T(8,128)S(1)}, u32[]{:S(2)}, u32[]{:S(2)}) %collective-permute-start.5) | collective-permute-done | bytes 135200 | tf_op jit(solution)/shard_map/ppermute | solution.py:63
  9.5 0.0 collective-permute-start.6
  9.5 2.5 %collective-permute-done.3.refs_4_ = f32[264,128]{1,0:T(8,128)S(1)} collective-permute-done((f32[264,128]{1,0:T(8,128)S(1)}, f32[264,128]{1,0:T(8,128)S(1)}, u32[]{:S(2)}, u32[]{:S(2)}) %collective-permute-start.3) | collective-permute-done | bytes 135200 | tf_op jit(solution)/shard_map/ppermute | solution.py:63
  12.0 0.0 collective-permute-start.4
  12.0 0.2 collective-permute-done.1.refs_2_
  12.2 0.3 %collective-permute-start.2 = (f32[264,128]{1,0:T(8,128)S(1)}, f32[264,128]{1,0:T(8,128)S(1)}, u32[]{:S(2)}, u32[]{:S(2)}) collective-permute-start(f32[264,128]{1,0:T(8,128)S(1)} %collective-permute-done.1.refs_2_), channel_id=1, source_target_pairs={{0,4},{4,0},{8,12},{12,8},{16,20},{20,16},{24,28},{28,24},{1,5},{5... | collective-permute-start | bytes 405512 | tf_op jit(solution)/shard_map/ppermute | solution.py:63
  12.5 0.0 collective-permute-done.refs_1_
  12.5 0.0 collective-permute-done.6.refs_7_
  12.5 0.8 %collective-permute-done.4.refs_5_ = f32[264,128]{1,0:T(8,128)S(1)} collective-permute-done((f32[264,128]{1,0:T(8,128)S(1)}, f32[264,128]{1,0:T(8,128)S(1)}, u32[]{:S(2)}, u32[]{:S(2)}) %collective-permute-start.4) | collective-permute-done | bytes 135200 | tf_op jit(solution)/shard_map/ppermute | solution.py:63
  13.3 0.2 %collective-permute-done.2.refs_3_ = f32[264,128]{1,0:T(8,128)S(1)} collective-permute-done((f32[264,128]{1,0:T(8,128)S(1)}, f32[264,128]{1,0:T(8,128)S(1)}, u32[]{:S(2)}, u32[]{:S(2)}) %collective-permute-start.2) | collective-permute-done | bytes 135200 | tf_op jit(solution)/shard_map/ppermute | solution.py:63
  13.6 1.8 %filter_grad.1 = (f32[1,1024]{1,0:T(1,128)S(1)}, bf16[2304,128]{1,0:T(8,128)(2,1)S(1)}, bf16[4096,128]{1,0:T(8,128)(2,1)S(1)}) custom-call(f32[264,128]{1,0:T(8,128)S(1)} %stack_local.1.refs_0_, f32[264,128]{1,0:T(8,128)S(1)} %collective-permute-done.refs_1_, f32[264,128]{1,0:T(8,128)S(1)} %collective-permute-done.1.refs_2_, ...), custom_call_target="tpu_custom_call" | custom-call | flops 1006632960 | bytes 1048576 | tf_op jit(solution)/shard_map/filter_grad/pallas_call | solution.py:128
  15.4 1.8 %collective-permute-start.7 = (f32[1,1024]{1,0:T(1,128)S(1)}, f32[1,1024]{1,0:T(1,128)S(1)}, u32[]{:S(2)}, u32[]{:S(2)}) collective-permute-start(f32[1,1024]{1,0:T(1,128)S(1)} %get-tuple-element.16), channel_id=1, source_target_pairs={{0,1},{1,0},{2,3},{3,2},{4,5},{5,4},{6,7},{7,6},{8,9},{9,8},{10,11... | collective-permute-start | bytes 12296 | tf_op jit(solution)/shard_map/ppermute | solution.py:296
  17.2 1.4 %toeplitz_tiles.1 = (bf16[65,128,128]{2,1,0:T(8,128)(2,1)S(1)}, bf16[65,128,128]{2,1,0:T(8,128)(2,1)S(1)}) custom-call(f32[264,128]{1,0:T(8,128)S(1)} %stack_local.1.refs_0_, f32[264,128]{1,0:T(8,128)S(1)} %collective-permute-done.refs_1_, f32[264,128]{1,0:T(8,128)S(1)} %collective-permute-done.1.refs_2_, f32[264,128]{1,0:T(8,128)S(1)} %collective-permute-done.2.refs_3_, ...), custom_call_target="tpu_custom_call" | custom-call | flops 17039360 | bytes 4259840 | tf_op jit(solution)/shard_map/toeplitz_tiles/pallas_call | solution.py:200
  18.6 0.5 %collective-permute-done.7 = f32[1,1024]{1,0:T(1,128)S(1)} collective-permute-done((f32[1,1024]{1,0:T(1,128)S(1)}, f32[1,1024]{1,0:T(1,128)S(1)}, u32[]{:S(2)}, u32[]{:S(2)}) %collective-permute-start.7) | collective-permute-done | bytes 4128 | tf_op jit(solution)/shard_map/ppermute | solution.py:296
  19.1 2.7 %collective-permute-start.8 = (f32[1,1024]{1,0:T(1,128)S(1)}, f32[1,1024]{1,0:T(1,128)S(1)}, u32[]{:S(2)}, u32[]{:S(2)}) collective-permute-start(f32[1,1024]{1,0:T(1,128)S(1)} %add.3.value_ref), channel_id=1, source_target_pairs={{0,2},{1,3},{2,0},{3,1},{4,6},{5,7},{6,4},{7,5},{8,10},{9,11},{10,... | collective-permute-start | bytes 12296 | tf_op jit(solution)/shard_map/ppermute | solution.py:296
  21.8 0.0 copy-done
  21.8 1.5 %convolve.1 = (f32[16,1024]{1,0:T(8,128)S(1)}, f32[16,1024]{1,0:T(8,128)S(1)}) custom-call(f32[264,128]{1,0:T(8,128)S(1)} %stack_local.1.refs_0_, bf16[2304,128]{1,0:T(8,128)(2,1)S(1)} %get-tuple-element.20.refs_1_, bf16[4096,128]{1,0:T(8,128)(2,1)S(1)} %get-tuple-element.21.refs_2_, bf16[65,128,128]{2,1,0:T(8,128)(2,1)S(1)} %get-tuple-element.22.refs_3_, ...), custom_call_target="tpu_custom_call" | custom-call | flops 1207959552 | bytes 2097152 | tf_op jit(solution)/shard_map/convolve/pallas_call | solution.py:250
  23.3 0.3 %collective-permute-done.8.other_ref = f32[1,1024]{1,0:T(1,128)S(1)} collective-permute-done((f32[1,1024]{1,0:T(1,128)S(1)}, f32[1,1024]{1,0:T(1,128)S(1)}, u32[]{:S(2)}, u32[]{:S(2)}) %collective-permute-start.8) | collective-permute-done | bytes 4128 | tf_op jit(solution)/shard_map/ppermute | solution.py:296
  23.6 0.7 %finish.1 = (f32[1,1024]{1,0:T(1,128)}, f32[16,1024]{1,0:T(8,128)}, f32[16,1024]{1,0:T(8,128)}) custom-call(f32[1,1024]{1,0:T(1,128)S(1)} %add.3.value_ref, f32[1,1024]{1,0:T(1,128)S(1)} %collective-permute-done.8.other_ref, f32[16,1024]{1,0:T(8,128)S(1)} %get-tuple-element.24.output_ref, f32[16,1024]{1,0:T(8,128)S(1)} %get-tuple-element.25.grad_ref), custom_call_target="tpu_custom_call" | custom-call | tf_op jit(solution)/shard_map/finish/pallas_call | solution.py:273
  (1 shorter events, 0.0 us)
Async XLA Ops:
  1.5 20.3 %copy-start = (f32[16]{0:T(128)S(1)}, f32[16]{0:T(128)}, u32[]{:S(2)}) copy-start(f32[16]{0:T(128)} %param.6) | copy-start | bytes 196
  1.5 8.0 %collective-permute-start.5 = (f32[264,128]{1,0:T(8,128)S(1)}, f32[264,128]{1,0:T(8,128)S(1)}, u32[]{:S(2)}, u32[]{:S(2)}) collective-permute-start(f32[264,128]{1,0:T(8,128)S(1)} %stack_local.1.refs_0_), channel_id=1, source_target_pairs={{0,24},{4,28},{8,16},{12,20},{16,8},{20,12},{24,0},{28,4},{1,25},{... | collective-permute-start | bytes 405512 | tf_op jit(solution)/shard_map/ppermute | solution.py:63
  5.5 6.5 %collective-permute-start.3 = (f32[264,128]{1,0:T(8,128)S(1)}, f32[264,128]{1,0:T(8,128)S(1)}, u32[]{:S(2)}, u32[]{:S(2)}) collective-permute-start(f32[264,128]{1,0:T(8,128)S(1)} %stack_local.1.refs_0_), channel_id=1, source_target_pairs={{0,16},{4,20},{8,24},{12,28},{16,0},{20,4},{24,8},{28,12},{1,17},{... | collective-permute-start | bytes 405512 | tf_op jit(solution)/shard_map/ppermute | solution.py:63
  6.0 6.2 %collective-permute-start.1 = (f32[264,128]{1,0:T(8,128)S(1)}, f32[264,128]{1,0:T(8,128)S(1)}, u32[]{:S(2)}, u32[]{:S(2)}) collective-permute-start(f32[264,128]{1,0:T(8,128)S(1)} %stack_local.1.refs_0_), channel_id=1, source_target_pairs={{0,8},{4,12},{8,0},{12,4},{16,24},{20,28},{24,16},{28,20},{1,9},{5... | collective-permute-start | bytes 405512 | tf_op jit(solution)/shard_map/ppermute | solution.py:63
  6.1 6.4 %collective-permute-start = (f32[264,128]{1,0:T(8,128)S(1)}, f32[264,128]{1,0:T(8,128)S(1)}, u32[]{:S(2)}, u32[]{:S(2)}) collective-permute-start(f32[264,128]{1,0:T(8,128)S(1)} %stack_local.1.refs_0_), channel_id=1, source_target_pairs={{0,4},{4,0},{8,12},{12,8},{16,20},{20,16},{24,28},{28,24},{1,5},{5... | collective-permute-start | bytes 405512 | tf_op jit(solution)/shard_map/ppermute | solution.py:63
  9.5 3.0 %collective-permute-start.6 = (f32[264,128]{1,0:T(8,128)S(1)}, f32[264,128]{1,0:T(8,128)S(1)}, u32[]{:S(2)}, u32[]{:S(2)}) collective-permute-start(f32[264,128]{1,0:T(8,128)S(1)} %collective-permute-done.5.refs_6_), channel_id=1, source_target_pairs={{0,4},{4,0},{8,12},{12,8},{16,20},{20,16},{24,28},{28,24},{1,5},{5... | collective-permute-start | bytes 405512 | tf_op jit(solution)/shard_map/ppermute | solution.py:63
  12.0 1.4 %collective-permute-start.4 = (f32[264,128]{1,0:T(8,128)S(1)}, f32[264,128]{1,0:T(8,128)S(1)}, u32[]{:S(2)}, u32[]{:S(2)}) collective-permute-start(f32[264,128]{1,0:T(8,128)S(1)} %collective-permute-done.3.refs_4_), channel_id=1, source_target_pairs={{0,4},{4,0},{8,12},{12,8},{16,20},{20,16},{24,28},{28,24},{1,5},{5... | collective-permute-start | bytes 405512 | tf_op jit(solution)/shard_map/ppermute | solution.py:63
  12.2 1.4 %collective-permute-start.2 = (f32[264,128]{1,0:T(8,128)S(1)}, f32[264,128]{1,0:T(8,128)S(1)}, u32[]{:S(2)}, u32[]{:S(2)}) collective-permute-start(f32[264,128]{1,0:T(8,128)S(1)} %collective-permute-done.1.refs_2_), channel_id=1, source_target_pairs={{0,4},{4,0},{8,12},{12,8},{16,20},{20,16},{24,28},{28,24},{1,5},{5... | collective-permute-start | bytes 405512 | tf_op jit(solution)/shard_map/ppermute | solution.py:63
  15.4 3.7 %collective-permute-start.7 = (f32[1,1024]{1,0:T(1,128)S(1)}, f32[1,1024]{1,0:T(1,128)S(1)}, u32[]{:S(2)}, u32[]{:S(2)}) collective-permute-start(f32[1,1024]{1,0:T(1,128)S(1)} %get-tuple-element.16), channel_id=1, source_target_pairs={{0,1},{1,0},{2,3},{3,2},{4,5},{5,4},{6,7},{7,6},{8,9},{9,8},{10,11... | collective-permute-start | bytes 12296 | tf_op jit(solution)/shard_map/ppermute | solution.py:296
  19.1 4.5 %collective-permute-start.8 = (f32[1,1024]{1,0:T(1,128)S(1)}, f32[1,1024]{1,0:T(1,128)S(1)}, u32[]{:S(2)}, u32[]{:S(2)}) collective-permute-start(f32[1,1024]{1,0:T(1,128)S(1)} %add.3.value_ref), channel_id=1, source_target_pairs={{0,2},{1,3},{2,0},{3,1},{4,6},{5,7},{6,4},{7,5},{8,10},{9,11},{10,... | collective-permute-start | bytes 12296 | tf_op jit(solution)/shard_map/ppermute | solution.py:296

commit v7 on v6

--- a/solution.py
+++ b/solution.py
@@ -10,6 +10,8 @@
 
 exact_mode = lax.Precision.HIGHEST
 
+SHARDS = 8
+FLIPS = ((0, 0), (2, 4), (6, 6), (4, 2))
 LANES = 128
 BLOCK = 256
 PACKED_ROWS = 16
@@ -25,14 +27,6 @@
 def dot(left, right, left_dim, right_dim):
     return lax.dot_general(
         left, right, (((left_dim,), (right_dim,)), ((), ())), preferred_element_type=jnp.float32
-    )
-
-
-def dot_halves(left, right, left_dim, right_dim):
-    return (
-        dot(left[0], right[0], left_dim, right_dim)
-        + dot(left[0], right[1], left_dim, right_dim)
-        + dot(left[1], right[0], left_dim, right_dim)
     )
 
 
@@ -58,16 +52,22 @@
     )(signal, cotangent, taps.reshape(tokens // LANES, LANES))
 
 
-def gather_blocks(stacked, shards):
-    def flipped(value, bits):
-        return lax.ppermute(value, "context", [(i, i ^ bits) for i in range(shards)])
+def source_index(me, entry):
+    core = me % 2 if entry % 2 == 0 else 1 - me % 2
+    even, odd = FLIPS[entry // 2]
+    return me ^ (even + (odd - even) * core + entry % 2)
+
+
+def gather_blocks(stacked):
+    def fetched(value, entry):
+        return lax.ppermute(value, "context", [(source_index(i, entry), i) for i in range(SHARDS)])
 
     found = {0: stacked}
-    for bits in range(2, shards, 2):
-        found[bits] = flipped(stacked, bits)
-    for bits in range(0, shards, 2):
-        found[bits + 1] = flipped(found[bits], 1)
-    return [found[bits] for bits in range(shards)]
+    for entry in range(2, SHARDS, 2):
+        found[entry] = fetched(stacked, entry)
+    for entry in range(0, SHARDS, 2):
+        found[entry + 1] = fetched(found[entry], 1)
+    return [found[entry] for entry in range(SHARDS)]
 
 
 def place_rows(block_ref, first, index, channels, tokens, ref, start):
@@ -98,8 +98,9 @@
     sig[:count, :] = jnp.zeros((count, LANES), jnp.bfloat16)
     cot[rows:, :] = jnp.zeros((rows, LANES), jnp.bfloat16)
     for bits in range(shards):
-        place_rows(blocks[bits], 0, me ^ bits, channels, tokens, sig, count)
-        place_rows(blocks[bits], channels * tiles, me ^ bits, channels, tokens, cot, 0)
+        index = source_index(me, bits)
+        place_rows(blocks[bits], 0, index, channels, tokens, sig, count)
+        place_rows(blocks[bits], channels * tiles, index, channels, tokens, cot, 0)
     held = [paired_tiles(sig, tiles, shards * tiles, channels, half) for half in range(2)]
     for lag in range(per + 1):
         window = [
@@ -164,7 +165,7 @@
     first = 2 * channels * tiles
     taps[0] = jnp.zeros((tiles, LANES), jnp.float32)
     for bits in range(shards):
-        taps[(me ^ bits) + 1] = blocks[bits][first : first + tiles, :]
+        taps[source_index(me, bits) + 1] = blocks[bits][first : first + tiles, :]
     high_ref[0] = jnp.zeros((LANES, LANES), jnp.bfloat16)
     low_ref[0] = jnp.zeros((LANES, LANES), jnp.bfloat16)
     width = (tiles + 1) * LANES
@@ -284,7 +285,7 @@
     shards, groups = lax.axis_size("context"), lax.axis_size("chan")
     channels, tokens = signal.shape
     stacked = stack_local(signal, cotangent, filter_taps)
-    blocks = gather_blocks(stacked, shards)
+    blocks = gather_blocks(stacked)
     value, *held = filter_grad(blocks, shards, channels, tokens)
     toeplitz = toeplitz_tiles(blocks, shards, channels, tokens)
     other = None
@@ -448,7 +449,7 @@
     scratch = 16 * shards * tokens * channels + 4 * (shards * tokens + LANES) * LANES
     groups = lax.axis_size("chan")
     whole = groups & (groups - 1) == 0 and channels % PACKED_ROWS == 0 and tokens % (8 * LANES) == 0 and shards & (shards - 1) == 0
-    return whole and shards > 1 and 2 * held + scratch < KERNEL_BYTES
+    return whole and shards == SHARDS and 2 * held + scratch < KERNEL_BYTES
 
 
 def body(signal, filter_taps, skip_gain, cotangent):

time: 24.4 us -> 24.2 us (level)
  waiting for transfers between devices: 7.86 us -> 7.59 us
    ppermute x7, waiting for transfers between devices: 7.16 us -> 6.64 us  [fetched(): lax.ppermute(value, 'context', [(source_index(i, entry), i) for i in rang...]
    ppermute x7, starting transfers between devices: 4.88 us -> 5.2 us  [fetched(): lax.ppermute(value, 'context', [(source_index(i, entry), i) for i in rang...]
    ppermute x2, waiting for transfers between devices: 0.7 us -> 0.95 us  [direct_body(): other = lax.ppermute(value, 'chan', [(i, i ^ bits) for i in range(groups)])]
    ppermute x2, starting transfers between devices: 4.5 us -> 4.26 us  [direct_body(): other = lax.ppermute(value, 'chan', [(i, i ^ bits) for i in range(groups)])]
where the time goes in v7:
time: 24.2 us; the launch traced here: 24.1 us
  starting transfers between devices  9.46 us (39%)
  waiting for transfers between devices  7.59 us (31%)
  Pallas kernels  6.35 us (26%)
  between operations  0.67 us (3%)
    ppermute x7, waiting for transfers between devices, fetched(): lax.ppermute(value, 'context', [(source_index(i, entry), i) for i in rang...  6.64 us
    ppermute x7, starting transfers between devices, fetched(): lax.ppermute(value, 'context', [(source_index(i, entry), i) for i in rang...  5.2 us
    ppermute x2, starting transfers between devices, direct_body(): other = lax.ppermute(value, 'chan', [(i, i ^ bits) for i in range(groups)])  4.26 us
    pallas_call x1, Pallas kernels, filter_grad(): pl.pallas_call(functools.partial(filter_grad_kernel, shards, channels, to...  1.84 us
    pallas_call x1, Pallas kernels, convolve(): pl.pallas_call(functools.partial(convolve_kernel, shards, channels, token...  1.52 us
    pallas_call x1, Pallas kernels, toeplitz_tiles(): pl.pallas_call(functools.partial(toeplitz_kernel, shards, channels, token...  1.44 us
    ppermute x2, waiting for transfers between devices, direct_body(): other = lax.ppermute(value, 'chan', [(i, i ^ bits) for i in range(groups)])  0.95 us
    pallas_call x1, Pallas kernels, stack_local(): pl.pallas_call(stack_kernel, out_shape=pltpu.VMEM((rows, LANES), jnp.floa...  0.88 us
  transfers between devices with their start and end apart: 9, of which 7 were waited for; matrix products, arithmetic and copies ran while one was open for 0% of the time, Pallas kernels for 12%

profile of v7, /device:TPU:0, one launch (start us, length us, event | category | flops | bytes accessed | tf_op | source)
XLA Modules:
  0.0 24.1 jit_solution(3030666380845547054)
XLA Ops:
  0.6 0.9 %stack_local.1.refs_0_ = f32[264,128]{1,0:T(8,128)S(1)} custom-call(f32[16,1024]{1,0:T(8,128)} %signal_ref.1, f32[16,1024]{1,0:T(8,128)} %cotangent_ref.1, f32[8,128]{1,0:T(8,128)} %bitcast.4), custom_call_target="tpu_custom_call" | custom-call | tf_op jit(solution)/shard_map/stack_local/pallas_call | solution.py:46
  1.5 0.0 copy-start
  1.5 3.0 %collective-permute-start.5 = (f32[264,128]{1,0:T(8,128)S(1)}, f32[264,128]{1,0:T(8,128)S(1)}, u32[]{:S(2)}, u32[]{:S(2)}) collective-permute-start(f32[264,128]{1,0:T(8,128)S(1)} %stack_local.1.refs_0_), channel_id=1, source_target_pairs={{16,0},{12,4},{24,8},{4,12},{0,16},{28,20},{8,24},{20,28},{17,1},{... | collective-permute-start | bytes 405512 | tf_op jit(solution)/shard_map/ppermute | solution.py:63
  4.6 1.4 %collective-permute-start.3 = (f32[264,128]{1,0:T(8,128)S(1)}, f32[264,128]{1,0:T(8,128)S(1)}, u32[]{:S(2)}, u32[]{:S(2)}) collective-permute-start(f32[264,128]{1,0:T(8,128)S(1)} %stack_local.1.refs_0_), channel_id=1, source_target_pairs={{24,0},{28,4},{16,8},{20,12},{8,16},{12,20},{0,24},{4,28},{25,1},{... | collective-permute-start | bytes 405512 | tf_op jit(solution)/shard_map/ppermute | solution.py:63
  6.0 0.1 collective-permute-start.1
  6.1 0.0 collective-permute-start
  6.1 5.2 %collective-permute-done.5.refs_6_ = f32[264,128]{1,0:T(8,128)S(1)} collective-permute-done((f32[264,128]{1,0:T(8,128)S(1)}, f32[264,128]{1,0:T(8,128)S(1)}, u32[]{:S(2)}, u32[]{:S(2)}) %collective-permute-start.5) | collective-permute-done | bytes 135200 | tf_op jit(solution)/shard_map/ppermute | solution.py:63
  11.3 0.0 collective-permute-start.6
  11.3 0.0 collective-permute-done.3.refs_4_
  11.3 0.5 %collective-permute-start.4 = (f32[264,128]{1,0:T(8,128)S(1)}, f32[264,128]{1,0:T(8,128)S(1)}, u32[]{:S(2)}, u32[]{:S(2)}) collective-permute-start(f32[264,128]{1,0:T(8,128)S(1)} %collective-permute-done.3.refs_4_), channel_id=1, source_target_pairs={{4,0},{0,4},{12,8},{8,12},{20,16},{16,20},{28,24},{24,28},{5,1},{1... | collective-permute-start | bytes 405512 | tf_op jit(solution)/shard_map/ppermute | solution.py:63
  11.9 0.2 collective-permute-done.1.refs_2_
  12.0 0.1 collective-permute-start.2
  12.1 0.0 collective-permute-done.refs_1_
  12.1 0.5 %collective-permute-done.6.refs_7_ = f32[264,128]{1,0:T(8,128)S(1)} collective-permute-done((f32[264,128]{1,0:T(8,128)S(1)}, f32[264,128]{1,0:T(8,128)S(1)}, u32[]{:S(2)}, u32[]{:S(2)}) %collective-permute-start.6) | collective-permute-done | bytes 135200 | tf_op jit(solution)/shard_map/ppermute | solution.py:63
  12.7 0.2 collective-permute-done.4.refs_5_
  12.9 0.5 %collective-permute-done.2.refs_3_ = f32[264,128]{1,0:T(8,128)S(1)} collective-permute-done((f32[264,128]{1,0:T(8,128)S(1)}, f32[264,128]{1,0:T(8,128)S(1)}, u32[]{:S(2)}, u32[]{:S(2)}) %collective-permute-start.2) | collective-permute-done | bytes 135200 | tf_op jit(solution)/shard_map/ppermute | solution.py:63
  13.4 1.8 %filter_grad.1 = (f32[1,1024]{1,0:T(1,128)S(1)}, bf16[2304,128]{1,0:T(8,128)(2,1)S(1)}, bf16[4096,128]{1,0:T(8,128)(2,1)S(1)}) custom-call(f32[264,128]{1,0:T(8,128)S(1)} %stack_local.1.refs_0_, f32[264,128]{1,0:T(8,128)S(1)} %collective-permute-done.refs_1_, f32[264,128]{1,0:T(8,128)S(1)} %collective-permute-done.1.refs_2_, ...), custom_call_target="tpu_custom_call" | custom-call | flops 1006632960 | bytes 1048576 | tf_op jit(solution)/shard_map/filter_grad/pallas_call | solution.py:129
  15.2 1.7 %collective-permute-start.7 = (f32[1,1024]{1,0:T(1,128)S(1)}, f32[1,1024]{1,0:T(1,128)S(1)}, u32[]{:S(2)}, u32[]{:S(2)}) collective-permute-start(f32[1,1024]{1,0:T(1,128)S(1)} %get-tuple-element.16), channel_id=1, source_target_pairs={{0,1},{1,0},{2,3},{3,2},{4,5},{5,4},{6,7},{7,6},{8,9},{9,8},{10,11... | collective-permute-start | bytes 12296 | tf_op jit(solution)/shard_map/ppermute | solution.py:297
  16.9 1.4 %toeplitz_tiles.1 = (bf16[65,128,128]{2,1,0:T(8,128)(2,1)S(1)}, bf16[65,128,128]{2,1,0:T(8,128)(2,1)S(1)}) custom-call(f32[264,128]{1,0:T(8,128)S(1)} %stack_local.1.refs_0_, f32[264,128]{1,0:T(8,128)S(1)} %collective-permute-done.refs_1_, f32[264,128]{1,0:T(8,128)S(1)} %collective-permute-done.1.refs_2_, f32[264,128]{1,0:T(8,128)S(1)} %collective-permute-done.2.refs_3_, ...), custom_call_target="tpu_custom_call" | custom-call | flops 17039360 | bytes 4259840 | tf_op jit(solution)/shard_map/toeplitz_tiles/pallas_call | solution.py:201
  18.3 0.6 %collective-permute-done.7 = f32[1,1024]{1,0:T(1,128)S(1)} collective-permute-done((f32[1,1024]{1,0:T(1,128)S(1)}, f32[1,1024]{1,0:T(1,128)S(1)}, u32[]{:S(2)}, u32[]{:S(2)}) %collective-permute-start.7) | collective-permute-done | bytes 4128 | tf_op jit(solution)/shard_map/ppermute | solution.py:297
  18.9 2.6 %collective-permute-start.8 = (f32[1,1024]{1,0:T(1,128)S(1)}, f32[1,1024]{1,0:T(1,128)S(1)}, u32[]{:S(2)}, u32[]{:S(2)}) collective-permute-start(f32[1,1024]{1,0:T(1,128)S(1)} %add.3.value_ref), channel_id=1, source_target_pairs={{0,2},{1,3},{2,0},{3,1},{4,6},{5,7},{6,4},{7,5},{8,10},{9,11},{10,... | collective-permute-start | bytes 12296 | tf_op jit(solution)/shard_map/ppermute | solution.py:297
  21.5 0.0 copy-done
  21.5 1.5 %convolve.1 = (f32[16,1024]{1,0:T(8,128)S(1)}, f32[16,1024]{1,0:T(8,128)S(1)}) custom-call(f32[264,128]{1,0:T(8,128)S(1)} %stack_local.1.refs_0_, bf16[2304,128]{1,0:T(8,128)(2,1)S(1)} %get-tuple-element.20.refs_1_, bf16[4096,128]{1,0:T(8,128)(2,1)S(1)} %get-tuple-element.21.refs_2_, bf16[65,128,128]{2,1,0:T(8,128)(2,1)S(1)} %get-tuple-element.22.refs_3_, ...), custom_call_target="tpu_custom_call" | custom-call | flops 1207959552 | bytes 2097152 | tf_op jit(solution)/shard_map/convolve/pallas_call | solution.py:251
  23.0 0.4 %collective-permute-done.8.other_ref = f32[1,1024]{1,0:T(1,128)S(1)} collective-permute-done((f32[1,1024]{1,0:T(1,128)S(1)}, f32[1,1024]{1,0:T(1,128)S(1)}, u32[]{:S(2)}, u32[]{:S(2)}) %collective-permute-start.8) | collective-permute-done | bytes 4128 | tf_op jit(solution)/shard_map/ppermute | solution.py:297
  23.4 0.7 %finish.1 = (f32[1,1024]{1,0:T(1,128)}, f32[16,1024]{1,0:T(8,128)}, f32[16,1024]{1,0:T(8,128)}) custom-call(f32[1,1024]{1,0:T(1,128)S(1)} %add.3.value_ref, f32[1,1024]{1,0:T(1,128)S(1)} %collective-permute-done.8.other_ref, f32[16,1024]{1,0:T(8,128)S(1)} %get-tuple-element.24.output_ref, f32[16,1024]{1,0:T(8,128)S(1)} %get-tuple-element.25.grad_ref), custom_call_target="tpu_custom_call" | custom-call | tf_op jit(solution)/shard_map/finish/pallas_call | solution.py:274
  (1 shorter events, 0.0 us)
Async XLA Ops:
  1.5 20.0 %copy-start = (f32[16]{0:T(128)S(1)}, f32[16]{0:T(128)}, u32[]{:S(2)}) copy-start(f32[16]{0:T(128)} %param.6) | copy-start | bytes 196
  1.5 9.8 %collective-permute-start.5 = (f32[264,128]{1,0:T(8,128)S(1)}, f32[264,128]{1,0:T(8,128)S(1)}, u32[]{:S(2)}, u32[]{:S(2)}) collective-permute-start(f32[264,128]{1,0:T(8,128)S(1)} %stack_local.1.refs_0_), channel_id=1, source_target_pairs={{16,0},{12,4},{24,8},{4,12},{0,16},{28,20},{8,24},{20,28},{17,1},{... | collective-permute-start | bytes 405512 | tf_op jit(solution)/shard_map/ppermute | solution.py:63
  4.6 6.8 %collective-permute-start.3 = (f32[264,128]{1,0:T(8,128)S(1)}, f32[264,128]{1,0:T(8,128)S(1)}, u32[]{:S(2)}, u32[]{:S(2)}) collective-permute-start(f32[264,128]{1,0:T(8,128)S(1)} %stack_local.1.refs_0_), channel_id=1, source_target_pairs={{24,0},{28,4},{16,8},{20,12},{8,16},{12,20},{0,24},{4,28},{25,1},{... | collective-permute-start | bytes 405512 | tf_op jit(solution)/shard_map/ppermute | solution.py:63
  6.0 6.0 %collective-permute-start.1 = (f32[264,128]{1,0:T(8,128)S(1)}, f32[264,128]{1,0:T(8,128)S(1)}, u32[]{:S(2)}, u32[]{:S(2)}) collective-permute-start(f32[264,128]{1,0:T(8,128)S(1)} %stack_local.1.refs_0_), channel_id=1, source_target_pairs={{8,0},{20,4},{0,8},{28,12},{24,16},{4,20},{16,24},{12,28},{9,1},{2... | collective-permute-start | bytes 405512 | tf_op jit(solution)/shard_map/ppermute | solution.py:63
  6.1 6.0 %collective-permute-start = (f32[264,128]{1,0:T(8,128)S(1)}, f32[264,128]{1,0:T(8,128)S(1)}, u32[]{:S(2)}, u32[]{:S(2)}) collective-permute-start(f32[264,128]{1,0:T(8,128)S(1)} %stack_local.1.refs_0_), channel_id=1, source_target_pairs={{4,0},{0,4},{12,8},{8,12},{20,16},{16,20},{28,24},{24,28},{5,1},{1... | collective-permute-start | bytes 405512 | tf_op jit(solution)/shard_map/ppermute | solution.py:63
  11.3 1.4 %collective-permute-start.6 = (f32[264,128]{1,0:T(8,128)S(1)}, f32[264,128]{1,0:T(8,128)S(1)}, u32[]{:S(2)}, u32[]{:S(2)}) collective-permute-start(f32[264,128]{1,0:T(8,128)S(1)} %collective-permute-done.5.refs_6_), channel_id=1, source_target_pairs={{4,0},{0,4},{12,8},{8,12},{20,16},{16,20},{28,24},{24,28},{5,1},{1... | collective-permute-start | bytes 405512 | tf_op jit(solution)/shard_map/ppermute | solution.py:63
  11.3 1.5 %collective-permute-start.4 = (f32[264,128]{1,0:T(8,128)S(1)}, f32[264,128]{1,0:T(8,128)S(1)}, u32[]{:S(2)}, u32[]{:S(2)}) collective-permute-start(f32[264,128]{1,0:T(8,128)S(1)} %collective-permute-done.3.refs_4_), channel_id=1, source_target_pairs={{4,0},{0,4},{12,8},{8,12},{20,16},{16,20},{28,24},{24,28},{5,1},{1... | collective-permute-start | bytes 405512 | tf_op jit(solution)/shard_map/ppermute | solution.py:63
  12.0 1.4 %collective-permute-start.2 = (f32[264,128]{1,0:T(8,128)S(1)}, f32[264,128]{1,0:T(8,128)S(1)}, u32[]{:S(2)}, u32[]{:S(2)}) collective-permute-start(f32[264,128]{1,0:T(8,128)S(1)} %collective-permute-done.1.refs_2_), channel_id=1, source_target_pairs={{4,0},{0,4},{12,8},{8,12},{20,16},{16,20},{28,24},{24,28},{5,1},{1... | collective-permute-start | bytes 405512 | tf_op jit(solution)/shard_map/ppermute | solution.py:63
  15.2 3.7 %collective-permute-start.7 = (f32[1,1024]{1,0:T(1,128)S(1)}, f32[1,1024]{1,0:T(1,128)S(1)}, u32[]{:S(2)}, u32[]{:S(2)}) collective-permute-start(f32[1,1024]{1,0:T(1,128)S(1)} %get-tuple-element.16), channel_id=1, source_target_pairs={{0,1},{1,0},{2,3},{3,2},{4,5},{5,4},{6,7},{7,6},{8,9},{9,8},{10,11... | collective-permute-start | bytes 12296 | tf_op jit(solution)/shard_map/ppermute | solution.py:297
  18.9 4.5 %collective-permute-start.8 = (f32[1,1024]{1,0:T(1,128)S(1)}, f32[1,1024]{1,0:T(1,128)S(1)}, u32[]{:S(2)}, u32[]{:S(2)}) collective-permute-start(f32[1,1024]{1,0:T(1,128)S(1)} %add.3.value_ref), channel_id=1, source_target_pairs={{0,2},{1,3},{2,0},{3,1},{4,6},{5,7},{6,4},{7,5},{8,10},{9,11},{10,... | collective-permute-start | bytes 12296 | tf_op jit(solution)/shard_map/ppermute | solution.py:297

commit v8 on v7

--- a/solution.py
+++ b/solution.py
@@ -286,8 +286,8 @@
     channels, tokens = signal.shape
     stacked = stack_local(signal, cotangent, filter_taps)
     blocks = gather_blocks(stacked)
+    toeplitz = toeplitz_tiles(blocks, shards, channels, tokens)
     value, *held = filter_grad(blocks, shards, channels, tokens)
-    toeplitz = toeplitz_tiles(blocks, shards, channels, tokens)
     other = None
     bits = 1
     while bits < groups:

time: 24.2 us -> 24.2 us (level)
  no operation moved by 1% of the time
where the time goes in v8:
time: 24.2 us; the launch traced here: 24.1 us
  starting transfers between devices  9.46 us (39%)
  waiting for transfers between devices  7.59 us (31%)
  Pallas kernels  6.35 us (26%)
  between operations  0.67 us (3%)
    ppermute x7, waiting for transfers between devices, fetched(): lax.ppermute(value, 'context', [(source_index(i, entry), i) for i in rang...  6.64 us
    ppermute x7, starting transfers between devices, fetched(): lax.ppermute(value, 'context', [(source_index(i, entry), i) for i in rang...  5.2 us
    ppermute x2, starting transfers between devices, direct_body(): other = lax.ppermute(value, 'chan', [(i, i ^ bits) for i in range(groups)])  4.26 us
    pallas_call x1, Pallas kernels, filter_grad(): pl.pallas_call(functools.partial(filter_grad_kernel, shards, channels, to...  1.84 us
    pallas_call x1, Pallas kernels, convolve(): pl.pallas_call(functools.partial(convolve_kernel, shards, channels, token...  1.52 us
    pallas_call x1, Pallas kernels, toeplitz_tiles(): pl.pallas_call(functools.partial(toeplitz_kernel, shards, channels, token...  1.44 us
    ppermute x2, waiting for transfers between devices, direct_body(): other = lax.ppermute(value, 'chan', [(i, i ^ bits) for i in range(groups)])  0.95 us
    pallas_call x1, Pallas kernels, stack_local(): pl.pallas_call(stack_kernel, out_shape=pltpu.VMEM((rows, LANES), jnp.floa...  0.88 us
  transfers between devices with their start and end apart: 9, of which 7 were waited for; matrix products, arithmetic and copies ran while one was open for 0% of the time, Pallas kernels for 12%

profile of v8, /device:TPU:0, one launch (start us, length us, event | category | flops | bytes accessed | tf_op | source)
XLA Modules:
  0.0 24.1 jit_solution(3030666380845547054)
XLA Ops:
  0.6 0.9 %stack_local.1.refs_0_ = f32[264,128]{1,0:T(8,128)S(1)} custom-call(f32[16,1024]{1,0:T(8,128)} %signal_ref.1, f32[16,1024]{1,0:T(8,128)} %cotangent_ref.1, f32[8,128]{1,0:T(8,128)} %bitcast.4), custom_call_target="tpu_custom_call" | custom-call | tf_op jit(solution)/shard_map/stack_local/pallas_call | solution.py:46
  1.5 0.0 copy-start
  1.5 3.0 %collective-permute-start.5 = (f32[264,128]{1,0:T(8,128)S(1)}, f32[264,128]{1,0:T(8,128)S(1)}, u32[]{:S(2)}, u32[]{:S(2)}) collective-permute-start(f32[264,128]{1,0:T(8,128)S(1)} %stack_local.1.refs_0_), channel_id=1, source_target_pairs={{16,0},{12,4},{24,8},{4,12},{0,16},{28,20},{8,24},{20,28},{17,1},{... | collective-permute-start | bytes 405512 | tf_op jit(solution)/shard_map/ppermute | solution.py:63
  4.6 1.4 %collective-permute-start.3 = (f32[264,128]{1,0:T(8,128)S(1)}, f32[264,128]{1,0:T(8,128)S(1)}, u32[]{:S(2)}, u32[]{:S(2)}) collective-permute-start(f32[264,128]{1,0:T(8,128)S(1)} %stack_local.1.refs_0_), channel_id=1, source_target_pairs={{24,0},{28,4},{16,8},{20,12},{8,16},{12,20},{0,24},{4,28},{25,1},{... | collective-permute-start | bytes 405512 | tf_op jit(solution)/shard_map/ppermute | solution.py:63
  6.0 0.1 collective-permute-start.1
  6.1 0.0 collective-permute-start
  6.1 5.2 %collective-permute-done.5.refs_6_ = f32[264,128]{1,0:T(8,128)S(1)} collective-permute-done((f32[264,128]{1,0:T(8,128)S(1)}, f32[264,128]{1,0:T(8,128)S(1)}, u32[]{:S(2)}, u32[]{:S(2)}) %collective-permute-start.5) | collective-permute-done | bytes 135200 | tf_op jit(solution)/shard_map/ppermute | solution.py:63
  11.3 0.0 collective-permute-start.6
  11.3 0.0 collective-permute-done.3.refs_4_
  11.3 0.5 %collective-permute-start.4 = (f32[264,128]{1,0:T(8,128)S(1)}, f32[264,128]{1,0:T(8,128)S(1)}, u32[]{:S(2)}, u32[]{:S(2)}) collective-permute-start(f32[264,128]{1,0:T(8,128)S(1)} %collective-permute-done.3.refs_4_), channel_id=1, source_target_pairs={{4,0},{0,4},{12,8},{8,12},{20,16},{16,20},{28,24},{24,28},{5,1},{1... | collective-permute-start | bytes 405512 | tf_op jit(solution)/shard_map/ppermute | solution.py:63
  11.9 0.2 collective-permute-done.1.refs_2_
  12.0 0.1 collective-permute-start.2
  12.1 0.0 collective-permute-done.refs_1_
  12.1 0.5 %collective-permute-done.6.refs_7_ = f32[264,128]{1,0:T(8,128)S(1)} collective-permute-done((f32[264,128]{1,0:T(8,128)S(1)}, f32[264,128]{1,0:T(8,128)S(1)}, u32[]{:S(2)}, u32[]{:S(2)}) %collective-permute-start.6) | collective-permute-done | bytes 135200 | tf_op jit(solution)/shard_map/ppermute | solution.py:63
  12.7 0.2 collective-permute-done.4.refs_5_
  12.9 0.5 %collective-permute-done.2.refs_3_ = f32[264,128]{1,0:T(8,128)S(1)} collective-permute-done((f32[264,128]{1,0:T(8,128)S(1)}, f32[264,128]{1,0:T(8,128)S(1)}, u32[]{:S(2)}, u32[]{:S(2)}) %collective-permute-start.2) | collective-permute-done | bytes 135200 | tf_op jit(solution)/shard_map/ppermute | solution.py:63
  13.4 1.8 %filter_grad.1 = (f32[1,1024]{1,0:T(1,128)S(1)}, bf16[2304,128]{1,0:T(8,128)(2,1)S(1)}, bf16[4096,128]{1,0:T(8,128)(2,1)S(1)}) custom-call(f32[264,128]{1,0:T(8,128)S(1)} %stack_local.1.refs_0_, f32[264,128]{1,0:T(8,128)S(1)} %collective-permute-done.refs_1_, f32[264,128]{1,0:T(8,128)S(1)} %collective-permute-done.1.refs_2_, ...), custom_call_target="tpu_custom_call" | custom-call | flops 1006632960 | bytes 1048576 | tf_op jit(solution)/shard_map/filter_grad/pallas_call | solution.py:129
  15.2 1.7 %collective-permute-start.7 = (f32[1,1024]{1,0:T(1,128)S(1)}, f32[1,1024]{1,0:T(1,128)S(1)}, u32[]{:S(2)}, u32[]{:S(2)}) collective-permute-start(f32[1,1024]{1,0:T(1,128)S(1)} %get-tuple-element.16), channel_id=1, source_target_pairs={{0,1},{1,0},{2,3},{3,2},{4,5},{5,4},{6,7},{7,6},{8,9},{9,8},{10,11... | collective-permute-start | bytes 12296 | tf_op jit(solution)/shard_map/ppermute | solution.py:297
  16.9 1.4 %toeplitz_tiles.1 = (bf16[65,128,128]{2,1,0:T(8,128)(2,1)S(1)}, bf16[65,128,128]{2,1,0:T(8,128)(2,1)S(1)}) custom-call(f32[264,128]{1,0:T(8,128)S(1)} %stack_local.1.refs_0_, f32[264,128]{1,0:T(8,128)S(1)} %collective-permute-done.refs_1_, f32[264,128]{1,0:T(8,128)S(1)} %collective-permute-done.1.refs_2_, f32[264,128]{1,0:T(8,128)S(1)} %collective-permute-done.2.refs_3_, ...), custom_call_target="tpu_custom_call" | custom-call | flops 17039360 | bytes 4259840 | tf_op jit(solution)/shard_map/toeplitz_tiles/pallas_call | solution.py:201
  18.3 0.6 %collective-permute-done.7 = f32[1,1024]{1,0:T(1,128)S(1)} collective-permute-done((f32[1,1024]{1,0:T(1,128)S(1)}, f32[1,1024]{1,0:T(1,128)S(1)}, u32[]{:S(2)}, u32[]{:S(2)}) %collective-permute-start.7) | collective-permute-done | bytes 4128 | tf_op jit(solution)/shard_map/ppermute | solution.py:297
  18.9 2.6 %collective-permute-start.8 = (f32[1,1024]{1,0:T(1,128)S(1)}, f32[1,1024]{1,0:T(1,128)S(1)}, u32[]{:S(2)}, u32[]{:S(2)}) collective-permute-start(f32[1,1024]{1,0:T(1,128)S(1)} %add.3.value_ref), channel_id=1, source_target_pairs={{0,2},{1,3},{2,0},{3,1},{4,6},{5,7},{6,4},{7,5},{8,10},{9,11},{10,... | collective-permute-start | bytes 12296 | tf_op jit(solution)/shard_map/ppermute | solution.py:297
  21.5 0.0 copy-done
  21.5 1.5 %convolve.1 = (f32[16,1024]{1,0:T(8,128)S(1)}, f32[16,1024]{1,0:T(8,128)S(1)}) custom-call(f32[264,128]{1,0:T(8,128)S(1)} %stack_local.1.refs_0_, bf16[2304,128]{1,0:T(8,128)(2,1)S(1)} %get-tuple-element.20.refs_1_, bf16[4096,128]{1,0:T(8,128)(2,1)S(1)} %get-tuple-element.21.refs_2_, bf16[65,128,128]{2,1,0:T(8,128)(2,1)S(1)} %get-tuple-element.22.refs_3_, ...), custom_call_target="tpu_custom_call" | custom-call | flops 1207959552 | bytes 2097152 | tf_op jit(solution)/shard_map/convolve/pallas_call | solution.py:251
  23.0 0.4 %collective-permute-done.8.other_ref = f32[1,1024]{1,0:T(1,128)S(1)} collective-permute-done((f32[1,1024]{1,0:T(1,128)S(1)}, f32[1,1024]{1,0:T(1,128)S(1)}, u32[]{:S(2)}, u32[]{:S(2)}) %collective-permute-start.8) | collective-permute-done | bytes 4128 | tf_op jit(solution)/shard_map/ppermute | solution.py:297
  23.4 0.7 %finish.1 = (f32[1,1024]{1,0:T(1,128)}, f32[16,1024]{1,0:T(8,128)}, f32[16,1024]{1,0:T(8,128)}) custom-call(f32[1,1024]{1,0:T(1,128)S(1)} %add.3.value_ref, f32[1,1024]{1,0:T(1,128)S(1)} %collective-permute-done.8.other_ref, f32[16,1024]{1,0:T(8,128)S(1)} %get-tuple-element.24.output_ref, f32[16,1024]{1,0:T(8,128)S(1)} %get-tuple-element.25.grad_ref), custom_call_target="tpu_custom_call" | custom-call | tf_op jit(solution)/shard_map/finish/pallas_call | solution.py:274
  (1 shorter events, 0.0 us)
Async XLA Ops:
  1.5 20.0 %copy-start = (f32[16]{0:T(128)S(1)}, f32[16]{0:T(128)}, u32[]{:S(2)}) copy-start(f32[16]{0:T(128)} %param.6) | copy-start | bytes 196
  1.5 9.8 %collective-permute-start.5 = (f32[264,128]{1,0:T(8,128)S(1)}, f32[264,128]{1,0:T(8,128)S(1)}, u32[]{:S(2)}, u32[]{:S(2)}) collective-permute-start(f32[264,128]{1,0:T(8,128)S(1)} %stack_local.1.refs_0_), channel_id=1, source_target_pairs={{16,0},{12,4},{24,8},{4,12},{0,16},{28,20},{8,24},{20,28},{17,1},{... | collective-permute-start | bytes 405512 | tf_op jit(solution)/shard_map/ppermute | solution.py:63
  4.6 6.8 %collective-permute-start.3 = (f32[264,128]{1,0:T(8,128)S(1)}, f32[264,128]{1,0:T(8,128)S(1)}, u32[]{:S(2)}, u32[]{:S(2)}) collective-permute-start(f32[264,128]{1,0:T(8,128)S(1)} %stack_local.1.refs_0_), channel_id=1, source_target_pairs={{24,0},{28,4},{16,8},{20,12},{8,16},{12,20},{0,24},{4,28},{25,1},{... | collective-permute-start | bytes 405512 | tf_op jit(solution)/shard_map/ppermute | solution.py:63
  6.0 6.0 %collective-permute-start.1 = (f32[264,128]{1,0:T(8,128)S(1)}, f32[264,128]{1,0:T(8,128)S(1)}, u32[]{:S(2)}, u32[]{:S(2)}) collective-permute-start(f32[264,128]{1,0:T(8,128)S(1)} %stack_local.1.refs_0_), channel_id=1, source_target_pairs={{8,0},{20,4},{0,8},{28,12},{24,16},{4,20},{16,24},{12,28},{9,1},{2... | collective-permute-start | bytes 405512 | tf_op jit(solution)/shard_map/ppermute | solution.py:63
  6.1 6.0 %collective-permute-start = (f32[264,128]{1,0:T(8,128)S(1)}, f32[264,128]{1,0:T(8,128)S(1)}, u32[]{:S(2)}, u32[]{:S(2)}) collective-permute-start(f32[264,128]{1,0:T(8,128)S(1)} %stack_local.1.refs_0_), channel_id=1, source_target_pairs={{4,0},{0,4},{12,8},{8,12},{20,16},{16,20},{28,24},{24,28},{5,1},{1... | collective-permute-start | bytes 405512 | tf_op jit(solution)/shard_map/ppermute | solution.py:63
  11.3 1.4 %collective-permute-start.6 = (f32[264,128]{1,0:T(8,128)S(1)}, f32[264,128]{1,0:T(8,128)S(1)}, u32[]{:S(2)}, u32[]{:S(2)}) collective-permute-start(f32[264,128]{1,0:T(8,128)S(1)} %collective-permute-done.5.refs_6_), channel_id=1, source_target_pairs={{4,0},{0,4},{12,8},{8,12},{20,16},{16,20},{28,24},{24,28},{5,1},{1... | collective-permute-start | bytes 405512 | tf_op jit(solution)/shard_map/ppermute | solution.py:63
  11.3 1.5 %collective-permute-start.4 = (f32[264,128]{1,0:T(8,128)S(1)}, f32[264,128]{1,0:T(8,128)S(1)}, u32[]{:S(2)}, u32[]{:S(2)}) collective-permute-start(f32[264,128]{1,0:T(8,128)S(1)} %collective-permute-done.3.refs_4_), channel_id=1, source_target_pairs={{4,0},{0,4},{12,8},{8,12},{20,16},{16,20},{28,24},{24,28},{5,1},{1... | collective-permute-start | bytes 405512 | tf_op jit(solution)/shard_map/ppermute | solution.py:63
  12.0 1.4 %collective-permute-start.2 = (f32[264,128]{1,0:T(8,128)S(1)}, f32[264,128]{1,0:T(8,128)S(1)}, u32[]{:S(2)}, u32[]{:S(2)}) collective-permute-start(f32[264,128]{1,0:T(8,128)S(1)} %collective-permute-done.1.refs_2_), channel_id=1, source_target_pairs={{4,0},{0,4},{12,8},{8,12},{20,16},{16,20},{28,24},{24,28},{5,1},{1... | collective-permute-start | bytes 405512 | tf_op jit(solution)/shard_map/ppermute | solution.py:63
  15.2 3.7 %collective-permute-start.7 = (f32[1,1024]{1,0:T(1,128)S(1)}, f32[1,1024]{1,0:T(1,128)S(1)}, u32[]{:S(2)}, u32[]{:S(2)}) collective-permute-start(f32[1,1024]{1,0:T(1,128)S(1)} %get-tuple-element.16), channel_id=1, source_target_pairs={{0,1},{1,0},{2,3},{3,2},{4,5},{5,4},{6,7},{7,6},{8,9},{9,8},{10,11... | collective-permute-start | bytes 12296 | tf_op jit(solution)/shard_map/ppermute | solution.py:297
  18.9 4.5 %collective-permute-start.8 = (f32[1,1024]{1,0:T(1,128)S(1)}, f32[1,1024]{1,0:T(1,128)S(1)}, u32[]{:S(2)}, u32[]{:S(2)}) collective-permute-start(f32[1,1024]{1,0:T(1,128)S(1)} %add.3.value_ref), channel_id=1, source_target_pairs={{0,2},{1,3},{2,0},{3,1},{4,6},{5,7},{6,4},{7,5},{8,10},{9,11},{10,... | collective-permute-start | bytes 12296 | tf_op jit(solution)/shard_map/ppermute | solution.py:297

commit v9 on v7

--- a/solution.py
+++ b/solution.py
@@ -289,13 +289,13 @@
     value, *held = filter_grad(blocks, shards, channels, tokens)
     toeplitz = toeplitz_tiles(blocks, shards, channels, tokens)
     other = None
-    bits = 1
-    while bits < groups:
+    bits = groups // 2
+    while bits:
         if other is not None:
             value = value + other
             value, *toeplitz = lax.optimization_barrier((value, *toeplitz))
         other = lax.ppermute(value, "chan", [(i, i ^ bits) for i in range(groups)])
-        bits *= 2
+        bits //= 2
     output, grad_signal = convolve(blocks[0], held, toeplitz, skip_gain, shards, channels, tokens)
     scale = 1.0 / math.sqrt(shards * tokens)
     grad_filter, output, grad_signal = finish(value, other, output, grad_signal, scale)

time: 24.2 us -> 24.2 us (level)
  no operation moved by 1% of the time
where the time goes in v9:
time: 24.2 us; the launch traced here: 24.1 us
  starting transfers between devices  9.46 us (39%)
  waiting for transfers between devices  7.59 us (31%)
  Pallas kernels  6.35 us (26%)
  between operations  0.67 us (3%)
    ppermute x7, waiting for transfers between devices, fetched(): lax.ppermute(value, 'context', [(source_index(i, entry), i) for i in rang...  6.64 us
    ppermute x7, starting transfers between devices, fetched(): lax.ppermute(value, 'context', [(source_index(i, entry), i) for i in rang...  5.2 us
    ppermute x2, starting transfers between devices, direct_body(): other = lax.ppermute(value, 'chan', [(i, i ^ bits) for i in range(groups)])  4.26 us
    pallas_call x1, Pallas kernels, filter_grad(): pl.pallas_call(functools.partial(filter_grad_kernel, shards, channels, to...  1.84 us
    pallas_call x1, Pallas kernels, convolve(): pl.pallas_call(functools.partial(convolve_kernel, shards, channels, token...  1.53 us
    pallas_call x1, Pallas kernels, toeplitz_tiles(): pl.pallas_call(functools.partial(toeplitz_kernel, shards, channels, token...  1.44 us
    ppermute x2, waiting for transfers between devices, direct_body(): other = lax.ppermute(value, 'chan', [(i, i ^ bits) for i in range(groups)])  0.95 us
    pallas_call x1, Pallas kernels, stack_local(): pl.pallas_call(stack_kernel, out_shape=pltpu.VMEM((rows, LANES), jnp.floa...  0.88 us
  transfers between devices with their start and end apart: 9, of which 7 were waited for; matrix products, arithmetic and copies ran while one was open for 0% of the time, Pallas kernels for 12%

profile of v9, /device:TPU:0, one launch (start us, length us, event | category | flops | bytes accessed | tf_op | source)
XLA Modules:
  0.0 24.1 jit_solution(9444585373345429990)
XLA Ops:
  0.6 0.9 %stack_local.1.refs_0_ = f32[264,128]{1,0:T(8,128)S(1)} custom-call(f32[16,1024]{1,0:T(8,128)} %signal_ref.1, f32[16,1024]{1,0:T(8,128)} %cotangent_ref.1, f32[8,128]{1,0:T(8,128)} %bitcast.4), custom_call_target="tpu_custom_call" | custom-call | tf_op jit(solution)/shard_map/stack_local/pallas_call | solution.py:46
  1.5 0.0 copy-start
  1.5 3.0 %collective-permute-start.5 = (f32[264,128]{1,0:T(8,128)S(1)}, f32[264,128]{1,0:T(8,128)S(1)}, u32[]{:S(2)}, u32[]{:S(2)}) collective-permute-start(f32[264,128]{1,0:T(8,128)S(1)} %stack_local.1.refs_0_), channel_id=1, source_target_pairs={{16,0},{12,4},{24,8},{4,12},{0,16},{28,20},{8,24},{20,28},{17,1},{... | collective-permute-start | bytes 405512 | tf_op jit(solution)/shard_map/ppermute | solution.py:63
  4.6 1.4 %collective-permute-start.3 = (f32[264,128]{1,0:T(8,128)S(1)}, f32[264,128]{1,0:T(8,128)S(1)}, u32[]{:S(2)}, u32[]{:S(2)}) collective-permute-start(f32[264,128]{1,0:T(8,128)S(1)} %stack_local.1.refs_0_), channel_id=1, source_target_pairs={{24,0},{28,4},{16,8},{20,12},{8,16},{12,20},{0,24},{4,28},{25,1},{... | collective-permute-start | bytes 405512 | tf_op jit(solution)/shard_map/ppermute | solution.py:63
  6.0 0.1 collective-permute-start.1
  6.1 0.0 collective-permute-start
  6.1 5.2 %collective-permute-done.5.refs_6_ = f32[264,128]{1,0:T(8,128)S(1)} collective-permute-done((f32[264,128]{1,0:T(8,128)S(1)}, f32[264,128]{1,0:T(8,128)S(1)}, u32[]{:S(2)}, u32[]{:S(2)}) %collective-permute-start.5) | collective-permute-done | bytes 135200 | tf_op jit(solution)/shard_map/ppermute | solution.py:63
  11.3 0.0 collective-permute-start.6
  11.3 0.0 collective-permute-done.3.refs_4_
  11.3 0.5 %collective-permute-start.4 = (f32[264,128]{1,0:T(8,128)S(1)}, f32[264,128]{1,0:T(8,128)S(1)}, u32[]{:S(2)}, u32[]{:S(2)}) collective-permute-start(f32[264,128]{1,0:T(8,128)S(1)} %collective-permute-done.3.refs_4_), channel_id=1, source_target_pairs={{4,0},{0,4},{12,8},{8,12},{20,16},{16,20},{28,24},{24,28},{5,1},{1... | collective-permute-start | bytes 405512 | tf_op jit(solution)/shard_map/ppermute | solution.py:63
  11.9 0.2 collective-permute-done.1.refs_2_
  12.0 0.1 collective-permute-start.2
  12.1 0.0 collective-permute-done.refs_1_
  12.1 0.5 %collective-permute-done.6.refs_7_ = f32[264,128]{1,0:T(8,128)S(1)} collective-permute-done((f32[264,128]{1,0:T(8,128)S(1)}, f32[264,128]{1,0:T(8,128)S(1)}, u32[]{:S(2)}, u32[]{:S(2)}) %collective-permute-start.6) | collective-permute-done | bytes 135200 | tf_op jit(solution)/shard_map/ppermute | solution.py:63
  12.7 0.2 collective-permute-done.4.refs_5_
  12.9 0.5 %collective-permute-done.2.refs_3_ = f32[264,128]{1,0:T(8,128)S(1)} collective-permute-done((f32[264,128]{1,0:T(8,128)S(1)}, f32[264,128]{1,0:T(8,128)S(1)}, u32[]{:S(2)}, u32[]{:S(2)}) %collective-permute-start.2) | collective-permute-done | bytes 135200 | tf_op jit(solution)/shard_map/ppermute | solution.py:63
  13.4 1.8 %filter_grad.1 = (f32[1,1024]{1,0:T(1,128)S(1)}, bf16[2304,128]{1,0:T(8,128)(2,1)S(1)}, bf16[4096,128]{1,0:T(8,128)(2,1)S(1)}) custom-call(f32[264,128]{1,0:T(8,128)S(1)} %stack_local.1.refs_0_, f32[264,128]{1,0:T(8,128)S(1)} %collective-permute-done.refs_1_, f32[264,128]{1,0:T(8,128)S(1)} %collective-permute-done.1.refs_2_, ...), custom_call_target="tpu_custom_call" | custom-call | flops 1006632960 | bytes 1048576 | tf_op jit(solution)/shard_map/filter_grad/pallas_call | solution.py:129
  15.2 2.7 %collective-permute-start.7 = (f32[1,1024]{1,0:T(1,128)S(1)}, f32[1,1024]{1,0:T(1,128)S(1)}, u32[]{:S(2)}, u32[]{:S(2)}) collective-permute-start(f32[1,1024]{1,0:T(1,128)S(1)} %get-tuple-element.16), channel_id=1, source_target_pairs={{0,2},{1,3},{2,0},{3,1},{4,6},{5,7},{6,4},{7,5},{8,10},{9,11},{10,... | collective-permute-start | bytes 12296 | tf_op jit(solution)/shard_map/ppermute | solution.py:297
  17.9 1.4 %toeplitz_tiles.1 = (bf16[65,128,128]{2,1,0:T(8,128)(2,1)S(1)}, bf16[65,128,128]{2,1,0:T(8,128)(2,1)S(1)}) custom-call(f32[264,128]{1,0:T(8,128)S(1)} %stack_local.1.refs_0_, f32[264,128]{1,0:T(8,128)S(1)} %collective-permute-done.refs_1_, f32[264,128]{1,0:T(8,128)S(1)} %collective-permute-done.1.refs_2_, f32[264,128]{1,0:T(8,128)S(1)} %collective-permute-done.2.refs_3_, ...), custom_call_target="tpu_custom_call" | custom-call | flops 17039360 | bytes 4259840 | tf_op jit(solution)/shard_map/toeplitz_tiles/pallas_call | solution.py:201
  19.3 0.5 %collective-permute-done.7 = f32[1,1024]{1,0:T(1,128)S(1)} collective-permute-done((f32[1,1024]{1,0:T(1,128)S(1)}, f32[1,1024]{1,0:T(1,128)S(1)}, u32[]{:S(2)}, u32[]{:S(2)}) %collective-permute-start.7) | collective-permute-done | bytes 4128 | tf_op jit(solution)/shard_map/ppermute | solution.py:297
  19.8 1.6 %collective-permute-start.8 = (f32[1,1024]{1,0:T(1,128)S(1)}, f32[1,1024]{1,0:T(1,128)S(1)}, u32[]{:S(2)}, u32[]{:S(2)}) collective-permute-start(f32[1,1024]{1,0:T(1,128)S(1)} %add.3.value_ref), channel_id=1, source_target_pairs={{0,1},{1,0},{2,3},{3,2},{4,5},{5,4},{6,7},{7,6},{8,9},{9,8},{10,11... | collective-permute-start | bytes 12296 | tf_op jit(solution)/shard_map/ppermute | solution.py:297
  21.4 0.0 copy-done
  21.4 1.5 %convolve.1 = (f32[16,1024]{1,0:T(8,128)S(1)}, f32[16,1024]{1,0:T(8,128)S(1)}) custom-call(f32[264,128]{1,0:T(8,128)S(1)} %stack_local.1.refs_0_, bf16[2304,128]{1,0:T(8,128)(2,1)S(1)} %get-tuple-element.20.refs_1_, bf16[4096,128]{1,0:T(8,128)(2,1)S(1)} %get-tuple-element.21.refs_2_, bf16[65,128,128]{2,1,0:T(8,128)(2,1)S(1)} %get-tuple-element.22.refs_3_, ...), custom_call_target="tpu_custom_call" | custom-call | flops 1207959552 | bytes 2097152 | tf_op jit(solution)/shard_map/convolve/pallas_call | solution.py:251
  22.9 0.5 %collective-permute-done.8.other_ref = f32[1,1024]{1,0:T(1,128)S(1)} collective-permute-done((f32[1,1024]{1,0:T(1,128)S(1)}, f32[1,1024]{1,0:T(1,128)S(1)}, u32[]{:S(2)}, u32[]{:S(2)}) %collective-permute-start.8) | collective-permute-done | bytes 4128 | tf_op jit(solution)/shard_map/ppermute | solution.py:297
  23.4 0.7 %finish.1 = (f32[1,1024]{1,0:T(1,128)}, f32[16,1024]{1,0:T(8,128)}, f32[16,1024]{1,0:T(8,128)}) custom-call(f32[1,1024]{1,0:T(1,128)S(1)} %add.3.value_ref, f32[1,1024]{1,0:T(1,128)S(1)} %collective-permute-done.8.other_ref, f32[16,1024]{1,0:T(8,128)S(1)} %get-tuple-element.24.output_ref, f32[16,1024]{1,0:T(8,128)S(1)} %get-tuple-element.25.grad_ref), custom_call_target="tpu_custom_call" | custom-call | tf_op jit(solution)/shard_map/finish/pallas_call | solution.py:274
  (1 shorter events, 0.0 us)
Async XLA Ops:
  1.5 19.9 %copy-start = (f32[16]{0:T(128)S(1)}, f32[16]{0:T(128)}, u32[]{:S(2)}) copy-start(f32[16]{0:T(128)} %param.6) | copy-start | bytes 196
  1.5 9.8 %collective-permute-start.5 = (f32[264,128]{1,0:T(8,128)S(1)}, f32[264,128]{1,0:T(8,128)S(1)}, u32[]{:S(2)}, u32[]{:S(2)}) collective-permute-start(f32[264,128]{1,0:T(8,128)S(1)} %stack_local.1.refs_0_), channel_id=1, source_target_pairs={{16,0},{12,4},{24,8},{4,12},{0,16},{28,20},{8,24},{20,28},{17,1},{... | collective-permute-start | bytes 405512 | tf_op jit(solution)/shard_map/ppermute | solution.py:63
  4.6 6.8 %collective-permute-start.3 = (f32[264,128]{1,0:T(8,128)S(1)}, f32[264,128]{1,0:T(8,128)S(1)}, u32[]{:S(2)}, u32[]{:S(2)}) collective-permute-start(f32[264,128]{1,0:T(8,128)S(1)} %stack_local.1.refs_0_), channel_id=1, source_target_pairs={{24,0},{28,4},{16,8},{20,12},{8,16},{12,20},{0,24},{4,28},{25,1},{... | collective-permute-start | bytes 405512 | tf_op jit(solution)/shard_map/ppermute | solution.py:63
  6.0 6.0 %collective-permute-start.1 = (f32[264,128]{1,0:T(8,128)S(1)}, f32[264,128]{1,0:T(8,128)S(1)}, u32[]{:S(2)}, u32[]{:S(2)}) collective-permute-start(f32[264,128]{1,0:T(8,128)S(1)} %stack_local.1.refs_0_), channel_id=1, source_target_pairs={{8,0},{20,4},{0,8},{28,12},{24,16},{4,20},{16,24},{12,28},{9,1},{2... | collective-permute-start | bytes 405512 | tf_op jit(solution)/shard_map/ppermute | solution.py:63
  6.1 6.0 %collective-permute-start = (f32[264,128]{1,0:T(8,128)S(1)}, f32[264,128]{1,0:T(8,128)S(1)}, u32[]{:S(2)}, u32[]{:S(2)}) collective-permute-start(f32[264,128]{1,0:T(8,128)S(1)} %stack_local.1.refs_0_), channel_id=1, source_target_pairs={{4,0},{0,4},{12,8},{8,12},{20,16},{16,20},{28,24},{24,28},{5,1},{1... | collective-permute-start | bytes 405512 | tf_op jit(solution)/shard_map/ppermute | solution.py:63
  11.3 1.4 %collective-permute-start.6 = (f32[264,128]{1,0:T(8,128)S(1)}, f32[264,128]{1,0:T(8,128)S(1)}, u32[]{:S(2)}, u32[]{:S(2)}) collective-permute-start(f32[264,128]{1,0:T(8,128)S(1)} %collective-permute-done.5.refs_6_), channel_id=1, source_target_pairs={{4,0},{0,4},{12,8},{8,12},{20,16},{16,20},{28,24},{24,28},{5,1},{1... | collective-permute-start | bytes 405512 | tf_op jit(solution)/shard_map/ppermute | solution.py:63
  11.3 1.5 %collective-permute-start.4 = (f32[264,128]{1,0:T(8,128)S(1)}, f32[264,128]{1,0:T(8,128)S(1)}, u32[]{:S(2)}, u32[]{:S(2)}) collective-permute-start(f32[264,128]{1,0:T(8,128)S(1)} %collective-permute-done.3.refs_4_), channel_id=1, source_target_pairs={{4,0},{0,4},{12,8},{8,12},{20,16},{16,20},{28,24},{24,28},{5,1},{1... | collective-permute-start | bytes 405512 | tf_op jit(solution)/shard_map/ppermute | solution.py:63
  12.0 1.4 %collective-permute-start.2 = (f32[264,128]{1,0:T(8,128)S(1)}, f32[264,128]{1,0:T(8,128)S(1)}, u32[]{:S(2)}, u32[]{:S(2)}) collective-permute-start(f32[264,128]{1,0:T(8,128)S(1)} %collective-permute-done.1.refs_2_), channel_id=1, source_target_pairs={{4,0},{0,4},{12,8},{8,12},{20,16},{16,20},{28,24},{24,28},{5,1},{1... | collective-permute-start | bytes 405512 | tf_op jit(solution)/shard_map/ppermute | solution.py:63
  15.2 4.6 %collective-permute-start.7 = (f32[1,1024]{1,0:T(1,128)S(1)}, f32[1,1024]{1,0:T(1,128)S(1)}, u32[]{:S(2)}, u32[]{:S(2)}) collective-permute-start(f32[1,1024]{1,0:T(1,128)S(1)} %get-tuple-element.16), channel_id=1, source_target_pairs={{0,2},{1,3},{2,0},{3,1},{4,6},{5,7},{6,4},{7,5},{8,10},{9,11},{10,... | collective-permute-start | bytes 12296 | tf_op jit(solution)/shard_map/ppermute | solution.py:297
  19.8 3.6 %collective-permute-start.8 = (f32[1,1024]{1,0:T(1,128)S(1)}, f32[1,1024]{1,0:T(1,128)S(1)}, u32[]{:S(2)}, u32[]{:S(2)}) collective-permute-start(f32[1,1024]{1,0:T(1,128)S(1)} %add.3.value_ref), channel_id=1, source_target_pairs={{0,1},{1,0},{2,3},{3,2},{4,5},{5,4},{6,7},{7,6},{8,9},{9,8},{10,11... | collective-permute-start | bytes 12296 | tf_op jit(solution)/shard_map/ppermute | solution.py:297
